TPU v7x, 32 devices: a whole 2x2x4 slice. The times are simulated.
32 devices in a mesh: ctx: 8 (over y, x, core), wt: 4 (over z).
Axes of the slice: x: 2, y: 2, z: 4, core: 2. Of those that a mesh axis runs over, the one named last changes fastest.
Arguments:
- tokens: bfloat16 [4, 4096, 768], P('wt', 'ctx'), may hold values from -6 to 6
- cotangent: bfloat16 [4, 4096, 768], P('wt', 'ctx'), may hold values from -6 to 6
- lengths: int32 [4], P('wt'), may hold values from 1024 to 4096, as said below
- rand_blocks: int32 [4, 64, 12, 3], P('wt', 'ctx'), may hold values from 0 to 63, as said below
- query_weight: bfloat16 [768, 768], P('wt'), may hold values from -0.4375 to 0.4375
- key_weight: bfloat16 [768, 768], P('wt'), may hold values from -0.21875 to 0.21875
- value_weight: bfloat16 [768, 768], P('wt'), may hold values from -0.21875 to 0.21875
- output_weight: bfloat16 [768, 768], P('wt'), may hold values from -0.875 to 0.875
- expand_weight: bfloat16 [768, 3072], P('wt'), may hold values from -0.21875 to 0.21875
- contract_weight: bfloat16 [3072, 768], P('wt'), may hold values from -0.15625 to 0.15625
- query_bias: bfloat16 [768], P('wt'), may hold values from -3 to 3
- value_bias: bfloat16 [768], P('wt'), may hold values from -3 to 3
- output_bias: bfloat16 [768], P('wt'), may hold values from -2 to 2
- expand_bias: bfloat16 [3072], P('wt'), may hold values from -2 to 2
- contract_bias: bfloat16 [768], P('wt'), may hold values from -2 to 2
- attn_gain: bfloat16 [768], P('wt'), may hold values from 0.5 to 1.5
- attn_shift: bfloat16 [768], P('wt'), may hold values from -2 to 2
- ffn_gain: bfloat16 [768], P('wt'), may hold values from 0.5 to 1.5
- ffn_shift: bfloat16 [768], P('wt'), may hold values from -2 to 2
Outputs:
- layer_out: bfloat16 [4, 4096, 768], P('wt', 'ctx')
- input_grad: float32 [4, 4096, 768], P('wt', 'ctx')
- query_wgrad: float32 [768, 768], P('wt')
- key_wgrad: float32 [768, 768], P('wt')
- value_wgrad: float32 [768, 768], P('wt')
- output_wgrad: float32 [768, 768], P('wt')
- expand_wgrad: float32 [768, 3072], P('wt')
- contract_wgrad: float32 [3072, 768], P('wt')
- query_bgrad: float32 [768], P('wt')
- value_bgrad: float32 [768], P('wt')
- output_bgrad: float32 [768], P('wt')
- expand_bgrad: float32 [3072], P('wt')
- contract_bgrad: float32 [768], P('wt')
- attn_ggrad: float32 [768], P('wt')
- attn_sgrad: float32 [768], P('wt')
- ffn_ggrad: float32 [768], P('wt')
- ffn_sgrad: float32 [768], P('wt')
Inputs may be any that keep to these rules, and one draw needn't show every extreme that they name: `lengths`: one sequence has exactly 4096 tokens. `rand_blocks`: entries of the row blocks of shard k (blocks k*8 .. k*8 + 7), for one head, are 24 blocks that lie, in a drawn order, one each on the shards k+1, k+2, ..., k+24, counted cyclically over the 8 shards; the block within that shard is drawn uniformly. So over all heads at most 36 entries of one shard lie on any one shard, and exactly 36 lie on the next shard. Entries of the first 2 row blocks are not used.
All inputs are finite; a program needn't handle non-finite values.
Results may differ from a plain program's by a relative error of at most 0.02.
Values may be sent and summed in bfloat16 or wider, within the bound.
No kernel may reach another device: no remote copies, remote signals or barrier semaphores. Data moves between devices by JAX's collectives and lax.ppermute only.
A program may use at most 384 MiB of HBM per device.

v0:
```python
from functools import partial

import jax
import jax.numpy as jnp
from jax import lax
from jax.sharding import PartitionSpec as P

H = 12
HD = 64
BLOCK = 64
GLOB = 2
RAND = 3


NEGATIVE = -1e30
EPSILON = 1e-12


def extended(shard, sides, width):
    for axis, dim in sides:
        peers, length = (lax.axis_size(axis), shard.shape[dim])
        up = [(i, (i + 1) % peers) for i in range(peers - 1)]
        down = [(j, i) for i, j in up]
        last = lax.slice_in_dim(shard, length - width, length, axis=dim)
        initial = lax.slice_in_dim(shard, 0, width, axis=dim)
        before = lax.ppermute(last, axis, up)
        after = lax.ppermute(initial, axis, down)
        shard = jnp.concatenate([before, shard, after], axis=dim)
    return shard


def spread(block, axis, source):
    block = jnp.where(lax.axis_index(axis) == source, block, jnp.zeros_like(block))
    return lax.psum(block, axis)


def combined_all(value, axis, join):
    pieces = jax.tree.map(lambda part: lax.all_gather(part, axis), value)
    head = jax.tree.map(lambda part: part[0], pieces)
    tail = jax.tree.map(lambda part: part[1:], pieces)
    running, _ = lax.scan(lambda running, slab: (join(running, slab), None), head, tail)
    return running


def layer_norm(values, norm_gain, norm_shift):
    centered = values - jnp.mean(values, axis=-1, keepdims=True)
    variance = jnp.mean(centered * centered, axis=-1, keepdims=True)
    return centered * lax.rsqrt(variance + EPSILON) * norm_gain + norm_shift


def inner_rows(left_side, right_side):
    return lax.dot_general(
        left_side, right_side, (((0,), (0,)), ((), ())), preferred_element_type=jnp.float32
    )


def times_transpose(left_side, right_side):
    return lax.dot_general(
        left_side, right_side, (((1,), (1,)), ((), ())), preferred_element_type=jnp.float32
    )


def block_products(query_side, window_side, global_side, random_side):
    global_part = jnp.einsum(
        "bqhd,jrhd->bhqjr", query_side, global_side, preferred_element_type=jnp.float32
    )
    window_part = jnp.einsum(
        "bqhd,bjrhd->bhqjr", query_side, window_side, preferred_element_type=jnp.float32
    )
    random_part = jnp.einsum(
        "bqhd,bhjrd->bhqjr", query_side, random_side, preferred_element_type=jnp.float32
    )
    return jnp.concatenate([global_part, window_part, random_part], axis=3)


def block_combine(weights, window_side, global_side, random_side):
    global_part = jnp.einsum(
        "bhqjr,jrhd->bqhd", weights[:, :, :, :GLOB], global_side, preferred_element_type=jnp.float32
    )
    window_part = jnp.einsum(
        "bhqjr,bjrhd->bqhd",
        weights[:, :, :, GLOB : GLOB + 3],
        window_side,
        preferred_element_type=jnp.float32,
    )
    random_part = jnp.einsum(
        "bhqjr,bhjrd->bqhd",
        weights[:, :, :, GLOB + 3 :],
        random_side,
        preferred_element_type=jnp.float32,
    )
    return global_part + window_part + random_part


def block_spread(weights, query_side):
    window_part = jnp.einsum(
        "bhqjr,bqhd->bjrhd",
        weights[:, :, :, GLOB : GLOB + 3],
        query_side,
        preferred_element_type=jnp.float32,
    )
    global_part = jnp.einsum(
        "bhqjr,bqhd->jrhd", weights[:, :, :, :GLOB], query_side, preferred_element_type=jnp.float32
    )
    random_part = jnp.einsum(
        "bhqjr,bqhd->bhjrd",
        weights[:, :, :, GLOB + 3 :],
        query_side,
        preferred_element_type=jnp.float32,
    )
    return (window_part, global_part, random_part)


def merge_parts(earlier, latter):
    summit = jnp.maximum(earlier[0], latter[0])
    weight_early = jnp.exp(earlier[0] - summit)
    weight_late = jnp.exp(latter[0] - summit)
    return (
        summit,
        earlier[1] * weight_early + latter[1] * weight_late,
        earlier[2] * weight_early[..., None] + latter[2] * weight_late[..., None],
    )


def body(
    tokens,
    cotangent,
    lengths,
    rand_blocks,
    query_weight,
    key_weight,
    value_weight,
    output_weight,
    expand_weight,
    contract_weight,
    query_bias,
    value_bias,
    output_bias,
    expand_bias,
    contract_bias,
    attn_gain,
    attn_shift,
    ffn_gain,
    ffn_shift,
):
    shards = lax.axis_size("ctx")
    shard_index = lax.axis_index("ctx")
    row_count = tokens.shape[1]
    model_width = tokens.shape[2]
    row_blocks = row_count // BLOCK
    global_count = GLOB * BLOCK
    factor = HD ** (-0.5)
    capacity = H * ((RAND * row_blocks + shards - 1) // shards)
    (
        w_query,
        w_key,
        w_value,
        w_output,
        w_expand,
        w_contract,
        b_query,
        b_value,
        b_output,
        b_expand,
        b_contract,
        g_attn,
        s_attn,
        g_ffn,
        s_ffn,
    ) = (
        lax.all_gather(query_weight, "wt", axis=0, tiled=True),
        lax.all_gather(key_weight, "wt", axis=0, tiled=True),
        lax.all_gather(value_weight, "wt", axis=0, tiled=True),
        lax.all_gather(output_weight, "wt", axis=0, tiled=True),
        lax.all_gather(expand_weight, "wt", axis=0, tiled=True),
        lax.all_gather(contract_weight, "wt", axis=0, tiled=True),
        lax.all_gather(query_bias, "wt", axis=0, tiled=True),
        lax.all_gather(value_bias, "wt", axis=0, tiled=True),
        lax.all_gather(output_bias, "wt", axis=0, tiled=True),
        lax.all_gather(expand_bias, "wt", axis=0, tiled=True),
        lax.all_gather(contract_bias, "wt", axis=0, tiled=True),
        lax.all_gather(attn_gain, "wt", axis=0, tiled=True),
        lax.all_gather(attn_shift, "wt", axis=0, tiled=True),
        lax.all_gather(ffn_gain, "wt", axis=0, tiled=True),
        lax.all_gather(ffn_shift, "wt", axis=0, tiled=True),
    )
    inputs = tokens[0]
    length = lengths[0]
    positions = shard_index * row_count + jnp.arange(row_count, dtype=jnp.int32)
    usable = positions < length
    queries = (
        jnp.dot(inputs, w_query, preferred_element_type=jnp.float32) + b_query.astype(jnp.float32)
    ).astype(jnp.bfloat16)
    key_rows = jnp.dot(inputs, w_key, preferred_element_type=jnp.float32).astype(jnp.bfloat16)
    value_rows = (
        jnp.dot(inputs, w_value, preferred_element_type=jnp.float32) + b_value.astype(jnp.float32)
    ).astype(jnp.bfloat16)
    local_keys = key_rows.reshape(row_count, H, HD)
    local_values = value_rows.reshape(row_count, H, HD)
    kv_rows = jnp.stack([local_keys, local_values], axis=2).reshape(row_count, 2 * model_width)
    kv_halo = extended(kv_rows, (("ctx", 0),), BLOCK)
    halo_blocks = kv_halo.reshape(row_blocks + 2, BLOCK, H, 2, HD)
    window_kv = jnp.stack(
        [
            halo_blocks[0:row_blocks],
            halo_blocks[1 : row_blocks + 1],
            halo_blocks[2 : row_blocks + 2],
        ],
        axis=1,
    )
    halo_positions = (
        shard_index * row_count - BLOCK + jnp.arange(row_count + 2 * BLOCK, dtype=jnp.int32)
    )
    halo_usable = ((halo_positions >= 0) & (halo_positions < length)).reshape(row_blocks + 2, BLOCK)
    window_usable = jnp.stack(
        [
            halo_usable[0:row_blocks],
            halo_usable[1 : row_blocks + 1],
            halo_usable[2 : row_blocks + 2],
        ],
        axis=1,
    )
    packed = spread(
        jnp.concatenate([queries[:global_count], kv_rows[:global_count]], axis=1), "ctx", 0
    )
    global_queries = packed[:, :model_width].reshape(global_count, H, HD)
    global_kv = packed[:, model_width:].reshape(GLOB, BLOCK, H, 2, HD)
    block_table = rand_blocks[0]
    owners = (block_table // row_blocks).reshape(-1)
    block_codes = (
        block_table % row_blocks * H + jnp.arange(H, dtype=jnp.int32)[None, :, None]
    ).reshape(-1)
    matches = (owners[:, None] == jnp.arange(shards, dtype=jnp.int32)[None, :]).astype(jnp.int32)
    slot_ranks = jnp.sum((jnp.cumsum(matches, axis=0) - 1) * matches, axis=1)
    slot_index = owners * capacity + slot_ranks
    requests = jnp.zeros((shards * capacity,), jnp.int32).at[slot_index].set(block_codes)
    wanted = lax.all_to_all(
        requests.reshape(shards, capacity), "ctx", split_axis=0, concat_axis=0, tiled=True
    )
    head_blocks = jnp.transpose(kv_rows.reshape(row_blocks, BLOCK, H, 2 * HD), (0, 2, 1, 3))
    head_blocks = head_blocks.reshape(row_blocks * H, BLOCK, 2 * HD)
    outgoing = jnp.take(head_blocks, wanted.reshape(-1), axis=0).reshape(
        shards, capacity, BLOCK, 2 * HD
    )
    arrived = lax.all_to_all(outgoing, "ctx", split_axis=0, concat_axis=0, tiled=True)
    random_kv = jnp.take(arrived.reshape(shards * capacity, BLOCK, 2 * HD), slot_index, axis=0)
    random_kv = random_kv.reshape(row_blocks, H, RAND, BLOCK, 2, HD)
    random_usable = block_table[..., None] * BLOCK + jnp.arange(BLOCK, dtype=jnp.int32) < length
    allowed = jnp.concatenate(
        [
            jnp.ones((row_blocks, H, 1, GLOB, BLOCK), jnp.bool_),
            jnp.broadcast_to(window_usable[:, None, None], (row_blocks, H, 1, 3, BLOCK)),
            random_usable[:, :, None],
        ],
        axis=3,
    )
    query_blocks = queries.reshape(row_blocks, BLOCK, H, HD)
    window_keys = window_kv[:, :, :, :, 0]
    window_values = window_kv[:, :, :, :, 1]
    global_keys = global_kv[:, :, :, 0]
    global_values = global_kv[:, :, :, 1]
    random_keys = random_kv[:, :, :, :, 0]
    random_values = random_kv[:, :, :, :, 1]
    scores = jnp.where(
        allowed,
        block_products(query_blocks, window_keys, global_keys, random_keys) * factor,
        NEGATIVE,
    )
    summit = jnp.max(scores, axis=(3, 4), keepdims=True)
    totals = jnp.sum(jnp.where(allowed, jnp.exp(scores - summit), 0.0), axis=(3, 4), keepdims=True)
    log_total = summit + jnp.log(totals)
    probabilities = jnp.where(allowed, jnp.exp(scores - log_total), 0.0)
    probs_low = probabilities.astype(jnp.bfloat16)
    window_out = block_combine(probs_low, window_values, global_values, random_values)
    window_out = window_out.reshape(row_count, model_width)
    global_scores = jnp.where(
        usable[None, None, :],
        jnp.einsum("qhd,khd->hqk", global_queries, local_keys, preferred_element_type=jnp.float32)
        * factor,
        NEGATIVE,
    )
    local_top = jnp.max(global_scores, axis=2)
    raised = jnp.where(usable[None, None, :], jnp.exp(global_scores - local_top[..., None]), 0.0)
    value_float = local_values.astype(jnp.float32)
    partial_out = jnp.einsum("hqk,khd->hqd", raised, value_float, precision=lax.Precision.HIGHEST)
    top_all, total_all, out_all = combined_all(
        (local_top, jnp.sum(raised, axis=2), partial_out), "ctx", merge_parts
    )
    global_lse = top_all + jnp.log(total_all)
    global_out = jnp.transpose(out_all / total_all[..., None], (1, 0, 2))
    on_global = (shard_index == 0) & (jnp.arange(row_count) < global_count)
    padded_global = jnp.pad(
        global_out.reshape(global_count, model_width), ((0, row_count - global_count), (0, 0))
    )
    attended = jnp.where(on_global[:, None], padded_global, window_out)
    attended_low = attended.astype(jnp.bfloat16)
    branch = jnp.dot(attended_low, w_output, preferred_element_type=jnp.float32) + b_output.astype(
        jnp.float32
    )
    residual_one = inputs.astype(jnp.float32) + branch
    normed_one, first_back = jax.vjp(
        layer_norm, residual_one, g_attn.astype(jnp.float32), s_attn.astype(jnp.float32)
    )
    normed_low = normed_one.astype(jnp.bfloat16)
    expand = jnp.dot(normed_low, w_expand, preferred_element_type=jnp.float32) + b_expand.astype(
        jnp.float32
    )
    hidden_low = jax.nn.gelu(expand, approximate=True).astype(jnp.bfloat16)
    second = jnp.dot(
        hidden_low, w_contract, preferred_element_type=jnp.float32
    ) + b_contract.astype(jnp.float32)
    result, norm_back = jax.vjp(
        layer_norm, normed_one + second, g_ffn.astype(jnp.float32), s_ffn.astype(jnp.float32)
    )
    layer_out = jnp.where(usable[:, None], result, 0.0).astype(jnp.bfloat16)[None]
    grad_result = jnp.where(usable[:, None], cotangent[0].astype(jnp.float32), 0.0)
    grad_two, grad_gain_ffn, grad_shift_ffn = norm_back(grad_result)
    grad_second = grad_two.astype(jnp.bfloat16)
    contract_grad = inner_rows(hidden_low, grad_second)
    contract_bgrad = jnp.sum(grad_second.astype(jnp.float32), axis=0)
    grad_hidden = times_transpose(grad_second, w_contract)
    gelu_back = jax.vjp(partial(jax.nn.gelu, approximate=True), expand)[1]
    grad_expand = gelu_back(grad_hidden)[0].astype(jnp.bfloat16)
    expand_grad = inner_rows(normed_low, grad_expand)
    expand_bgrad = jnp.sum(grad_expand.astype(jnp.float32), axis=0)
    grad_first = grad_two + times_transpose(grad_expand, w_expand)
    grad_one, grad_gain_attn, grad_shift_attn = first_back(grad_first)
    grad_branch = grad_one.astype(jnp.bfloat16)
    output_grad = inner_rows(attended_low, grad_branch)
    output_bgrad = jnp.sum(grad_branch.astype(jnp.float32), axis=0)
    grad_attended = times_transpose(grad_branch, w_output).astype(jnp.bfloat16)
    global_grad_out = spread(grad_attended[:global_count], "ctx", 0)
    global_grad_out = global_grad_out.reshape(global_count, H, HD)
    global_delta = jnp.sum(global_grad_out.astype(jnp.float32) * global_out, axis=2)
    global_probs = jnp.where(
        usable[None, None, :], jnp.exp(global_scores - global_lse[..., None]), 0.0
    )
    global_dprobs = jnp.einsum(
        "qhd,khd->hqk", global_grad_out, local_values, preferred_element_type=jnp.float32
    )
    global_dscores = (
        global_probs * (global_dprobs - jnp.transpose(global_delta)[..., None])
    ).astype(jnp.bfloat16)
    global_query_part = (
        jnp.einsum("hqk,khd->qhd", global_dscores, local_keys, preferred_element_type=jnp.float32)
        * factor
    )
    keys_from_global = (
        jnp.einsum(
            "hqk,qhd->khd", global_dscores, global_queries, preferred_element_type=jnp.float32
        )
        * factor
    )
    values_from_global = jnp.einsum(
        "hqk,qhd->khd",
        global_probs,
        global_grad_out.astype(jnp.float32),
        precision=lax.Precision.HIGHEST,
    )
    grad_blocks = jnp.where(on_global[:, None], jnp.zeros_like(grad_attended), grad_attended)
    grad_blocks = grad_blocks.reshape(row_blocks, BLOCK, H, HD)
    dprobs = block_products(grad_blocks, window_values, global_values, random_values)
    row_delta = jnp.sum(probabilities * dprobs, axis=(3, 4), keepdims=True)
    dscores = (probabilities * (dprobs - row_delta)).astype(jnp.bfloat16)
    grad_queries = block_combine(dscores, window_keys, global_keys, random_keys).reshape(
        row_count, model_width
    )
    grad_queries = grad_queries * factor
    key_window, key_global, key_random = block_spread(dscores, query_blocks)
    value_window, value_global, value_random = block_spread(probs_low, grad_blocks)
    grad_window = jnp.stack([key_window * factor, value_window], axis=4).reshape(
        row_blocks, 3, BLOCK, 2 * model_width
    )
    grad_global = jnp.stack([key_global * factor, value_global], axis=3).reshape(
        global_count, 2 * model_width
    )
    grad_random = jnp.stack([key_random * factor, value_random], axis=4).reshape(-1, BLOCK, 2 * HD)
    halo_grad = (
        jnp.pad(grad_window[:, 0], ((0, 2), (0, 0), (0, 0)))
        + jnp.pad(grad_window[:, 1], ((1, 1), (0, 0), (0, 0)))
        + jnp.pad(grad_window[:, 2], ((2, 0), (0, 0), (0, 0)))
    )
    rim_rows = jnp.concatenate([halo_grad[0], halo_grad[row_blocks + 1]], axis=0)
    returned = extended(rim_rows.astype(jnp.bfloat16), (("ctx", 0),), BLOCK).astype(rim_rows.dtype)
    kv_grad = halo_grad[1 : row_blocks + 1].reshape(row_count, 2 * model_width)
    kv_grad = (
        kv_grad.at[:BLOCK].add(returned[:BLOCK]).at[row_count - BLOCK :].add(returned[3 * BLOCK :])
    )
    sending = (
        jnp.zeros((shards * capacity, BLOCK, 2 * HD), jnp.float32).at[slot_index].set(grad_random)
    )
    came_back = lax.all_to_all(
        sending.reshape(shards, capacity, BLOCK, 2 * HD).astype(jnp.bfloat16),
        "ctx",
        split_axis=0,
        concat_axis=0,
        tiled=True,
    ).astype(jnp.float32)
    summed = jax.ops.segment_sum(
        came_back.reshape(shards * capacity, BLOCK, 2 * HD),
        wanted.reshape(-1),
        num_segments=row_blocks * H,
    )
    kv_grad = kv_grad + jnp.transpose(
        summed.reshape(row_blocks, H, BLOCK, 2 * HD), (0, 2, 1, 3)
    ).reshape(row_count, 2 * model_width)
    kv_grad = kv_grad + jnp.stack([keys_from_global, values_from_global], axis=2).reshape(
        row_count, 2 * model_width
    )
    query_sum, kv_sum = (
        lax.psum(
            global_query_part.reshape(global_count, model_width).astype(jnp.bfloat16), "ctx"
        ).astype(jnp.float32),
        lax.psum(grad_global.astype(jnp.bfloat16), "ctx").astype(jnp.float32),
    )
    first_rows = on_global[:, None]
    kv_grad = kv_grad + jnp.where(
        first_rows, jnp.pad(kv_sum, ((0, row_count - global_count), (0, 0))), 0.0
    )
    grad_queries = grad_queries + jnp.where(
        first_rows, jnp.pad(query_sum, ((0, row_count - global_count), (0, 0))), 0.0
    )
    kv_split = kv_grad.reshape(row_count, H, 2, HD)
    grad_keys = kv_split[:, :, 0].reshape(row_count, model_width).astype(jnp.bfloat16)
    grad_values = kv_split[:, :, 1].reshape(row_count, model_width).astype(jnp.bfloat16)
    grad_query_low = grad_queries.astype(jnp.bfloat16)
    query_grad = inner_rows(inputs, grad_query_low)
    query_bgrad = jnp.sum(grad_query_low.astype(jnp.float32), axis=0)
    key_grad = inner_rows(inputs, grad_keys)
    value_grad = inner_rows(inputs, grad_values)
    value_bgrad = jnp.sum(grad_values.astype(jnp.float32), axis=0)
    input_grad = (
        grad_one
        + times_transpose(grad_query_low, w_query)
        + times_transpose(grad_keys, w_key)
        + times_transpose(grad_values, w_value)
    )
    gradients = [
        query_grad,
        key_grad,
        value_grad,
        output_grad,
        expand_grad,
        contract_grad,
        query_bgrad,
        value_bgrad,
        output_bgrad,
        expand_bgrad,
        contract_bgrad,
        grad_gain_attn,
        grad_shift_attn,
        grad_gain_ffn,
        grad_shift_ffn,
    ]
    pieces = (
        lax.psum_scatter(
            gradients[0].astype(jnp.bfloat16), "wt", scatter_dimension=0, tiled=True
        ).astype(jnp.float32),
        lax.psum_scatter(
            gradients[1].astype(jnp.bfloat16), "wt", scatter_dimension=0, tiled=True
        ).astype(jnp.float32),
        lax.psum_scatter(
            gradients[2].astype(jnp.bfloat16), "wt", scatter_dimension=0, tiled=True
        ).astype(jnp.float32),
        lax.psum_scatter(
            gradients[3].astype(jnp.bfloat16), "wt", scatter_dimension=0, tiled=True
        ).astype(jnp.float32),
        lax.psum_scatter(
            gradients[4].astype(jnp.bfloat16), "wt", scatter_dimension=0, tiled=True
        ).astype(jnp.float32),
        lax.psum_scatter(
            gradients[5].astype(jnp.bfloat16), "wt", scatter_dimension=0, tiled=True
        ).astype(jnp.float32),
        lax.psum_scatter(
            gradients[6].astype(jnp.bfloat16), "wt", scatter_dimension=0, tiled=True
        ).astype(jnp.float32),
        lax.psum_scatter(
            gradients[7].astype(jnp.bfloat16), "wt", scatter_dimension=0, tiled=True
        ).astype(jnp.float32),
        lax.psum_scatter(
            gradients[8].astype(jnp.bfloat16), "wt", scatter_dimension=0, tiled=True
        ).astype(jnp.float32),
        lax.psum_scatter(
            gradients[9].astype(jnp.bfloat16), "wt", scatter_dimension=0, tiled=True
        ).astype(jnp.float32),
        lax.psum_scatter(
            gradients[10].astype(jnp.bfloat16), "wt", scatter_dimension=0, tiled=True
        ).astype(jnp.float32),
        lax.psum_scatter(
            gradients[11].astype(jnp.bfloat16), "wt", scatter_dimension=0, tiled=True
        ).astype(jnp.float32),
        lax.psum_scatter(
            gradients[12].astype(jnp.bfloat16), "wt", scatter_dimension=0, tiled=True
        ).astype(jnp.float32),
        lax.psum_scatter(
            gradients[13].astype(jnp.bfloat16), "wt", scatter_dimension=0, tiled=True
        ).astype(jnp.float32),
        lax.psum_scatter(
            gradients[14].astype(jnp.bfloat16), "wt", scatter_dimension=0, tiled=True
        ).astype(jnp.float32),
    )
    shares = (
        lax.psum(pieces[0].astype(jnp.bfloat16), "ctx").astype(jnp.float32),
        lax.psum(pieces[1].astype(jnp.bfloat16), "ctx").astype(jnp.float32),
        lax.psum(pieces[2].astype(jnp.bfloat16), "ctx").astype(jnp.float32),
        lax.psum(pieces[3].astype(jnp.bfloat16), "ctx").astype(jnp.float32),
        lax.psum(pieces[4].astype(jnp.bfloat16), "ctx").astype(jnp.float32),
        lax.psum(pieces[5].astype(jnp.bfloat16), "ctx").astype(jnp.float32),
        lax.psum(pieces[6].astype(jnp.bfloat16), "ctx").astype(jnp.float32),
        lax.psum(pieces[7].astype(jnp.bfloat16), "ctx").astype(jnp.float32),
        lax.psum(pieces[8].astype(jnp.bfloat16), "ctx").astype(jnp.float32),
        lax.psum(pieces[9].astype(jnp.bfloat16), "ctx").astype(jnp.float32),
        lax.psum(pieces[10].astype(jnp.bfloat16), "ctx").astype(jnp.float32),
        lax.psum(pieces[11].astype(jnp.bfloat16), "ctx").astype(jnp.float32),
        lax.psum(pieces[12].astype(jnp.bfloat16), "ctx").astype(jnp.float32),
        lax.psum(pieces[13].astype(jnp.bfloat16), "ctx").astype(jnp.float32),
        lax.psum(pieces[14].astype(jnp.bfloat16), "ctx").astype(jnp.float32),
    )
    return (
        layer_out,
        input_grad[None],
        shares[0],
        shares[1],
        shares[2],
        shares[3],
        shares[4],
        shares[5],
        shares[6],
        shares[7],
        shares[8],
        shares[9],
        shares[10],
        shares[11],
        shares[12],
        shares[13],
        shares[14],
    )


def solution(mesh):
    placed = (
        P("wt", "ctx", None),
        P("wt", "ctx", None),
        P("wt"),
        P("wt", "ctx", None, None),
        P("wt", None),
        P("wt", None),
        P("wt", None),
        P("wt", None),
        P("wt", None),
        P("wt", None),
        P("wt"),
        P("wt"),
        P("wt"),
        P("wt"),
        P("wt"),
        P("wt"),
        P("wt"),
        P("wt"),
        P("wt"),
    )
    return jax.shard_map(
        body,
        mesh=mesh,
        in_specs=placed,
        out_specs=(
            P("wt", "ctx", None),
            P("wt", "ctx", None),
            P("wt", None),
            P("wt", None),
            P("wt", None),
            P("wt", None),
            P("wt", None),
            P("wt", None),
            P("wt"),
            P("wt"),
            P("wt"),
            P("wt"),
            P("wt"),
            P("wt"),
            P("wt"),
            P("wt"),
            P("wt"),
        ),
        check_vma=False,
    )
```

profile of v0, /device:TPU:0, one launch (start us, length us, event | category | flops | bytes accessed | tf_op | source)
XLA Modules:
  0.0 1364.2 jit_solution(2464391503254816998)
XLA Ops:
  17.3 21.2 %all-reduce.28 = (bf16[768]{0:T(1024)(128)(2,1)S(1)}, bf16[768]{0:T(1024)(128)(2,1)S(1)}, bf16[768]{0:T(1024)(128)(2,1)S(1)}, bf16[768]{0:T(1024)(128)(2,1)S(1)}...) all-reduce(bf16[768]{0:T(1024)(128)(2,1)S(1)} %dynamic-update-slice, ...), channel_id=1, replica_groups=mesh['ctx'=8,'wt'=4] {'wt'}, use_global_device_ids=true, to_apply=%add.9 | all-reduce | flops 5376 | bytes 21504
  45.5 29.0 %all-gather.16.cloned.1.call-done = bf16[768,768]{1,0:T(8,128)(2,1)} async-done(((bf16[192,768]{1,0:T(8,128)(2,1)}), bf16[768,768]{1,0:T(8,128)(2,1)}) %all-gather.16.cloned.1.call-update) | async-done | bytes 1179664 | tf_op jit(solution)/shard_map/all_gather | solution.py:172
  76.9 28.7 %all-gather.14.cloned.1.call-done = bf16[768,768]{1,0:T(8,128)(2,1)} async-done(((bf16[192,768]{1,0:T(8,128)(2,1)}), bf16[768,768]{1,0:T(8,128)(2,1)}) %all-gather.14.cloned.1.call-update) | async-done | bytes 1179664 | tf_op jit(solution)/shard_map/all_gather | solution.py:171
  110.7 53.5 %all-reduce.34.cloned.1.call-done = bf16[128,2304]{0,1:T(8,128)(2,1)} async-done(((bf16[128,2304]{0,1:T(8,128)(2,1)}), bf16[128,2304]{0,1:T(8,128)(2,1)}) %all-reduce.34.cloned.1.call-update) | async-done | bytes 589840 | tf_op jit(solution)/shard_map/psum | solution.py:34
  183.6 13.3 all-gather.5
  209.2 13.3 gather_fusion
  297.0 47.0 %all-gather.3 = f32[8,12,128]{2,1,0:T(8,128)S(1)} all-gather(f32[1,12,128]{2,1,0:T(8,128)S(1)} %bitcast.408), channel_id=2, replica_groups=mesh['ctx'=8,'wt'=4] {'ctx'}, dimensions={0}, use_global_device_ids=true | all-gather | bytes 55296 | tf_op jit(solution)/shard_map/all_gather | solution.py:38
  365.6 16.5 %gather.15 = bf16[8,12,3,64,2,64]{5,4,3,2,1,0:T(2,128)(2,1)} reshape(bf16[288,64,128]{2,1,0:T(8,128)(2,1)} %gather_fusion.1) | data formatting | bytes 9437184 | tf_op jit(solution)/shard_map/jit(_take)/gather | solution.py:246
  398.0 10.8 slice_bitcast_fusion.1
  408.8 12.8 fusion.157
  421.7 12.9 select_reduce_fusion
  435.3 12.4 fusion.4
  477.1 14.5 %while.16 = (s32[]{:T(128)}, f32[12,128]{1,0:T(8,128)S(1)}, f32[12,128]{1,0:T(8,128)S(1)}, f32[12,128,64]{2,1,0:T(8,128)S(1)}, f32[7,12,128]{2,1,0:T(8,128)S(1)}...) while((s32[]{:T(128)}, f32[12,128]{1,0:T(8,128)S(1)}, f32[12,128]{1,0:T(8,128)S(1)}, ...), condition=%wide.region_4.5_spmd, body=%wide.region_3.4_spmd.sunk | while | flops 304130 | bytes 2814053 | solution.py:41
  561.6 15.4 %multiply_reduce_fusion = f32[8,12,64]{2,1,0:T(8,128)S(1)} fusion(f32[8,12,64,3,64]{2,4,3,1,0:T(8,128)} %fusion.112, f32[8,12,64,3,64]{2,4,3,1,0:T(8,128)} %bitcast.357, f32[8,12,64,2,64]{2,4,3,1,0:T(8,128)} %convolution_bitcast_fusion.2, f32[8,12,64]{2,1,0:T(8,128)S(1)} %copy-done.58, pred[8,12,8,64]{3,2,1,0:T(8,128)(4,1)S(1)} %copy-done.39, ...), kind=kLoop, calls=%fused_computation.18 | loop fusion | flops 31451136 | bytes 25264128 | tf_op jit(solution)/shard_map/reduce_sum | solution.py:363
  577.1 16.9 %multiply_convert_fusion = bf16[8,12,64,8,64]{2,4,3,1,0:T(8,128)(2,1)} fusion(f32[8,12,64,3,64]{2,4,3,1,0:T(8,128)} %fusion.112, f32[8,12,64,3,64]{2,4,3,1,0:T(8,128)} %bitcast.358, f32[8,12,64,2,64]{2,4,3,1,0:T(8,128)} %convolution_bitcast_fusion.2, f32[8,12,64]{2,1,0:T(8,128)S(1)} %multiply_reduce_fusion, f32[8,12,64]{2,1,0:T(8,128)S(1)} %copy-done.58, ...), kind=kLoop, calls=%fused_computation.17 | loop fusion | flops 34603008 | bytes 31555584 | tf_op jit(solution)/shard_map/convert_element_type | solution.py:364
  594.0 10.8 fusion.168
  627.9 11.3 pad_maximum_fusion.1
  639.2 26.3 %copy.317 = f32[8,3,64,12,2,64]{5,4,3,2,1,0:T(2,128)} copy(f32[8,3,64,12,2,64]{2,5,1,3,0,4:T(8,128)} %pad_maximum_fusion.1) | data formatting | bytes 18874368 | tf_op jit(solution)/shard_map/stack | solution.py:371
  665.5 21.6 %reshape.530 = f32[8,3,64,1536]{3,2,1,0:T(8,128)} reshape(f32[8,3,64,12,2,64]{5,4,3,2,1,0:T(2,128)} %copy.317) | data formatting | bytes 18874368 | tf_op jit(solution)/shard_map/reshape | solution.py:371
  702.4 15.1 %copy.322 = f32[8,12,3,64,2,64]{5,4,3,2,1,0:T(2,128)} copy(f32[8,12,3,64,2,64]{5,3,2,1,0,4:T(8,128)S(1)} %pad_maximum_fusion.2) | data formatting | bytes 18874368 | tf_op jit(solution)/shard_map/stack | solution.py:377
  717.5 18.1 %reshape.572 = f32[288,64,128]{2,1,0:T(8,128)} reshape(f32[8,12,3,64,2,64]{5,4,3,2,1,0:T(2,128)} %copy.322) | data formatting | bytes 18874368 | tf_op jit(solution)/shard_map/reshape | solution.py:377
  740.4 42.7 %scatter_fusion = f32[288,64,128]{2,1,0:T(8,128)} fusion(f32[288,64,128]{2,1,0:T(8,128)} %broadcast_in_dim.215, s32[288]{0:T(512)S(1)} %copy-done.94, f32[288,64,128]{2,1,0:T(8,128)} %reshape.572), kind=kCustom, calls=%fused_computation.3 | custom fusion | bytes 28312704 | tf_op jit(solution)/shard_map/scatter | solution.py:390
  838.6 42.8 %all-reduce.36.cloned.1.call-done = bf16[128,12,64]{0,2,1:T(8,128)(2,1)} async-done(((bf16[128,12,64]{0,2,1:T(8,128)(2,1)}), bf16[128,12,64]{0,2,1:T(8,128)(2,1)}) %all-reduce.36.cloned.1.call-update) | async-done | bytes 196624 | tf_op jit(solution)/shard_map/psum | solution.py:34
  894.3 52.5 %all-reduce.40.cloned.1.call-done = (bf16[128,768]{1,0:T(8,128)(2,1)}, bf16[128,1536]{1,0:T(8,128)(2,1)}) async-done(((bf16[128,768]{1,0:T(8,128)(2,1)}, bf16[128,1536]{1,0:T(8,128)(2,1)}), (bf16[128,768]{1,0:T(8,128)(2,1)}, bf16[128,1536]{1,0:T(8,128)(2,1)})) %all-reduce.40.cloned.1.call-update) | async-done | bytes 589840 | tf_op jit(solution)/shard_map/psum | solution.py:411
  961.3 29.8 %scatter_fusion.1 = f32[96,64,128]{2,1,0:T(8,128)S(1)} fusion(f32[96,64,128]{2,1,0:T(8,128)S(1)} %broadcast_in_dim.214, s32[288]{0:T(512)S(1)} %copy-done.100, f32[288,64,128]{2,1,0:T(8,128)} %bitcast_convert_fusion), kind=kCustom, calls=%fused_computation.4 | custom fusion | flops 2359296 | bytes 28312704 | tf_op jit(solution)/shard_map/scatter-add | solution.py:399
  1030.6 28.3 %reduce-scatter.23.cloned.1.call-done = bf16[192,768]{1,0:T(8,128)(2,1)} async-done(((bf16[768,768]{1,0:T(8,128)(2,1)}), bf16[192,768]{1,0:T(8,128)(2,1)}) %reduce-scatter.23.cloned.1.call-update) | async-done | bytes 294928
  1060.8 28.2 %reduce-scatter.13.cloned.1.call-done = bf16[192,768]{1,0:T(8,128)(2,1)} async-done(((bf16[768,768]{1,0:T(8,128)(2,1)}), bf16[192,768]{1,0:T(8,128)(2,1)}) %reduce-scatter.13.cloned.1.call-update) | async-done | bytes 294928 | tf_op jit(solution)/shard_map/reduce_scatter | solution.py:465
  1089.1 86.2 %reduce-scatter.15.cloned.1.call-done = bf16[192,3072]{1,0:T(8,128)(2,1)} async-done(((bf16[768,3072]{1,0:T(8,128)(2,1)}), bf16[192,3072]{1,0:T(8,128)(2,1)}) %reduce-scatter.15.cloned.1.call-update) | async-done | bytes 1179664 | tf_op jit(solution)/shard_map/reduce_scatter | solution.py:468
  1175.2 88.0 %reduce-scatter.17.cloned.1.call-done = bf16[768,768]{1,0:T(8,128)(2,1)} async-done(((bf16[3072,768]{1,0:T(8,128)(2,1)}), bf16[768,768]{1,0:T(8,128)(2,1)}) %reduce-scatter.17.cloned.1.call-update) | async-done | bytes 1179664 | tf_op jit(solution)/shard_map/reduce_scatter | solution.py:471
  1268.3 18.3 %all-reduce.27 = (bf16[768]{0:T(1024)(128)(2,1)S(1)}, bf16[768]{0:T(1024)(128)(2,1)S(1)}, bf16[768]{0:T(1024)(128)(2,1)S(1)}, bf16[768]{0:T(1024)(128)(2,1)S(1)}...) all-reduce(bf16[768]{0:T(1024)(128)(2,1)S(1)} %dynamic-update-slice, ...), channel_id=1, replica_groups=mesh['ctx'=8,'wt'=4] {'wt'}, use_global_device_ids=true, to_apply=%add.14 | all-reduce | flops 9984 | bytes 39936
  1287.3 12.0 all-reduce.24
  1310.8 36.3 %all-reduce.38.cloned.1.call-done = (bf16[192,768]{0,1:T(8,128)(2,1)}, bf16[192,768]{0,1:T(8,128)(2,1)}, bf16[192,768]{0,1:T(8,128)(2,1)}, bf16[192,768]{1,0:T(8...) async-done(((bf16[192,768]{0,1:T(8,128)(2,1)}, bf16[192,768]{0,1:T(8,128)(2,1)}, bf16[192,768]{0,1:T(8,128)(2,1)}, bf16[192,768]{1,0:T(8,128)(2,1)}, ...) | async-done | bytes 3538960 | tf_op jit(solution)/shard_map/psum | solution.py:503
  (623 shorter events, 472.5 us)
Async XLA Ops:
  7.2 35.7 %all-gather.18.cloned.1.call-start = ((), (), s32[]{:S(2)}) async-start(), calls=%async_computation.11 | async-start | bytes 1474560 | tf_op jit(solution)/shard_map/all_gather | solution.py:173
  7.9 66.5 %all-gather.16.cloned.1.call-start = ((), (), s32[]{:S(2)}) async-start(), calls=%async_computation.10 | async-start | bytes 1474560 | tf_op jit(solution)/shard_map/all_gather | solution.py:172
  8.7 97.0 %all-gather.14.cloned.1.call-start = ((), (), s32[]{:S(2)}) async-start(), calls=%async_computation.9 | async-start | bytes 1474560 | tf_op jit(solution)/shard_map/all_gather | solution.py:171
  9.4 154.7 %all-reduce.34.cloned.1.call-start = ((), (), s32[]{:S(2)}) async-start(), calls=%async_computation.12 | async-start | bytes 1179648 | tf_op jit(solution)/shard_map/psum | solution.py:34
  45.4 186.0 %copy-start.16 = (bf16[512,768]{0,1:T(8,128)(2,1)}, bf16[512,768]{0,1:T(8,128)(2,1)S(1)}, u32[]{:S(2)}) copy-start(bf16[512,768]{0,1:T(8,128)(2,1)S(1)} %copy.255) | copy-start | bytes 2359300
  76.8 154.6 %copy-start.12 = (bf16[512,768]{0,1:T(8,128)(2,1)}, bf16[512,768]{0,1:T(8,128)(2,1)S(1)}, u32[]{:S(2)}) copy-start(bf16[512,768]{0,1:T(8,128)(2,1)S(1)} %copy.254) | copy-start | bytes 2359300
  110.0 361.8 %all-gather.26.cloned.1.call-start = ((), (), s32[]{:S(2)}) async-start(), calls=%async_computation.20 | async-start | bytes 3538944 | tf_op jit(solution)/shard_map/all_gather | solution.py:38
  110.7 402.1 %copy-start.86 = (pred[512]{0:T(512)(128)(4,1)}, pred[512]{0:T(512)(128)(4,1)S(1)}, u32[]{:S(2)}) copy-start(pred[512]{0:T(512)(128)(4,1)S(1)} %add_compare_fusion.1) | copy-start | bytes 1540
  170.7 321.9 %all-gather.20.cloned.1.call-start = ((), (), s32[]{:S(2)}) async-start(), calls=%async_computation.13 | async-start | bytes 1474560 | tf_op jit(solution)/shard_map/all_gather | solution.py:174
  171.3 324.2 %all-gather.22.cloned.1.call-start = ((), (), s32[]{:S(2)}) async-start(), calls=%async_computation.14 | async-start | bytes 5898240 | tf_op jit(solution)/shard_map/all_gather | solution.py:175
  177.7 23.0 %all-to-all-start = ((s32[8,1,36]{2,1,0:T(1,128)}), s32[8,1,36]{2,1,0:T(1,128)S(1)}, u32[]{:S(2)}, u32[]{:S(2)}) async-start(s32[8,1,36]{2,1,0:T(1,128)} %all_to_all.12), calls=%async_computation | async-start | bytes 8192 | tf_op jit(solution)/shard_map/all_to_all | solution.py:237
  181.0 321.8 %all-gather.24.cloned.1.call-start = ((), (), s32[]{:S(2)}) async-start(), calls=%async_computation.15 | async-start | bytes 5898240 | tf_op jit(solution)/shard_map/all_gather | solution.py:176
  200.6 312.1 %copy-start.79 = (f32[768]{0:T(1024)}, f32[768]{0:T(1024)S(1)}, u32[]{:S(2)}) copy-start(f32[768]{0:T(1024)S(1)} %convert_element_type.279) | copy-start | bytes 9220
  226.8 132.9 %all-to-all-start.1 = ((bf16[8,36,64,128]{3,2,1,0:T(8,128)(2,1)}), bf16[8,36,64,128]{3,2,1,0:T(8,128)(2,1)}, u32[]{:S(2)}, u32[]{:S(2)}) async-start(bf16[8,36,64,128]{3,2,1,0:T(8,128)(2,1)} %broadcast_select_fusion), calls=%async_computation.1 | async-start | bytes 9437184 | tf_op jit(solution)/shard_map/all_to_all | solution.py:245
  232.3 19.0 %collective-permute-start = (bf16[64,1536]{1,0:T(8,128)(2,1)S(1)}, bf16[64,1536]{1,0:T(8,128)(2,1)}, u32[]{:S(2)}, u32[]{:S(2)}) collective-permute-start(bf16[64,1536]{1,0:T(8,128)(2,1)S(1)} %slice.217), channel_id=1, source_target_pairs={{0,4},{4,8},{8,12},{12,16},{16,20},{20,24},{24,28},{1,5},{5,9},{9,... | collective-permute-start | bytes 589832 | tf_op jit(solution)/shard_map/ppermute | solution.py:26
  236.0 16.4 %collective-permute-start.1 = (bf16[64,1536]{0,1:T(8,128)(2,1)}, bf16[64,1536]{0,1:T(8,128)(2,1)}, u32[]{:S(2)}, u32[]{:S(2)}) collective-permute-start(bf16[64,1536]{0,1:T(8,128)(2,1)} %bitcast.30), channel_id=1, source_target_pairs={{4,0},{8,4},{12,8},{16,12},{20,16},{24,20},{28,24},{5,1},{9,5},{13... | collective-permute-start | bytes 589832 | tf_op jit(solution)/shard_map/ppermute | solution.py:27
  245.9 144.8 %copy-start.6 = (bf16[8,64,12,64]{1,0,3,2:T(8,128)(2,1)}, bf16[8,64,12,64]{1,0,3,2:T(8,128)(2,1)S(1)}, u32[]{:S(2)}) copy-start(bf16[8,64,12,64]{1,0,3,2:T(8,128)(2,1)S(1)} %reshape.519) | copy-start | bytes 2359300
  297.0 156.8 %copy-start.34 = (bf16[2,64,12,1,64]{1,4,0,2,3:T(8,128)(2,1)}, bf16[2,64,12,1,64]{1,4,0,2,3:T(8,128)(2,1)S(1)}, u32[]{:S(2)}) copy-start(bf16[2,64,12,1,64]{1,4,0,2,3:T(8,128)(2,1)S(1)} %copy.423) | copy-start | bytes 589828
  790.3 163.1 %all-to-all-start.2 = ((bf16[8,36,64,128]{3,2,1,0:T(8,128)(2,1)}), bf16[8,36,64,128]{3,2,1,0:T(8,128)(2,1)}, u32[]{:S(2)}, u32[]{:S(2)}) async-start(bf16[8,36,64,128]{3,2,1,0:T(8,128)(2,1)} %bitcast.385), calls=%async_computation.2 | async-start | bytes 9437184 | tf_op jit(solution)/shard_map/all_to_all | solution.py:392
  795.0 86.4 %all-reduce.36.cloned.1.call-start = ((), (), s32[]{:S(2)}) async-start(), calls=%async_computation.16 | async-start | bytes 393216 | tf_op jit(solution)/shard_map/psum | solution.py:34
  822.0 124.9 %all-reduce.40.cloned.1.call-start = ((), (), s32[]{:S(2)}) async-start(), calls=%async_computation.25 | async-start | bytes 1179648 | tf_op jit(solution)/shard_map/psum | solution.py:411
  833.5 58.8 %collective-permute-start.3 = (bf16[64,1536]{1,0:T(8,128)(2,1)}, bf16[64,1536]{1,0:T(8,128)(2,1)}, u32[]{:S(2)}, u32[]{:S(2)}) collective-permute-start(bf16[64,1536]{1,0:T(8,128)(2,1)} %get-tuple-element.267), channel_id=1, source_target_pairs={{4,0},{8,4},{12,8},{16,12},{20,16},{24,20},{28,24},{5,1},{9,5},{13... | collective-permute-start | bytes 589832 | tf_op jit(solution)/shard_map/ppermute | solution.py:27
  834.8 57.5 %collective-permute-start.2 = (bf16[64,1536]{1,0:T(8,128)(2,1)}, bf16[64,1536]{1,0:T(8,128)(2,1)}, u32[]{:S(2)}, u32[]{:S(2)}) collective-permute-start(bf16[64,1536]{1,0:T(8,128)(2,1)} %get-tuple-element.266), channel_id=1, source_target_pairs={{0,4},{4,8},{8,12},{12,16},{16,20},{20,24},{24,28},{1,5},{5,9},{9,... | collective-permute-start | bytes 589832 | tf_op jit(solution)/shard_map/ppermute | solution.py:26
  892.3 131.2 %reduce-scatter.19.cloned.1.call-start = ((), (), s32[]{:S(2)}) async-start(), calls=%async_computation.21 | async-start | bytes 1474560
  951.2 77.5 %reduce-scatter.21.cloned.1.call-start = ((), (), s32[]{:S(2)}) async-start(), calls=%async_computation.22 | async-start | bytes 1474560
  1000.2 58.8 %reduce-scatter.23.cloned.1.call-start = ((), (), s32[]{:S(2)}) async-start(), calls=%async_computation.23 | async-start | bytes 1474560
  1003.8 85.3 %reduce-scatter.13.cloned.1.call-start = ((), (), s32[]{:S(2)}) async-start(), calls=%async_computation.17 | async-start | bytes 1474560 | tf_op jit(solution)/shard_map/reduce_scatter | solution.py:465
  1006.9 168.4 %reduce-scatter.15.cloned.1.call-start = ((), (), s32[]{:S(2)}) async-start(), calls=%async_computation.18 | async-start | bytes 5898240 | tf_op jit(solution)/shard_map/reduce_scatter | solution.py:468
  1013.5 249.7 %reduce-scatter.17.cloned.1.call-start = ((), (), s32[]{:S(2)}) async-start(), calls=%async_computation.19 | async-start | bytes 5898240 | tf_op jit(solution)/shard_map/reduce_scatter | solution.py:471
  1023.3 241.4 %copy-start.122 = (bf16[192]{0:T(256)(128)(2,1)S(1)}, bf16[192]{0:T(256)(128)(2,1)}, u32[]{:S(2)}) copy-start(bf16[192]{0:T(256)(128)(2,1)} %param.43) | copy-start | bytes 1156
  1023.3 241.6 %copy-start.67 = (bf16[512,768]{1,0:T(8,128)(2,1)S(1)}, bf16[512,768]{1,0:T(8,128)(2,1)}, u32[]{:S(2)}) copy-start(bf16[512,768]{1,0:T(8,128)(2,1)} %copy-done.66) | copy-start | bytes 2359300
  1023.4 323.7 %all-reduce.38.cloned.1.call-start = ((), (), s32[]{:S(2)}) async-start(), calls=%async_computation.24 | async-start | bytes 7667712 | tf_op jit(solution)/shard_map/psum | solution.py:503
  (139 other events, 1626.5 us)
Sparse Core Ops, SparseCore 0:
  9.6 33.2 all-gather.17
  44.4 29.9 all-gather.15
  76.0 29.5 all-gather.13
  110.1 54.0 all-reduce.33
  170.8 31.6 all-gather.25
  204.0 30.4 all-gather.19
  236.2 88.5 all-gather.21
  326.4 87.8 all-gather.23
  822.1 59.2 all-reduce.35
  892.4 54.4 all-reduce.39
  951.4 28.4 reduce-scatter.18
  1000.3 28.4 reduce-scatter.20
  1031.1 27.8 reduce-scatter.22
  1061.1 27.8 reduce-scatter.12
  1091.2 83.9 reduce-scatter.14
  1177.4 85.7 reduce-scatter.16
  1267.7 79.2 all-reduce.37
where the time goes:
time: 1380 us; the launch traced here: 1360 us
  waiting for transfers between devices  485 us (35%)
  local copies, waits for them, and re-layouts  342 us (25%)
  other arithmetic  202 us (15%)
  matrix products  171 us (12%)
  blocking collectives  121 us (9%)
  starting transfers between devices  23.6 us (2%)
  between operations  19.2 us (1%)
    psum x2, waiting for transfers between devices, spread(): return lax.psum(block, axis)  96.3 us
    reduce_scatter x1, waiting for transfers between devices, body(): lax.psum_scatter(gradients[5].astype(jnp.bfloat16), 'wt', scatter_dimensi...  88 us
    reduce_scatter x1, waiting for transfers between devices, body(): lax.psum_scatter(gradients[4].astype(jnp.bfloat16), 'wt', scatter_dimensi...  86.2 us
    all_gather x2, blocking collectives, combined_all(): pieces = jax.tree.map(lambda part: lax.all_gather(part, axis), value)  56.3 us
    psum x1, waiting for transfers between devices, body(): lax.psum(global_query_part.reshape(global_count, model_width).astype(jnp....  52.5 us
    scatter x1, local copies, waits for them, and re-layouts, body(): jnp.zeros((shards * capacity, BLOCK, 2 * HD), jnp.float32).at[slot_index]  42.7 us
    unnamed x326, local copies, waits for them, and re-layouts  40.2 us
    unnamed x2, blocking collectives  39.5 us
  transfers between devices with their start and end apart: 24, of which 12 were waited for; matrix products, arithmetic and copies ran while one was open for 29% of the time, Pallas kernels for 0%

commit v1 on v0

v1 whole, which is shorter than its diff:
```python
from functools import partial

import jax
import jax.numpy as jnp
from jax import lax
from jax.experimental import pallas as pl
from jax.experimental.pallas import tpu as pltpu
from jax.sharding import PartitionSpec as P

H = 12
HD = 64
BLOCK = 64
GLOB = 2
RAND = 3
PAIR = 2 * HD
PIECES = 8
NEGATIVE = -1e30
EPSILON = 1e-12
FACTOR = HD ** (-0.5)
F32 = jnp.float32
BF16 = jnp.bfloat16


def groups_of(shards):
    return [list(range(s, s + PIECES)) for s in range(0, shards, PIECES)]


def across_groups(shards):
    return [list(range(s, shards, PIECES)) for s in range(PIECES)]


def dot(a, b):
    return jnp.dot(a, b, preferred_element_type=F32)


def dot_t(a, b):
    return lax.dot_general(a, b, (((1,), (1,)), ((), ())), preferred_element_type=F32)


def t_dot(a, b):
    return lax.dot_general(a, b, (((0,), (0,)), ((), ())), preferred_element_type=F32)


def listed_rows(table, meta, pair, head, block, seq_blocks):
    length, first = meta[0], meta[1]
    own = first + block
    starts, limits = [], []
    for step in (-1, 0, 1):
        at = own + step
        inside = (at >= 0) & (at < seq_blocks)
        at = jnp.clip(at, 0, seq_blocks - 1)
        starts.append(pl.multiple_of(at * BLOCK, BLOCK))
        limits.append(jnp.where(inside, length - at * BLOCK, 0))
    for slot in range(RAND):
        at = table[(block * H + 2 * pair + head) * RAND + slot]
        starts.append(pl.multiple_of(at * BLOCK, BLOCK))
        limits.append(length - at * BLOCK)
    return starts, limits


def gathered(kv_ref, starts, columns):
    parts = [kv_ref[0 : GLOB * BLOCK, columns]]
    parts += [kv_ref[pl.ds(at, BLOCK), columns] for at in starts]
    return jnp.concatenate(parts, axis=0)


def forward_kernel(table, meta, q_ref, kv_ref, out_ref, p_ref, pg_ref, *, row_blocks, extra):
    pair = pl.program_id(0)
    rows = row_blocks * BLOCK
    seq = kv_ref.shape[0]
    listed = (GLOB + 3 + RAND) * BLOCK
    low = lax.broadcasted_iota(jnp.int32, (1, PAIR), 1) < HD
    lane = lax.broadcasted_iota(jnp.int32, (1, listed), 1)
    group = lane // BLOCK
    within = lane % BLOCK

    def one_block(block, carry):
        at = pl.multiple_of(block * BLOCK, BLOCK)
        q_both = q_ref[pl.ds(at, BLOCK), :]
        zero = jnp.zeros_like(q_both)
        outs = []
        for head in range(2):
            columns = slice(head * PAIR, (head + 1) * PAIR)
            q = jnp.where(low, zero, q_both) if head == 0 else jnp.where(low, q_both, zero)
            starts, limits = listed_rows(table, meta, pair, head, block, seq // BLOCK)
            kv = gathered(kv_ref, starts, columns)
            limit = jnp.full((1, listed), BLOCK, jnp.int32)
            for i, value in enumerate(limits):
                limit = jnp.where(group == GLOB + i, value, limit)
            scores = dot_t(q, kv) + jnp.where(within < limit, 0.0, NEGATIVE)
            raised = jnp.exp(scores - jnp.max(scores, axis=1, keepdims=True))
            probs = (raised / jnp.sum(raised, axis=1, keepdims=True)).astype(BF16)
            p_ref[block, head] = probs
            outs.append(dot(probs, kv))
        out_ref[pl.ds(at, BLOCK), :] = jnp.where(low, outs[0], outs[1]).astype(BF16)
        return carry

    lax.fori_loop(0, row_blocks, one_block, 0)

    q_both = q_ref[rows : rows + extra, :]
    zero = jnp.zeros_like(q_both)
    wide = jnp.concatenate(
        [
            jnp.concatenate([jnp.where(low, zero, q_both), zero], axis=1),
            jnp.concatenate([zero, jnp.where(low, q_both, zero)], axis=1),
        ],
        axis=0,
    )
    position = lax.broadcasted_iota(jnp.int32, (1, seq), 1)
    scores = dot_t(wide, kv_ref[...]) + jnp.where(position < meta[0], 0.0, NEGATIVE)
    raised = jnp.exp(scores - jnp.max(scores, axis=1, keepdims=True))
    probs = (raised / jnp.sum(raised, axis=1, keepdims=True)).astype(BF16)
    pg_ref[0] = probs
    out = dot(probs, kv_ref[...])
    out_ref[rows : rows + extra, :] = jnp.where(
        low, out[:extra, :PAIR], out[extra:, PAIR:]
    ).astype(BF16)


def backward_kernel(
    table, meta, q_ref, do_ref, kv_ref, p_ref, pg_ref, dq_ref, dkv_ref, acc, *, row_blocks, extra
):
    pair = pl.program_id(0)
    rows = row_blocks * BLOCK
    seq = kv_ref.shape[0]
    low = lax.broadcasted_iota(jnp.int32, (1, PAIR), 1) < HD

    q_both = q_ref[rows : rows + extra, :]
    do_both = do_ref[rows : rows + extra, :]
    zero = jnp.zeros_like(q_both)
    wide_q = jnp.concatenate(
        [
            jnp.concatenate([jnp.where(low, zero, q_both), zero], axis=1),
            jnp.concatenate([zero, jnp.where(low, q_both, zero)], axis=1),
        ],
        axis=0,
    )
    wide_do = jnp.concatenate(
        [
            jnp.concatenate([jnp.where(low, do_both, zero), zero], axis=1),
            jnp.concatenate([zero, jnp.where(low, zero, do_both)], axis=1),
        ],
        axis=0,
    )
    probs = pg_ref[0]
    wide = probs.astype(F32)
    dp = dot_t(wide_do, kv_ref[...])
    ds = (wide * (dp - jnp.sum(wide * dp, axis=1, keepdims=True))).astype(BF16)
    dq = dot(ds, kv_ref[...])
    dq_ref[rows : rows + extra, :] = (
        jnp.where(low, dq[extra:, PAIR:], dq[:extra, :PAIR]) * FACTOR
    ).astype(BF16)
    acc[...] = t_dot(
        jnp.concatenate([probs, ds], axis=0), jnp.concatenate([wide_do, wide_q], axis=0)
    )

    def one_block(block, carry):
        at = pl.multiple_of(block * BLOCK, BLOCK)
        q_both = q_ref[pl.ds(at, BLOCK), :]
        do_both = do_ref[pl.ds(at, BLOCK), :]
        zero = jnp.zeros_like(q_both)
        dqs = []
        for head in range(2):
            columns = slice(head * PAIR, (head + 1) * PAIR)
            q = jnp.where(low, zero, q_both) if head == 0 else jnp.where(low, q_both, zero)
            do = jnp.where(low, do_both, zero) if head == 0 else jnp.where(low, zero, do_both)
            starts, _ = listed_rows(table, meta, pair, head, block, seq // BLOCK)
            kv = gathered(kv_ref, starts, columns)
            probs = p_ref[block, head]
            wide = probs.astype(F32)
            dp = dot_t(do, kv)
            ds = (wide * (dp - jnp.sum(wide * dp, axis=1, keepdims=True))).astype(BF16)
            dqs.append(dot(ds, kv))
            dkv = t_dot(jnp.concatenate([probs, ds], axis=0), jnp.concatenate([do, q], axis=0))
            acc[0 : GLOB * BLOCK, columns] += dkv[: GLOB * BLOCK]
            for i, start in enumerate(starts):
                here = dkv[(GLOB + i) * BLOCK : (GLOB + i + 1) * BLOCK]
                acc[pl.ds(start, BLOCK), columns] += here
        dq_ref[pl.ds(at, BLOCK), :] = (jnp.where(low, dqs[1], dqs[0]) * FACTOR).astype(BF16)
        return carry

    lax.fori_loop(0, row_blocks, one_block, 0)
    dkv_ref[...] = acc[...].astype(BF16)


def attention_forward(table, meta, q, kv, row_blocks, extra):
    rows, seq, pairs = q.shape[0], kv.shape[0], H // 2
    listed = (GLOB + 3 + RAND) * BLOCK
    return pl.pallas_call(
        partial(forward_kernel, row_blocks=row_blocks, extra=extra),
        grid_spec=pltpu.PrefetchScalarGridSpec(
            num_scalar_prefetch=2,
            grid=(pairs,),
            in_specs=[
                pl.BlockSpec((rows, PAIR), lambda p, *_: (0, p)),
                pl.BlockSpec((seq, 2 * PAIR), lambda p, *_: (0, p)),
            ],
            out_specs=[
                pl.BlockSpec((rows, PAIR), lambda p, *_: (0, p)),
                pl.BlockSpec((row_blocks, 2, BLOCK, listed), lambda p, *_: (0, p, 0, 0)),
                pl.BlockSpec((1, 2 * extra, seq), lambda p, *_: (p, 0, 0)),
            ],
        ),
        out_shape=[
            jax.ShapeDtypeStruct((rows, H * HD), BF16),
            jax.ShapeDtypeStruct((row_blocks, H, BLOCK, listed), BF16),
            jax.ShapeDtypeStruct((pairs, 2 * extra, seq), BF16),
        ],
        compiler_params=pltpu.CompilerParams(vmem_limit_bytes=50 * 2**20),
        name="attention_forward",
    )(table, meta, q, kv)


def attention_backward(table, meta, q, do, kv, probs, global_probs, row_blocks, extra):
    rows, seq, pairs = q.shape[0], kv.shape[0], H // 2
    listed = (GLOB + 3 + RAND) * BLOCK
    tile = pl.BlockSpec((rows, PAIR), lambda p, *_: (0, p))
    wide = pl.BlockSpec((seq, 2 * PAIR), lambda p, *_: (0, p))
    return pl.pallas_call(
        partial(backward_kernel, row_blocks=row_blocks, extra=extra),
        grid_spec=pltpu.PrefetchScalarGridSpec(
            num_scalar_prefetch=2,
            grid=(pairs,),
            in_specs=[
                tile,
                tile,
                wide,
                pl.BlockSpec((row_blocks, 2, BLOCK, listed), lambda p, *_: (0, p, 0, 0)),
                pl.BlockSpec((1, 2 * extra, seq), lambda p, *_: (p, 0, 0)),
            ],
            out_specs=[tile, wide],
            scratch_shapes=[pltpu.VMEM((seq, 2 * PAIR), F32)],
        ),
        out_shape=[
            jax.ShapeDtypeStruct((rows, H * HD), BF16),
            jax.ShapeDtypeStruct((seq, 2 * H * HD), BF16),
        ],
        compiler_params=pltpu.CompilerParams(vmem_limit_bytes=58 * 2**20),
        name="attention_backward",
    )(table, meta, q, do, kv, probs, global_probs)


def swap_heads(columns):
    lead = columns.shape[:-1]
    split = columns.reshape(*lead, H // 2, 2, HD)
    return jnp.concatenate([split[..., 1, :], split[..., 0, :]], axis=-1).reshape(*lead, H * HD)


def interleave(keys, values):
    lead = keys.shape[:-1]
    k, v = (a.reshape(*lead, H // 2, 2, HD) for a in (keys, values))
    parts = [v[..., 0, :], k[..., 0, :], k[..., 1, :], v[..., 1, :]]
    return jnp.concatenate(parts, axis=-1).reshape(*lead, 2 * H * HD)


def separate(columns):
    lead = columns.shape[:-1]
    split = columns.reshape(*lead, H // 2, 4, HD)
    keys = jnp.concatenate([split[..., 1, :], split[..., 2, :]], axis=-1)
    values = jnp.concatenate([split[..., 0, :], split[..., 3, :]], axis=-1)
    return keys.reshape(*lead, H * HD), values.reshape(*lead, H * HD)


def in_pieces(grad, parts, width):
    rows, columns = grad.shape
    split = grad.reshape(parts, PIECES, rows // parts // PIECES, columns // width, width)
    return jnp.transpose(split, (1, 0, 3, 2, 4)).reshape(PIECES, parts, -1, width)


def from_pieces(pieces, columns, width):
    split = pieces.reshape(PIECES, columns // width, -1, width)
    return jnp.transpose(split, (0, 2, 1, 3)).reshape(-1, columns)


def reduced(pieces, shards):
    mine = lax.psum_scatter(
        pieces, "ctx", scatter_dimension=0, axis_index_groups=groups_of(shards), tiled=False
    )
    if shards > PIECES:
        mine = lax.psum(mine, "ctx", axis_index_groups=across_groups(shards))
    mine = lax.psum_scatter(mine, "wt", scatter_dimension=0, tiled=False)
    return lax.all_gather(mine, "ctx", axis_index_groups=groups_of(shards))


def body(
    tokens,
    cotangent,
    lengths,
    rand_blocks,
    query_weight,
    key_weight,
    value_weight,
    output_weight,
    expand_weight,
    contract_weight,
    query_bias,
    value_bias,
    output_bias,
    expand_bias,
    contract_bias,
    attn_gain,
    attn_shift,
    ffn_gain,
    ffn_shift,
):
    shards = lax.axis_size("ctx")
    parts = lax.axis_size("wt")
    c = lax.axis_index("ctx")
    rows, width = tokens.shape[1], tokens.shape[2]
    row_blocks = rows // BLOCK
    global_count = GLOB * BLOCK
    extra = 16 * (-(-global_count // (16 * shards)))
    hidden_width = expand_weight.shape[1]
    length = lengths[0]
    inputs = tokens[0]

    everything = lax.all_gather(inputs, "ctx", axis=0, tiled=True)
    qkv_shard = jnp.concatenate(
        [swap_heads(query_weight), interleave(key_weight, value_weight)], axis=1
    )
    w_qkv = lax.all_gather(qkv_shard, "wt", axis=0, tiled=True)
    w_query, w_kv = w_qkv[:, :width], w_qkv[:, width:]

    small = jnp.concatenate(
        [
            query_bias,
            value_bias,
            output_bias,
            contract_bias,
            attn_gain,
            attn_shift,
            ffn_gain,
            ffn_shift,
            expand_bias,
        ]
    ).reshape(1, -1)
    small = lax.all_gather(small, "wt", axis=0, tiled=True)
    each = width // parts
    b_query, b_value, b_output, b_contract, g_attn, s_attn, g_ffn, s_ffn = (
        small[:, i * each : (i + 1) * each].reshape(-1).astype(F32) for i in range(8)
    )
    b_expand = small[:, 8 * each :].reshape(-1).astype(F32)

    others = jnp.concatenate(
        [
            in_pieces(output_weight, 1, width)[:, 0],
            in_pieces(expand_weight, 1, width)[:, 0],
            in_pieces(contract_weight, 1, width)[:, 0],
        ],
        axis=1,
    )
    others = lax.dynamic_index_in_dim(others, c % PIECES, 0, keepdims=False)
    others = lax.all_gather(others, "wt")
    others = lax.all_gather(others, "ctx", axis_index_groups=groups_of(shards))
    n_out = width // parts // PIECES
    n_exp = n_out * (hidden_width // width)

    def whole(pieces, columns):
        pieces = jnp.transpose(pieces, (1, 0, 2, 3))
        return jax.vmap(lambda a: from_pieces(a, columns, width))(pieces).reshape(-1, columns)

    w_output = whole(others[:, :, :n_out], width)
    w_expand = whole(others[:, :, n_out : n_out + n_exp], hidden_width)
    w_contract = whole(others[:, :, n_out + n_exp :], width)

    start = jnp.minimum(c * extra, everything.shape[0] - extra)
    x = jnp.concatenate([inputs, lax.dynamic_slice_in_dim(everything, start, extra, 0)], axis=0)
    first_cot = jnp.where(c == 0, cotangent[0, :global_count], jnp.zeros((), BF16))
    first_cot = lax.psum(first_cot, "ctx")
    first_cot = jnp.pad(first_cot, ((0, max(0, shards * extra - global_count)), (0, 0)))
    cot = jnp.concatenate(
        [cotangent[0], lax.dynamic_slice_in_dim(first_cot, c * extra, extra, 0)], axis=0
    )
    index = jnp.arange(rows + extra, dtype=jnp.int32)
    position = jnp.where(index < rows, c * rows + index, c * extra + index - rows)
    is_global = position < global_count
    usable = (position < length) & (is_global == (index >= rows))

    q = ((dot(x, w_query) + swap_heads(b_query)).astype(BF16) * FACTOR).astype(BF16)
    kv = (dot(everything, w_kv) + interleave(jnp.zeros_like(b_value), b_value)).astype(BF16)
    table = rand_blocks.reshape(-1)
    meta = jnp.stack([length, c * row_blocks]).astype(jnp.int32)
    attended, probs, global_probs = attention_forward(table, meta, q, kv, row_blocks, extra)

    residual = x.astype(F32) + dot(attended, w_output) + b_output
    centered = residual - jnp.mean(residual, axis=1, keepdims=True)
    root_one = lax.rsqrt(jnp.mean(centered * centered, axis=1, keepdims=True) + EPSILON)
    norm_one = centered * root_one
    normed_one = norm_one * g_attn + s_attn
    normed_low = normed_one.astype(BF16)
    expand = dot(normed_low, w_expand) + b_expand
    hidden = jax.nn.gelu(expand, approximate=True).astype(BF16)
    second = normed_one + dot(hidden, w_contract) + b_contract
    centered = second - jnp.mean(second, axis=1, keepdims=True)
    root_two = lax.rsqrt(jnp.mean(centered * centered, axis=1, keepdims=True) + EPSILON)
    norm_two = centered * root_two
    result = norm_two * g_ffn + s_ffn
    layer_out = jnp.where(usable[:, None], result, 0.0).astype(BF16)

    grad_result = jnp.where(usable[:, None], cot.astype(F32), 0.0)
    ffn_ggrad = jnp.sum(grad_result * norm_two, axis=0)
    ffn_sgrad = jnp.sum(grad_result, axis=0)
    e = g_ffn * grad_result
    grad_two = root_two * (
        e
        - jnp.mean(e, axis=1, keepdims=True)
        - norm_two * jnp.mean(e * norm_two, axis=1, keepdims=True)
    )
    grad_second = grad_two.astype(BF16)
    contract_grad = t_dot(hidden, grad_second)
    contract_bgrad = jnp.sum(grad_second.astype(F32), axis=0)
    grad_hidden = dot_t(grad_second, w_contract)
    gelu_back = jax.vjp(partial(jax.nn.gelu, approximate=True), expand)[1]
    grad_expand = gelu_back(grad_hidden)[0].astype(BF16)
    expand_grad = t_dot(normed_low, grad_expand)
    expand_bgrad = jnp.sum(grad_expand.astype(F32), axis=0)
    grad_first = grad_two + dot_t(grad_expand, w_expand)
    attn_ggrad = jnp.sum(grad_first * norm_one, axis=0)
    attn_sgrad = jnp.sum(grad_first, axis=0)
    e = g_attn * grad_first
    grad_one = root_one * (
        e
        - jnp.mean(e, axis=1, keepdims=True)
        - norm_one * jnp.mean(e * norm_one, axis=1, keepdims=True)
    )
    grad_branch = grad_one.astype(BF16)
    output_grad = t_dot(attended, grad_branch)
    output_bgrad = jnp.sum(grad_branch.astype(F32), axis=0)
    grad_attended = dot_t(grad_branch, w_output).astype(BF16)

    early = reduced(
        jnp.concatenate(
            [
                in_pieces(contract_grad.astype(BF16), parts, width),
                in_pieces(expand_grad.astype(BF16), parts, width),
                in_pieces(output_grad.astype(BF16), parts, width),
            ],
            axis=2,
        ),
        shards,
    ).astype(F32)
    n_con = hidden_width // parts // PIECES
    contract_wgrad = from_pieces(early[:, :n_con], width, width)
    expand_wgrad = from_pieces(early[:, n_con : n_con + n_exp], hidden_width, width)
    output_wgrad = from_pieces(early[:, n_con + n_exp :], width, width)

    dq, dkv = attention_backward(
        table, meta, q, grad_attended, kv, probs, global_probs, row_blocks, extra
    )
    qkv_grad = jnp.concatenate([t_dot(x, dq), t_dot(everything, dkv)], axis=1).astype(BF16)
    query_bgrad = swap_heads(jnp.sum(dq.astype(F32), axis=0))
    _, value_bgrad = separate(jnp.sum(dkv.astype(F32), axis=0))
    vectors = jnp.concatenate(
        [
            a.reshape(parts, -1)
            for a in (
                query_bgrad,
                value_bgrad,
                output_bgrad,
                contract_bgrad,
                attn_ggrad,
                attn_sgrad,
                ffn_ggrad,
                ffn_sgrad,
                expand_bgrad,
            )
        ],
        axis=1,
    )
    vector_rows = -(-vectors.shape[1] // (PIECES * width))
    vectors = jnp.pad(vectors, ((0, 0), (0, vector_rows * PIECES * width - vectors.shape[1])))
    vectors = vectors.reshape(parts, PIECES, vector_rows, width).transpose(1, 0, 2, 3)
    late = reduced(
        jnp.concatenate([in_pieces(qkv_grad, parts, width), vectors.astype(BF16)], axis=2), shards
    ).astype(F32)
    qkv_wgrad = from_pieces(late[:, :-vector_rows], 3 * width, width)
    query_wgrad = swap_heads(qkv_wgrad[:, :width])
    key_wgrad, value_wgrad = separate(qkv_wgrad[:, width:])
    vectors = late[:, -vector_rows:].reshape(-1)
    small_grads = [vectors[i * each : (i + 1) * each] for i in range(8)]
    expand_bias_grad = vectors[8 * each : 8 * each + hidden_width // parts]

    grad_x = dot_t(dkv, w_kv)
    own = grad_one + dot_t(dq, w_query)
    share = jnp.where(c * extra < global_count, own[rows:], 0.0)
    here = lax.dynamic_slice_in_dim(grad_x, start, extra, 0)
    grad_x = lax.dynamic_update_slice_in_dim(grad_x, here + share, start, 0)
    input_grad = own[:rows] + lax.psum_scatter(
        grad_x.astype(BF16), "ctx", scatter_dimension=0, tiled=True
    ).astype(F32)

    finished = lax.all_gather(layer_out[rows:], "ctx", axis=0, tiled=True)
    on_first = (c == 0) & (index[:rows] < global_count)
    finished = jnp.pad(finished[:global_count], ((0, rows - global_count), (0, 0)))
    layer_out = jnp.where(on_first[:, None], finished, layer_out[:rows])

    return (
        layer_out[None],
        input_grad[None],
        query_wgrad,
        key_wgrad,
        value_wgrad,
        output_wgrad,
        expand_wgrad,
        contract_wgrad,
        small_grads[0],
        small_grads[1],
        small_grads[2],
        expand_bias_grad,
        small_grads[3],
        small_grads[4],
        small_grads[5],
        small_grads[6],
        small_grads[7],
    )


def solution(mesh):
    tokens, weight, vector = P("wt", "ctx", None), P("wt", None), P("wt")
    return jax.shard_map(
        body,
        mesh=mesh,
        in_specs=(tokens, tokens, vector, P("wt", "ctx", None, None)) + (weight,) * 6 + (vector,) * 9,
        out_specs=(tokens, tokens) + (weight,) * 6 + (vector,) * 9,
        check_vma=False,
    )
```

time: 1380 us -> 691 us (0.50)
  local copies, waits for them, and re-layouts: 342 us -> 81.7 us
  waiting for transfers between devices: 485 us -> 316 us
  other arithmetic: 202 us -> 36.5 us
  Pallas kernels: 0 us -> 111 us
  blocking collectives: 121 us -> 33.5 us
  matrix products: 171 us -> 87 us
  starting transfers between devices: 23.6 us -> 0.67 us
    psum x4 -> x1, waiting for transfers between devices: 185 us -> 11.2 us  [body(): first_cot = lax.psum(first_cot, 'ctx')]
    pallas_call x0 -> x2, Pallas kernels: none -> 111 us  [the longest x1 57.2 us: attention_backward(): pl.pallas_call(partial(backward_kernel, row_blocks=row_blocks, extra=extr...]
    reduce_scatter x3 -> x4, waiting for transfers between devices: 202 us -> 109 us  [the longest x1 50.4 us: reduced(): lax.psum_scatter(pieces, 'ctx', scatter_dimension=0, axis_index_groups=gr...]
    all_gather x7 -> x5, waiting for transfers between devices: 62.1 us -> 152 us  [the longest x1 71.4 us: body(): w_qkv = lax.all_gather(qkv_shard, 'wt', axis=0, tiled=True)]
    dot_general x40 -> x15, matrix products: 161 us -> 87 us  [the longest x5 30.8 us: dot_t(): lax.dot_general(a, b, (((1,), (1,)), ((), ())), preferred_element_type=F32)]
    another operation x15 -> x4, local copies, waits for them, and re-layouts: 74.2 us -> 0.35 us  [the longest x2 0.18 us: body(): a.reshape(parts, -1)]
    scatter x2 -> x0, local copies, waits for them, and re-layouts: 45.6 us -> none  [the longest x1 42.7 us: body(): jnp.zeros((shards * capacity, BLOCK, 2 * HD), jnp.float32).at[slot_index]]
    unnamed x2 -> x0, blocking collectives: 39.5 us -> none
  transfers between devices with their start and end apart: 24 -> 11, of which waited for: 12 -> 10; matrix products, arithmetic and copies ran while one was open for 29% -> 17% of each run, Pallas kernels for 0% -> 16%
where the time goes in v1:
time: 691 us; the launch traced here: 683 us
  waiting for transfers between devices  316 us (46%)
  Pallas kernels  111 us (16%)
  matrix products  87 us (13%)
  local copies, waits for them, and re-layouts  81.7 us (12%)
  other arithmetic  36.5 us (5%)
  blocking collectives  33.5 us (5%)
  between operations  17.1 us (2%)
    all_gather x1, waiting for transfers between devices, body(): w_qkv = lax.all_gather(qkv_shard, 'wt', axis=0, tiled=True)  71.4 us
    pallas_call x1, Pallas kernels, attention_backward(): pl.pallas_call(partial(backward_kernel, row_blocks=row_blocks, extra=extr...  57.2 us
    pallas_call x1, Pallas kernels, attention_forward(): pl.pallas_call(partial(forward_kernel, row_blocks=row_blocks, extra=extra...  53.8 us
    reduce_scatter x1, waiting for transfers between devices, reduced(): lax.psum_scatter(pieces, 'ctx', scatter_dimension=0, axis_index_groups=gr...  50.4 us
    unnamed x12, waiting for transfers between devices  44 us
    reduce_scatter x1, waiting for transfers between devices, body(): lax.psum_scatter(grad_x.astype(BF16), 'ctx', scatter_dimension=0, tiled=T...  39.9 us
    all_gather x1, waiting for transfers between devices, body(): others = lax.all_gather(others, 'wt')  31.8 us
    dot_general x5, matrix products, dot_t(): lax.dot_general(a, b, (((1,), (1,)), ((), ())), preferred_element_type=F32)  30.8 us
  transfers between devices with their start and end apart: 11, of which 10 were waited for; matrix products, arithmetic and copies ran while one was open for 17% of the time, Pallas kernels for 16%

profile of v1, /device:TPU:0, one launch (start us, length us, event | category | flops | bytes accessed | tf_op | source)
XLA Modules:
  0.0 683.3 jit_solution(15966428694352755839)
XLA Ops:
  16.9 31.8 %all-gather.12.cloned.1.call-done = bf16[4,216,768]{2,1,0:T(8,128)(2,1)} async-done(((bf16[1,216,768]{2,1,0:T(8,128)(2,1)}), bf16[4,216,768]{2,1,0:T(8,128)(2,1)}) %all-gather.12.cloned.1.call-update) | async-done | bytes 1327120 | tf_op jit(solution)/shard_map/all_gather | solution.py:353
  49.6 13.1 %all-gather.3 = bf16[4,1,2304]{2,1,0:T(2,128)(2,1)S(1)} all-gather(bf16[1,1,2304]{2,1,0:T(2,128)(2,1)S(1)} %reshape.342), channel_id=3, replica_groups=mesh['ctx'=8,'wt'=4] {'wt'}, dimensions={0}, use_global_device_ids=true | all-gather | bytes 23040 | tf_op jit(solution)/shard_map/all_gather | solution.py:337
  64.2 11.2 %all-reduce.6.cloned.1.call-done = bf16[128,768]{1,0:T(8,128)(2,1)} async-done(((bf16[128,768]{1,0:T(8,128)(2,1)}), bf16[128,768]{1,0:T(8,128)(2,1)}) %all-reduce.6.cloned.1.call-update) | async-done | bytes 196624 | tf_op jit(solution)/shard_map/psum | solution.py:369
  76.2 19.1 %all-gather.16.cloned.1.call-done = bf16[1,4096,768]{2,1,0:T(8,128)(2,1)} async-done(((bf16[1,512,768]{2,1,0:T(8,128)(2,1)}), bf16[1,4096,768]{2,1,0:T(8,128)(2,1)}) %all-gather.16.cloned.1.call-update) | async-done | bytes 6291472 | tf_op jit(solution)/shard_map/all_gather | solution.py:317
  96.0 71.4 %all-gather.10.cloned.1.call-done = bf16[768,2304]{1,0:T(8,128)(2,1)} async-done(((bf16[192,2304]{1,0:T(8,128)(2,1)}), bf16[768,2304]{1,0:T(8,128)(2,1)}) %all-gather.10.cloned.1.call-update) | async-done | bytes 3538960 | tf_op jit(solution)/shard_map/all_gather | solution.py:321
  169.8 15.5 %fusion.kv_ref = bf16[4096,1536]{1,0:T(8,128)(2,1)} fusion(f32[1536]{0:T(1024)S(1)} %add.169, bf16[1,4096,768]{2,1,0:T(8,128)(2,1)} %all-gather.16.cloned.1.call-done, bf16[768,2304]{1,0:T(8,128)(2,1)S(1)} %copy-done.20), kind=kOutput, calls=%fused_computation.1 | convolution fusion | flops 9676259328 | bytes 21241856 | tf_op jit(solution)/shard_map/dot_general | solution.py:33
  185.3 53.8 %attention_forward.1 = (bf16[528,768]{1,0:T(8,128)(2,1)S(1)}, bf16[8,12,64,512]{3,2,1,0:T(8,128)(2,1)}, bf16[6,32,4096]{2,1,0:T(8,128)(2,1)S(1)}) custom-call(s32[288]{0:T(512)S(1)} %reshape.289.table, s32[2]{0:T(128)S(1)} %pad_add_fusion.meta, bf16[528,768]{1,0:T(8,128)(2,1)S(1)} %fusion.25.q_ref, bf16[4096,1536]{1,0:T(8,128)(2,1)} %fusion.kv_ref), custom_call_target="tpu_custom_call" | custom-call | tf_op jit(solution)/shard_map/attention_forward/pallas_call | solution.py:189
  241.6 6.9 %fusion.49 = (bf16[8,4,96,768]{3,2,1,0:T(8,128)(2,1)}, bf16[4,8,96,768]{3,2,0,1:T(8,128)(2,1)S(1)}) fusion(bf16[8,4,216,768]{3,2,1,0:T(8,128)(2,1)} %bitcast.178), kind=kLoop, calls=%fused_computation.144 | loop fusion | bytes 18874368 | tf_op jit(solution)/shard_map/slice | solution.py:363
  248.5 4.7 copy.141
  260.1 4.3 fusion.57
  267.5 6.8 fusion.58
  274.2 7.0 %convolution_convert_fusion.1 = bf16[3072,768]{1,0:T(8,128)(2,1)} fusion(f32[528,768]{1,0:T(8,128)S(1)} %get-tuple-element.36, f32[528,3072]{1,0:T(8,128)S(1)} %fusion.47, f32[3072]{0:T(1024)S(1)} %reshape.332), kind=kOutput, calls=%fused_computation.17 | convolution fusion | flops 2510401536 | bytes 12840960 | tf_op jit(solution)/shard_map/dot_general | solution.py:41
  281.3 4.3 multiply_reduce_fusion.1
  285.5 6.1 convolution_convert_fusion
  291.6 9.7 %reshape.320 = bf16[4,8,24,4,768]{4,3,2,1,0:T(4,128)(2,1)} reshape(bf16[768,3072]{1,0:T(8,128)(2,1)} %convolution_convert_fusion) | data formatting | bytes 9437184 | tf_op jit(solution)/shard_map/reshape | solution.py:266
  301.4 3.4 copy.155
  307.7 4.9 pad_maximum_fusion
  316.2 57.2 %attention_backward.1 = (bf16[528,768]{1,0:T(8,128)(2,1)}, bf16[4096,1536]{1,0:T(8,128)(2,1)}) custom-call(s32[288]{0:T(512)} %copy-done.2, s32[2]{0:T(128)} %copy-done.3, bf16[528,768]{1,0:T(8,128)(2,1)} %copy-done, bf16[528,768]{1,0:T(8,128)(2,1)} %convolution_convert_fusion.4.do_ref, bf16[4096,1536]{1,0:T(8,128)(2,1)} %fusion.kv_ref, ...), custom_call_target="tpu_custom_call" | custom-call | tf_op jit(solution)/shard_map/attention_backward/pallas_call | solution.py:219
  374.9 6.6 reduce.4
  383.8 15.0 %fusion.14 = bf16[768,1536]{0,1:T(8,128)(2,1)S(1)} fusion(bf16[4096,1536]{1,0:T(8,128)(2,1)} %get-tuple-element.26, bf16[1,4096,768]{2,1,0:T(8,128)(2,1)} %all-gather.16.cloned.1.call-done), kind=kOutput, calls=%fused_computation.22 | convolution fusion | flops 9664856064 | bytes 21233664 | tf_op jit(solution)/shard_map/dot_general | solution.py:41
  399.1 4.1 copy.143
  403.1 8.8 %convert_element_type.203 = bf16[4,8,24,3,768]{4,3,2,1,0:T(4,128)(2,1)} reshape(bf16[768,2304]{1,0:T(8,128)(2,1)} %copy.143) | data formatting | bytes 7077888 | tf_op jit(solution)/shard_map/convert_element_type | solution.py:450
  418.5 43.2 %all-reduce.8.cloned.1.call-done = bf16[8,4,216,768]{3,2,0,1:T(8,128)(2,1)} async-done(((bf16[8,4,216,768]{3,2,0,1:T(8,128)(2,1)}), bf16[8,4,216,768]{3,2,0,1:T(8,128)(2,1)}) %all-reduce.8.cloned.1.call-update) | async-done | bytes 10616848
  465.1 50.4 %reduce-scatter.8.cloned.1.call-done = bf16[1,4,73,768]{3,2,1,0:T(8,128)(2,1)} async-done(((bf16[8,4,73,768]{3,2,1,0:T(8,128)(2,1)}), bf16[1,4,73,768]{3,2,1,0:T(8,128)(2,1)}) %reduce-scatter.8.cloned.1.call-update) | async-done | bytes 448528 | tf_op jit(solution)/shard_map/reduce_scatter | solution.py:276
  515.6 13.8 %fusion.17 = f32[4096,768]{1,0:T(8,128)S(1)} fusion(bf16[4096,1536]{1,0:T(8,128)(2,1)} %get-tuple-element.26, bf16[768,2304]{1,0:T(8,128)(2,1)} %all-gather.10.cloned.1.call-done), kind=kOutput, calls=%fused_computation.26 | convolution fusion | flops 9663676416 | bytes 27525120 | tf_op jit(solution)/shard_map/dot_general | solution.py:37
  535.6 8.0 %convert_element_type.201 = bf16[4096,768]{1,0:T(8,128)(2,1)} convert(f32[4096,768]{1,0:T(8,128)} %dynamic_update_slice.3) | non-fusion elementwise | flops 3145728 | bytes 18874368 | tf_op jit(solution)/shard_map/convert_element_type | solution.py:489
  543.6 6.5 reduce-scatter.12.cloned.1.call-done
  550.2 9.2 %all_gather.34 = bf16[128,768]{1,0:T(8,128)(2,1)S(1)} all-gather(bf16[16,768]{1,0:T(8,128)(2,1)S(1)} %slice.257), channel_id=1, replica_groups=mesh['ctx'=8,'wt'=4] {'ctx'}, dimensions={0}, use_global_device_ids=true | all-gather | bytes 221184 | tf_op jit(solution)/shard_map/all_gather | solution.py:492
  560.5 12.0 %reduce-scatter.10.cloned.1.call-done = bf16[1,73,768]{2,1,0:T(8,128)(2,1)} async-done(((bf16[4,73,768]{2,1,0:T(8,128)(2,1)}), bf16[1,73,768]{2,1,0:T(8,128)(2,1)}) %reduce-scatter.10.cloned.1.call-update) | async-done | bytes 112144 | tf_op jit(solution)/shard_map/reduce_scatter | solution.py:281
  572.5 11.2 %all_gather.35 = bf16[8,73,768]{2,1,0:T(8,128)(2,1)S(1)} all-gather(bf16[1,73,768]{2,1,0:T(8,128)(2,1)} %reduce-scatter.10.cloned.1.call-done), channel_id=1, replica_groups={{0,4,8,12,16,20,24,28},{1,5,9,13,17,21,25,29},{2,6,10,14,18,22,26,30},{..., dimensions={0}, use_global_device_ids=true | all-gather | bytes 1009152 | tf_op jit(solution)/shard_map/all_gather | solution.py:282
  596.3 39.9 %reduce-scatter.6.cloned.1.call-done = bf16[512,768]{1,0:T(8,128)(2,1)} async-done(((bf16[4096,768]{1,0:T(8,128)(2,1)}), bf16[512,768]{1,0:T(8,128)(2,1)}) %reduce-scatter.6.cloned.1.call-update) | async-done | bytes 786448 | tf_op jit(solution)/shard_map/reduce_scatter | solution.py:488
  638.6 29.4 %all-gather.14.cloned.1.call-done = bf16[8,216,768]{2,1,0:T(8,128)(2,1)} async-done(((bf16[1,216,768]{2,1,0:T(8,128)(2,1)}), bf16[8,216,768]{2,1,0:T(8,128)(2,1)}) %all-gather.14.cloned.1.call-update) | async-done | bytes 2654224 | tf_op jit(solution)/shard_map/all_gather | solution.py:282
  (228 shorter events, 77.1 us)
Async XLA Ops:
  8.0 40.6 %all-gather.12.cloned.1.call-start = ((), (), s32[]{:S(2)}) async-start(), calls=%async_computation.5 | async-start | bytes 1658880 | tf_op jit(solution)/shard_map/all_gather | solution.py:353
  12.8 62.6 %all-reduce.6.cloned.1.call-start = ((), (), s32[]{:S(2)}) async-start(), calls=%async_computation.6 | async-start | bytes 393216 | tf_op jit(solution)/shard_map/psum | solution.py:369
  13.6 81.7 %all-gather.16.cloned.1.call-start = ((), (), s32[]{:S(2)}) async-start(), calls=%async_computation.12 | async-start | bytes 7077888 | tf_op jit(solution)/shard_map/all_gather | solution.py:317
  14.4 153.1 %all-gather.10.cloned.1.call-start = ((), (), s32[]{:S(2)}) async-start(), calls=%async_computation.4 | async-start | bytes 4423680 | tf_op jit(solution)/shard_map/all_gather | solution.py:321
  15.5 33.9 %copy-start.27 = (bf16[768]{0:T(1024)(128)(2,1)S(1)}, bf16[768]{0:T(1024)(128)(2,1)}, u32[]{:S(2)}) copy-start(bf16[768]{0:T(1024)(128)(2,1)} %param.32) | copy-start | bytes 4612
  15.5 33.9 %copy-start.28 = (bf16[192]{0:T(256)(128)(2,1)S(1)}, bf16[192]{0:T(256)(128)(2,1)}, u32[]{:S(2)}) copy-start(bf16[192]{0:T(256)(128)(2,1)} %param.29) | copy-start | bytes 1156
  15.5 33.9 %copy-start.29 = (bf16[192]{0:T(256)(128)(2,1)S(1)}, bf16[192]{0:T(256)(128)(2,1)}, u32[]{:S(2)}) copy-start(bf16[192]{0:T(256)(128)(2,1)} %param.30) | copy-start | bytes 1156
  15.5 33.9 %copy-start.30 = (bf16[192]{0:T(256)(128)(2,1)S(1)}, bf16[192]{0:T(256)(128)(2,1)}, u32[]{:S(2)}) copy-start(bf16[192]{0:T(256)(128)(2,1)} %param.31) | copy-start | bytes 1156
  15.5 33.9 %copy-start.31 = (bf16[192]{0:T(256)(128)(2,1)S(1)}, bf16[192]{0:T(256)(128)(2,1)}, u32[]{:S(2)}) copy-start(bf16[192]{0:T(256)(128)(2,1)} %param.33) | copy-start | bytes 1156
  15.5 33.9 %copy-start.32 = (bf16[192]{0:T(256)(128)(2,1)S(1)}, bf16[192]{0:T(256)(128)(2,1)}, u32[]{:S(2)}) copy-start(bf16[192]{0:T(256)(128)(2,1)} %param.34) | copy-start | bytes 1156
  15.5 33.9 %copy-start.33 = (bf16[192]{0:T(256)(128)(2,1)S(1)}, bf16[192]{0:T(256)(128)(2,1)}, u32[]{:S(2)}) copy-start(bf16[192]{0:T(256)(128)(2,1)} %param.35) | copy-start | bytes 1156
  15.5 33.9 %copy-start.34 = (bf16[192]{0:T(256)(128)(2,1)S(1)}, bf16[192]{0:T(256)(128)(2,1)}, u32[]{:S(2)}) copy-start(bf16[192]{0:T(256)(128)(2,1)} %param.36) | copy-start | bytes 1156
  15.5 33.9 %copy-start.35 = (bf16[192]{0:T(256)(128)(2,1)S(1)}, bf16[192]{0:T(256)(128)(2,1)}, u32[]{:S(2)}) copy-start(bf16[192]{0:T(256)(128)(2,1)} %param.37) | copy-start | bytes 1156
  15.8 47.8 %copy-start.26 = (s32[1,8,12,3]{2,1,3,0:T(8,128)S(1)}, s32[1,8,12,3]{2,1,3,0:T(8,128)}, u32[]{:S(2)}) copy-start(s32[1,8,12,3]{2,1,3,0:T(8,128)} %param.22) | copy-start | bytes 3460
  15.8 151.6 %copy-start.17 = (bf16[1,512,768]{2,1,0:T(8,128)(2,1)S(1)}, bf16[1,512,768]{2,1,0:T(8,128)(2,1)}, u32[]{:S(2)}) copy-start(bf16[1,512,768]{2,1,0:T(8,128)(2,1)} %param.19) | copy-start | bytes 2359300
  16.8 223.4 %all-gather.18.cloned.1.call-start = ((), (), s32[]{:S(2)}) async-start(), calls=%async_computation.13 | async-start | bytes 11943936 | tf_op jit(solution)/shard_map/all_gather | solution.py:354
  48.7 413.0 %all-reduce.8.cloned.1.call-start = ((), (), s32[]{:S(2)}) async-start(), calls=%async_computation.14 | async-start | bytes 21233664
  64.0 121.3 %copy-start.2 = (s32[288]{0:T(512)}, s32[288]{0:T(512)S(1)}, u32[]{:S(2)}) copy-start(s32[288]{0:T(512)S(1)} %reshape.289.table) | copy-start | bytes 3460
  64.1 121.2 %copy-start.3 = (s32[2]{0:T(128)}, s32[2]{0:T(128)S(1)}, u32[]{:S(2)}) copy-start(s32[2]{0:T(128)S(1)} %pad_add_fusion.meta) | copy-start | bytes 28
  169.8 15.5 %copy-start = (bf16[528,768]{1,0:T(8,128)(2,1)}, bf16[528,768]{1,0:T(8,128)(2,1)S(1)}, u32[]{:S(2)}) copy-start(bf16[528,768]{1,0:T(8,128)(2,1)S(1)} %fusion.25.q_ref) | copy-start | bytes 2433028
  256.9 28.6 %copy-start.7 = (f32[528,768]{1,0:T(8,128)}, f32[528,768]{1,0:T(8,128)S(1)}, u32[]{:S(2)}) copy-start(f32[528,768]{1,0:T(8,128)S(1)} %get-tuple-element.81) | copy-start | bytes 4866052
  305.4 7.8 %copy-start.5 = (f32[528,768]{1,0:T(8,128)}, f32[528,768]{1,0:T(8,128)S(1)}, u32[]{:S(2)}) copy-start(f32[528,768]{1,0:T(8,128)S(1)} %get-tuple-element.38) | copy-start | bytes 4866052
  312.6 202.9 %reduce-scatter.8.cloned.1.call-start = ((), (), s32[]{:S(2)}) async-start(), calls=%async_computation.8 | async-start | bytes 4423680 | tf_op jit(solution)/shard_map/reduce_scatter | solution.py:276
  374.9 7.7 %copy-start.10 = (bf16[528,768]{1,0:T(8,128)(2,1)S(1)}, bf16[528,768]{1,0:T(8,128)(2,1)}, u32[]{:S(2)}) copy-start(bf16[528,768]{1,0:T(8,128)(2,1)} %get-tuple-element.25) | copy-start | bytes 2433028
  374.9 7.7 %copy-start.19 = (bf16[1,512,768]{2,1,0:T(8,128)(2,1)S(1)}, bf16[1,512,768]{2,1,0:T(8,128)(2,1)}, u32[]{:S(2)}) copy-start(bf16[1,512,768]{2,1,0:T(8,128)(2,1)} %param.19) | copy-start | bytes 2359300
  417.3 132.8 %reduce-scatter.12.cloned.1.call-start = ((), (), s32[]{:S(2)}) async-start(), calls=%async_computation.10 | async-start | bytes 1658880 | tf_op jit(solution)/shard_map/reduce_scatter | solution.py:281
  464.8 107.6 %reduce-scatter.10.cloned.1.call-start = ((), (), s32[]{:S(2)}) async-start(), calls=%async_computation.9 | async-start | bytes 614400 | tf_op jit(solution)/shard_map/reduce_scatter | solution.py:281
  515.5 13.9 %copy-start.6 = (f32[528,768]{1,0:T(8,128)S(1)}, f32[528,768]{1,0:T(8,128)}, u32[]{:S(2)}) copy-start(f32[528,768]{1,0:T(8,128)} %copy-done.5) | copy-start | bytes 4866052
  515.5 120.6 %reduce-scatter.6.cloned.1.call-start = ((), (), s32[]{:S(2)}) async-start(), calls=%async_computation.7 | async-start | bytes 7077888 | tf_op jit(solution)/shard_map/reduce_scatter | solution.py:488
  515.6 13.8 %copy-start.11 = (bf16[528,768]{1,0:T(8,128)(2,1)S(1)}, bf16[528,768]{1,0:T(8,128)(2,1)}, u32[]{:S(2)}) copy-start(bf16[528,768]{1,0:T(8,128)(2,1)} %get-tuple-element.25) | copy-start | bytes 2433028
  543.6 6.6 copy-start.12
  543.6 124.5 %all-gather.14.cloned.1.call-start = ((), (), s32[]{:S(2)}) async-start(), calls=%async_computation.11 | async-start | bytes 2985984 | tf_op jit(solution)/shard_map/all_gather | solution.py:282
  (18 other events, 41.2 us)
Sparse Core Ops, SparseCore 0:
  12.9 35.6 all-gather.11
  50.5 44.6 all-gather.15
  97.4 69.9 all-gather.9
  169.2 62.7 all-gather.17
Sparse Core Ops, SparseCore 1:
  16.9 58.4 all-reduce.5
  312.7 149.0 all-reduce.7
  465.5 49.9 reduce-scatter.7
  518.4 31.6 reduce-scatter.11
  552.4 20.0 reduce-scatter.9
  576.3 59.9 reduce-scatter.5
  637.9 30.1 all-gather.13

commit v2 on v1

v2 whole, which is shorter than its diff:
```python
from functools import partial, reduce

import jax
import jax.numpy as jnp
from jax import lax
from jax.experimental import pallas as pl
from jax.experimental.pallas import tpu as pltpu
from jax.sharding import PartitionSpec as P

H = 12
HD = 64
BLOCK = 64
GLOB = 2
RAND = 3
PAIR = 2 * HD
PAIRS = H // 2
AHEAD = 2
GROUPS = ((0, AHEAD), (AHEAD, PAIRS - AHEAD))
BACK = ((0, 0, 2), (1, 0, 2), (1, 2, 1), (1, 3, 1))
BACK_COST = (8, 8, 8, 20)
MOVING = 3 + RAND
UNROLL = 2
LISTED = (GLOB + MOVING) * BLOCK
PIECES = 8
NEGATIVE = -1e30
EPSILON = 1e-12
FACTOR = HD ** (-0.5)
SLOPE = (2.0 / jnp.pi) ** 0.5
CUBIC = 0.044715
F32 = jnp.float32
BF16 = jnp.bfloat16
MIB = 2**20


def taking(microseconds):
    return pl.CostEstimate(
        flops=int(microseconds * 10**9), bytes_accessed=10**6, transcendentals=0
    )


def groups_of(shards):
    return [list(range(s, s + PIECES)) for s in range(0, shards, PIECES)]


def across_groups(shards):
    return [list(range(s, shards, PIECES)) for s in range(PIECES)]


def dot(a, b):
    return jnp.dot(a, b, preferred_element_type=F32)


def dot_t(a, b):
    return lax.dot_general(a, b, (((1,), (1,)), ((), ())), preferred_element_type=F32)


def t_dot(a, b):
    return lax.dot_general(a, b, (((0,), (0,)), ((), ())), preferred_element_type=F32)


def after(value, *earlier):
    return pl.pallas_call(
        lambda *refs: None,
        in_specs=[pl.BlockSpec(memory_space=pl.ANY)] * (1 + len(earlier)),
        out_specs=pl.BlockSpec(memory_space=pl.ANY),
        out_shape=jax.ShapeDtypeStruct(value.shape, value.dtype),
        input_output_aliases={0: 0},
        name="after",
    )(value, *earlier)


def by_head(both, low, inner):
    zero = jnp.zeros_like(both)
    first, second = jnp.where(low, both, zero), jnp.where(low, zero, both)
    if inner:
        first, second = second, first
    return jnp.concatenate(
        [jnp.concatenate([first, zero], axis=1), jnp.concatenate([zero, second], axis=1)], axis=0
    )


def listed_keys(starts, spot, top, kv_ref):
    rows = [
        [pl.multiple_of(starts[spot + head * MOVING + i], BLOCK) for i in range(MOVING)]
        for head in range(2)
    ]
    parts = [kv_ref[pl.ds(top, GLOB * BLOCK), :]]
    parts += [kv_ref[pl.ds(at, BLOCK), :] for at in rows[0][:3]]
    parts += [
        jnp.concatenate(
            [kv_ref[pl.ds(first, BLOCK), :PAIR], kv_ref[pl.ds(second, BLOCK), PAIR:]], axis=1
        )
        for first, second in zip(rows[0][3:], rows[1][3:])
    ]
    return jnp.concatenate(parts, axis=0), rows


def loader(refs, streamed):
    if not streamed:
        return lambda i: refs[i][...]
    buffer, semaphore = streamed

    def load(i):
        copy = pltpu.make_async_copy(refs[i], buffer, semaphore)
        copy.start()
        copy.wait()
        return buffer[...]

    return load


def softmax(scores):
    raised = jnp.exp(scores - jnp.max(scores, axis=0, keepdims=True))
    return (raised * (1.0 / jnp.sum(raised, axis=0, keepdims=True))).astype(BF16)


def by_core(grad, core, parts):
    half = grad.shape[0] // parts // 2
    halves = [
        jnp.concatenate([grad[at : at + half] for at in range(i * half, grad.shape[0], 2 * half)])
        for i in range(2)
    ]
    first = core == 0
    return jnp.where(first, halves[0], halves[1]), jnp.where(first, halves[1], halves[0])


def forward_kernel(
    starts, limits, x_ref, w_ref, b_ref, *rest, first, row_blocks, extra, shards, waits
):
    seen_refs = rest[:shards]
    q_ref, kv_ref, out_ref, p_ref, pg_ref = rest[shards + waits :][:5]
    tokens = loader(seen_refs, rest[shards + waits + 5 :])
    top = pl.multiple_of(starts[row_blocks * H * MOVING], BLOCK)
    pair = first + pl.program_id(0)
    rows = row_blocks * BLOCK
    low = lax.broadcasted_iota(jnp.int32, (1, PAIR), 1) < HD
    within = lax.broadcasted_iota(jnp.int32, (BLOCK, PAIR), 0)

    queries = dot(x_ref[...], w_ref[:, :PAIR]) + b_ref[0, :, :PAIR]
    q_ref[...] = (queries.astype(BF16).astype(F32) * FACTOR).astype(BF16)

    for i in range(shards):
        kv = dot(tokens(i), w_ref[:, PAIR:]) + b_ref[0, :, PAIR:]
        kv_ref[i * rows : (i + 1) * rows, :] = kv.astype(BF16)

    def one_block(block, carry):
        at = pl.ds(pl.multiple_of(block * BLOCK, BLOCK), BLOCK)
        spot = (block * H + 2 * pair) * MOVING
        kv, _ = listed_keys(starts, spot, top, kv_ref)
        scores = dot_t(kv, by_head(q_ref[at, :], low, True))
        masked = [scores[: GLOB * BLOCK]]
        for i in range(MOVING):
            limit = jnp.where(low, limits[spot + i], limits[spot + MOVING + i])
            here = scores[(GLOB + i) * BLOCK : (GLOB + i + 1) * BLOCK]
            masked.append(jnp.where(within < limit, here, NEGATIVE))
        probs = softmax(jnp.concatenate(masked, axis=0))
        p_ref[block, 0] = probs
        out = t_dot(probs, kv)
        out_ref[at, :] = jnp.where(low, out[:BLOCK, :PAIR], out[BLOCK:, PAIR:]).astype(BF16)
        return carry

    lax.fori_loop(0, row_blocks, one_block, 0, unroll=UNROLL)

    wide = by_head(q_ref[rows : rows + extra, :], low, True)
    within = lax.broadcasted_iota(jnp.int32, (rows, 2 * extra), 0)
    scores = []
    for i in range(shards):
        limit = limits[row_blocks * H * MOVING + i]
        here = dot_t(kv_ref[i * rows : (i + 1) * rows, :], wide)
        scores.append(jnp.where(within < limit, here, NEGATIVE))
    summit = jnp.max(reduce(jnp.maximum, scores), axis=0, keepdims=True)
    raised = [jnp.exp(here - summit) for here in scores]
    share = 1.0 / jnp.sum(reduce(jnp.add, raised), axis=0, keepdims=True)
    out = None
    for i in range(shards):
        here = slice(i * rows, (i + 1) * rows)
        probs = (raised[i] * share).astype(BF16)
        pg_ref[0, here, :] = probs
        term = t_dot(probs, kv_ref[here, :])
        out = term if out is None else out + term
    out_ref[rows : rows + extra, :] = jnp.where(
        low, out[:extra, :PAIR], out[extra:, PAIR:]
    ).astype(BF16)


def backward_kernel(
    starts,
    x_ref,
    q_ref,
    do_ref,
    kv_ref,
    p_ref,
    pg_ref,
    *rest,
    first,
    row_blocks,
    extra,
    shards,
    parts,
    waits,
):
    seen_refs = rest[:shards]
    dq_ref, dkv_ref, near_ref, away_ref, qsum_ref, vsum_ref, acc = rest[shards + waits :][:7]
    tokens = loader(seen_refs, rest[shards + waits + 7 :])
    core = starts[row_blocks * H * MOVING + 1]
    top = pl.multiple_of(starts[row_blocks * H * MOVING], BLOCK)
    pair = first + pl.program_id(0)
    rows = row_blocks * BLOCK
    low = lax.broadcasted_iota(jnp.int32, (1, PAIR), 1) < HD

    def back(kv, probs, q_both, do_both):
        count = q_both.shape[0]
        wide_do = by_head(do_both, low, False)
        wide = probs.astype(F32)
        dp = dot_t(kv, wide_do)
        ds = (wide * (dp - jnp.sum(wide * dp, axis=0, keepdims=True))).astype(BF16)
        dq = t_dot(ds, kv)
        dq = (jnp.where(low, dq[count:, PAIR:], dq[:count, :PAIR]) * FACTOR).astype(BF16)
        rows_in = jnp.concatenate([wide_do, by_head(q_both, low, True)], axis=0)
        return dq, dot(jnp.concatenate([probs, ds], axis=1), rows_in)

    last = slice(rows, rows + extra)
    wide_do = by_head(do_ref[last, :], low, False)
    cuts = [slice(i * rows, (i + 1) * rows) for i in range(shards)]
    dps = [dot_t(kv_ref[here, :], wide_do) for here in cuts]
    terms = [pg_ref[0, here, :].astype(F32) * dp for here, dp in zip(cuts, dps)]
    delta = jnp.sum(reduce(jnp.add, terms), axis=0, keepdims=True)
    rows_in = jnp.concatenate([wide_do, by_head(q_ref[last, :], low, True)], axis=0)
    dq = None
    for here, dp in zip(cuts, dps):
        probs = pg_ref[0, here, :]
        ds = (probs.astype(F32) * (dp - delta)).astype(BF16)
        term = t_dot(ds, kv_ref[here, :])
        dq = term if dq is None else dq + term
        acc[here, :] = dot(jnp.concatenate([probs, ds], axis=1), rows_in)
    dq = jnp.where(low, dq[extra:, PAIR:], dq[:extra, :PAIR]) * FACTOR
    dq_ref[last, :] = dq.astype(BF16)

    def one_block(block, carry):
        at = pl.ds(pl.multiple_of(block * BLOCK, BLOCK), BLOCK)
        spot = (block * H + 2 * pair) * MOVING
        kv, places = listed_keys(starts, spot, top, kv_ref)
        dq_ref[at, :], dkv = back(kv, p_ref[block, 0], q_ref[at, :], do_ref[at, :])
        acc[pl.ds(top, GLOB * BLOCK), :] += dkv[: GLOB * BLOCK]
        for i in range(MOVING):
            here = dkv[(GLOB + i) * BLOCK : (GLOB + i + 1) * BLOCK]
            if i < 3:
                acc[pl.ds(places[0][i], BLOCK), :] += here
            else:
                acc[pl.ds(places[0][i], BLOCK), :PAIR] += here[:, :PAIR]
                acc[pl.ds(places[1][i], BLOCK), PAIR:] += here[:, PAIR:]
        return carry

    lax.fori_loop(0, row_blocks, one_block, 0, unroll=UNROLL)
    dkv_ref[...] = acc[...].astype(BF16)
    total = jnp.sum(acc[...], axis=0, keepdims=True)
    vsum_ref[0] = jnp.where(low, total[:, :PAIR], total[:, PAIR:])
    total = jnp.sum(dq_ref[...].astype(F32), axis=0, keepdims=True)
    qsum_ref[0] = jnp.concatenate([total[:, HD:], total[:, :HD]], axis=1)
    near, away = by_core(t_dot(x_ref[...], dq_ref[...]), core, parts)
    near_ref[:, :PAIR], away_ref[:, :PAIR] = near.astype(BF16), away.astype(BF16)
    total = None
    for i in range(shards):
        term = t_dot(tokens(i), dkv_ref[i * rows : (i + 1) * rows, :])
        total = term if total is None else total + term
    near, away = by_core(total, core, parts)
    near_ref[:, PAIR:], away_ref[:, PAIR:] = near.astype(BF16), away.astype(BF16)


def piece_specs(rows, width, shards):
    if shards > PIECES:
        scratch = [pltpu.VMEM((rows, width), BF16), pltpu.SemaphoreType.DMA]
        return [pl.BlockSpec(memory_space=pl.ANY)] * shards, scratch
    spec = pl.BlockSpec((rows, width), lambda p, *_: (0, 0), pipeline_mode=pl.Buffered(1))
    return [spec] * shards, []


def long_spec(shape, place, shards):
    if shards > PIECES:
        return pl.BlockSpec(shape, place, pipeline_mode=pl.Buffered(1))
    return pl.BlockSpec(shape, place)


def attention_forward(starts, limits, x, pieces, weights, b_qkv, waits, first, count, extra):
    rows, width, shards = x.shape[0], x.shape[1], len(pieces)
    seq = shards * (rows - extra)
    row_blocks = (rows - extra) // BLOCK
    specs, scratch = piece_specs(rows - extra, width, shards)
    return pl.pallas_call(
        partial(
            forward_kernel,
            first=first,
            row_blocks=row_blocks,
            extra=extra,
            shards=shards,
            waits=len(waits),
        ),
        grid_spec=pltpu.PrefetchScalarGridSpec(
            num_scalar_prefetch=2,
            grid=(count,),
            in_specs=[
                pl.BlockSpec((rows, width), lambda p, *_: (0, 0)),
                pl.BlockSpec((width, 3 * PAIR), lambda p, *_: (0, p)),
                pl.BlockSpec((1, 1, 3 * PAIR), lambda p, *_: (first + p, 0, 0)),
            ]
            + specs
            + [pl.BlockSpec(memory_space=pl.ANY)] * len(waits),
            out_specs=[
                pl.BlockSpec((rows, PAIR), lambda p, *_: (0, p)),
                long_spec((seq, 2 * PAIR), lambda p, *_: (0, p), shards),
                pl.BlockSpec((rows, PAIR), lambda p, *_: (0, p)),
                pl.BlockSpec((row_blocks, 1, LISTED, PAIR), lambda p, *_: (0, p, 0, 0)),
                long_spec((1, seq, 2 * extra), lambda p, *_: (p, 0, 0), shards),
            ],
            scratch_shapes=scratch,
        ),
        out_shape=[
            jax.ShapeDtypeStruct((rows, count * PAIR), BF16),
            jax.ShapeDtypeStruct((seq, 2 * count * PAIR), BF16),
            jax.ShapeDtypeStruct((rows, count * PAIR), BF16),
            jax.ShapeDtypeStruct((row_blocks, count, LISTED, PAIR), BF16),
            jax.ShapeDtypeStruct((count, seq, 2 * extra), BF16),
        ],
        compiler_params=pltpu.CompilerParams(vmem_limit_bytes=58 * MIB),
        cost_estimate=taking(10 * count),
        name="attention_forward",
    )(starts, limits, x, weights, b_qkv, *pieces, *waits)


def attention_backward(
    starts, x, pieces, q, do, kv, probs, global_probs, waits, first, offset, count, cost, extra
):
    rows, seq, width, shards = q.shape[0], kv.shape[0], x.shape[1], len(pieces)
    parts = lax.axis_size("wt")
    row_blocks = (rows - extra) // BLOCK
    specs, scratch = piece_specs(rows - extra, width, shards)
    return pl.pallas_call(
        partial(
            backward_kernel,
            first=first,
            row_blocks=row_blocks,
            extra=extra,
            shards=shards,
            parts=parts,
            waits=len(waits),
        ),
        grid_spec=pltpu.PrefetchScalarGridSpec(
            num_scalar_prefetch=1,
            grid=(count,),
            in_specs=[
                pl.BlockSpec((rows, width), lambda p, *_: (0, 0)),
                pl.BlockSpec((rows, PAIR), lambda p, *_: (0, offset + p)),
                pl.BlockSpec((rows, PAIR), lambda p, *_: (0, first + p)),
                long_spec((seq, 2 * PAIR), lambda p, *_: (0, offset + p), shards),
                pl.BlockSpec((row_blocks, 1, LISTED, PAIR), lambda p, *_: (0, offset + p, 0, 0)),
                long_spec((1, seq, 2 * extra), lambda p, *_: (offset + p, 0, 0), shards),
            ]
            + specs
            + [pl.BlockSpec(memory_space=pl.ANY)] * len(waits),
            out_specs=[
                pl.BlockSpec((rows, PAIR), lambda p, *_: (0, p)),
                long_spec((seq, 2 * PAIR), lambda p, *_: (0, p), shards),
                pl.BlockSpec((width // 2, 3 * PAIR), lambda p, *_: (0, p)),
                pl.BlockSpec((width // 2, 3 * PAIR), lambda p, *_: (0, p)),
                pl.BlockSpec((1, 1, PAIR), lambda p, *_: (p, 0, 0)),
                pl.BlockSpec((1, 1, PAIR), lambda p, *_: (p, 0, 0)),
            ],
            scratch_shapes=[pltpu.VMEM((seq, 2 * PAIR), F32), *scratch],
        ),
        out_shape=[
            jax.ShapeDtypeStruct((rows, count * PAIR), BF16),
            jax.ShapeDtypeStruct((seq, 2 * count * PAIR), BF16),
            jax.ShapeDtypeStruct((width // 2, 3 * count * PAIR), BF16),
            jax.ShapeDtypeStruct((width // 2, 3 * count * PAIR), BF16),
            jax.ShapeDtypeStruct((count, 1, PAIR), F32),
            jax.ShapeDtypeStruct((count, 1, PAIR), F32),
        ],
        compiler_params=pltpu.CompilerParams(vmem_limit_bytes=60 * MIB),
        cost_estimate=taking(cost),
        name="attention_backward",
    )(starts, x, q, do, kv, probs, global_probs, *pieces, *waits)


def centered_root(value):
    centered = value - jnp.mean(value, axis=1, keepdims=True)
    root = lax.rsqrt(jnp.mean(centered * centered, axis=1, keepdims=True) + EPSILON)
    return centered * root, root


def norm_back(grad, normed, root):
    mean = jnp.mean(grad, axis=1, keepdims=True)
    return root * (grad - mean - normed * jnp.mean(grad * normed, axis=1, keepdims=True))


def expand_piece(ref, piece):
    half = ref.shape[3] // 2
    blocks = []
    for part in range(ref.shape[1]):
        blocks += [ref[piece, part, :, :half], ref[piece, part, :, half:]]
    return jnp.concatenate(blocks, axis=0)


def contract_piece(ref, piece):
    return jnp.concatenate([ref[piece, part] for part in range(ref.shape[1])], axis=0)


def layer_kernel(
    me,
    x_ref,
    att0_ref,
    att1_ref,
    cot_ref,
    keep_ref,
    wo_ref,
    we_ref,
    wc_ref,
    be_ref,
    vec_ref,
    out_ref,
    one_ref,
    do_ref,
    wok_ref,
    woa_ref,
    ck_ref,
    ca_ref,
    ek_ref,
    ea_ref,
    beg_ref,
    vecg_ref,
    norm_ref,
    root_ref,
    low_ref,
    slope_ref,
    hid_ref,
    acc_ref,
    two_ref,
):
    step = pl.program_id(0)
    core = me[0] % 2
    row = lambda i: vec_ref[i : i + 1, :]

    @pl.when(step == 0)
    def _():
        cut = att0_ref.shape[1]
        branch = dot(att0_ref[...], wo_ref[:cut]) + dot(att1_ref[...], wo_ref[cut:])
        normed, root = centered_root(x_ref[...].astype(F32) + branch + row(0))
        norm_ref[...] = normed
        root_ref[...] = root
        normed = normed * row(1) + row(2)
        low_ref[...] = normed.astype(BF16)
        acc_ref[...] = normed + row(3)

    @pl.when(step < 4)
    def _():
        for i, piece in enumerate((core, 1 - core)):
            u = dot(low_ref[...], expand_piece(we_ref, piece)) + be_ref[piece]
            square = u * u
            t = jnp.tanh(SLOPE * u * (1.0 + CUBIC * square))
            half = 0.5 * (1.0 + t)
            hidden = (u * half).astype(BF16)
            slope_ref[step, i] = half + (0.5 * SLOPE) * u * (1.0 - t * t) * (
                1.0 + (3.0 * CUBIC) * square
            )
            hid_ref[step, i] = hidden
            acc_ref[...] += dot(hidden, contract_piece(wc_ref, piece))

    @pl.when(step == 4)
    def _():
        normed, root = centered_root(acc_ref[...])
        out_ref[...] = (keep_ref[...] * (normed * row(4) + row(5))).astype(BF16)
        cot = cot_ref[...].astype(F32)
        vecg_ref[4:5, :] = jnp.sum(cot * normed, axis=0, keepdims=True)
        vecg_ref[5:6, :] = jnp.sum(cot, axis=0, keepdims=True)
        two = norm_back(cot * row(4), normed, root)
        acc_ref[...] = two
        two = two.astype(BF16)
        two_ref[...] = two
        vecg_ref[3:4, :] = jnp.sum(two.astype(F32), axis=0, keepdims=True)

    @pl.when(step >= 4)
    def _():
        at = step - 4
        for i, (piece, c_ref, e_ref) in enumerate(
            ((core, ck_ref, ek_ref), (1 - core, ca_ref, ea_ref))
        ):
            c_ref[0] = t_dot(hid_ref[at, i], two_ref[...]).astype(BF16)
            grad = (dot_t(two_ref[...], contract_piece(wc_ref, piece)) * slope_ref[at, i]).astype(BF16)
            e_ref[0] = t_dot(low_ref[...], grad).astype(BF16)
            beg_ref[piece] = jnp.sum(grad.astype(F32), axis=0, keepdims=True)
            acc_ref[...] += dot_t(grad, expand_piece(we_ref, piece))

    @pl.when(step == 7)
    def _():
        first = acc_ref[...]
        normed = norm_ref[...]
        vecg_ref[1:2, :] = jnp.sum(first * normed, axis=0, keepdims=True)
        vecg_ref[2:3, :] = jnp.sum(first, axis=0, keepdims=True)
        one = norm_back(first * row(1), normed, root_ref[...])
        one_ref[...] = one
        one = one.astype(BF16)
        vecg_ref[0:1, :] = jnp.sum(one.astype(F32), axis=0, keepdims=True)
        vecg_ref[6:8, :] = jnp.zeros((2, one.shape[1]), F32)
        grad = [t_dot(att_ref[...], one) for att_ref in (att0_ref, att1_ref)]
        near, away = by_core(jnp.concatenate(grad, axis=0), core, we_ref.shape[1])
        wok_ref[...], woa_ref[...] = near.astype(BF16), away.astype(BF16)
        do_ref[...] = dot_t(one, wo_ref[...]).astype(BF16)


def layer(c, x, attended, cot, keep, w_output, w_hidden, b_expand, vectors):
    rows, width = x.shape
    parts, piece = w_hidden.shape[1], b_expand.shape[2]
    each = piece // parts
    steps = PIECES // 2
    whole = lambda *shape: pl.BlockSpec(shape, lambda s, me: (0,) * len(shape))
    chip = lambda s, me: (s % steps) ^ ((me[0] % PIECES) // 2)
    sent = lambda *shape: pl.BlockSpec((1, *shape), lambda s, me: (jnp.maximum(s - steps, 0), 0, 0))
    return pl.pallas_call(
        layer_kernel,
        grid_spec=pltpu.PrefetchScalarGridSpec(
            num_scalar_prefetch=1,
            grid=(2 * steps,),
            in_specs=[
                whole(rows, width),
                *[whole(*a.shape) for a in attended],
                whole(rows, width),
                whole(rows, 1),
                whole(width, width),
                pl.BlockSpec((2, parts, each, width), lambda s, me: (chip(s, me), 0, 0, 0)),
                pl.BlockSpec((2, parts, each, width), lambda s, me: (chip(s, me), 0, 1, 0)),
                pl.BlockSpec((2, 1, piece), lambda s, me: (chip(s, me), 0, 0)),
                whole(8, width),
            ],
            out_specs=[
                whole(rows, width),
                whole(rows, width),
                whole(rows, width),
                whole(width // 2, width),
                whole(width // 2, width),
                sent(piece, width),
                sent(piece, width),
                sent(width, piece),
                sent(width, piece),
                pl.BlockSpec((2, 1, piece), lambda s, me: (chip(jnp.maximum(s - steps, 0), me), 0, 0)),
                whole(8, width),
            ],
            scratch_shapes=[
                pltpu.VMEM((rows, width), F32),
                pltpu.VMEM((rows, 1), F32),
                pltpu.VMEM((rows, width), BF16),
                pltpu.VMEM((steps, 2, rows, piece), F32),
                pltpu.VMEM((steps, 2, rows, piece), BF16),
                pltpu.VMEM((rows, width), F32),
                pltpu.VMEM((rows, width), BF16),
            ],
        ),
        out_shape=[
            jax.ShapeDtypeStruct((rows, width), BF16),
            jax.ShapeDtypeStruct((rows, width), F32),
            jax.ShapeDtypeStruct((rows, width), BF16),
            jax.ShapeDtypeStruct((width // 2, width), BF16),
            jax.ShapeDtypeStruct((width // 2, width), BF16),
            jax.ShapeDtypeStruct((steps, piece, width), BF16),
            jax.ShapeDtypeStruct((steps, piece, width), BF16),
            jax.ShapeDtypeStruct((steps, width, piece), BF16),
            jax.ShapeDtypeStruct((steps, width, piece), BF16),
            jax.ShapeDtypeStruct((PIECES, 1, piece), F32),
            jax.ShapeDtypeStruct((8, width), F32),
        ],
        compiler_params=pltpu.CompilerParams(vmem_limit_bytes=58 * MIB),
        cost_estimate=taking(35),
        name="layer",
    )(
        jnp.reshape(c, (1,)).astype(jnp.int32),
        x,
        *attended,
        cot,
        keep,
        w_output,
        w_hidden,
        w_hidden,
        b_expand,
        vectors,
    )


def pair_sum(grad_refs, weight_refs, columns, at):
    total = None
    for (group, offset, count), ref in zip(BACK, grad_refs):
        for pair in range(count):
            start = 3 * PAIR * (offset + pair) + at
            term = dot_t(
                ref[:, pair * columns : (pair + 1) * columns],
                weight_refs[group][:, start : start + columns],
            )
            total = term if total is None else total + term
    return total


def token_kernel(me, *refs, away, extra, count):
    sides = len(BACK)
    dkv_refs, w_refs = refs[:sides], refs[sides : sides + 2]
    c, step = me[0], pl.program_id(0)
    piece = 2 * step + (1 if away else 0)
    half = dkv_refs[0].shape[0] // 2
    if away:
        dq_refs, one_ref = refs[sides + 2 : 2 * sides + 2], refs[2 * sides + 2]
        above_ref, below_ref, share_ref = refs[-3:]

        @pl.when(step == 0)
        def _():
            share_ref[...] = one_ref[...] + pair_sum(dq_refs, w_refs, PAIR, 0)

        share = lambda: share_ref[2 * half : 2 * half + extra, :]
    else:
        share_ref, above_ref, below_ref = refs[sides + 2], *refs[-2:]
        share = lambda: share_ref[...]
    total = pair_sum(dkv_refs, w_refs, 2 * PAIR, PAIR).astype(BF16)
    above_ref[0], below_ref[0] = total[:half], total[half:]

    @pl.when((piece == c) & (c < count))
    def _():
        at = pl.ds(pl.multiple_of(c * extra, extra), extra)
        above_ref[0, at, :] = (above_ref[0, at, :].astype(F32) + share()).astype(BF16)


def token_share(c, dkvs, weights, more, away, waits, rows, extra, count):
    seq, width = dkvs[0].shape[0], weights[0].shape[0]
    chips = seq // rows // 2
    other = 1 if away else 0
    full = lambda a: pl.BlockSpec(a.shape, lambda j, me: (0,) * a.ndim)
    out_specs = [pl.BlockSpec((1, rows // 2, width), lambda j, me: (j, 0, 0))] * 2
    out_shape = [jax.ShapeDtypeStruct((chips, rows // 2, width), BF16)] * 2
    if away:
        out_specs.append(pl.BlockSpec((rows + extra, width), lambda j, me: (0, 0)))
        out_shape.append(jax.ShapeDtypeStruct((rows + extra, width), F32))
    return pl.pallas_call(
        partial(token_kernel, away=away, extra=extra, count=count),
        grid_spec=pltpu.PrefetchScalarGridSpec(
            num_scalar_prefetch=1,
            grid=(chips,),
            in_specs=[
                pl.BlockSpec((rows, a.shape[1]), lambda j, me: (2 * j + other, 0))
                for a in dkvs
            ]
            + [full(a) for a in (*weights, *more)]
            + [pl.BlockSpec(memory_space=pl.ANY)] * len(waits),
            out_specs=out_specs,
        ),
        out_shape=out_shape,
        compiler_params=pltpu.CompilerParams(vmem_limit_bytes=48 * MIB),
        cost_estimate=taking(3),
        name="token_share",
    )(jnp.reshape(c, (1,)).astype(jnp.int32), *dkvs, *weights, *more, *waits)


def by_pair(queries, keys, values):
    count = queries.shape[0]
    together = [a.reshape(count, PAIRS, PAIR) for a in (queries, keys, values)]
    together = jnp.concatenate(together, axis=2).reshape(count * PAIRS, 3 * PAIR)
    places = jnp.arange(3 * PAIR, dtype=jnp.int32)
    source = jnp.array((1, 0, 4, 2, 3, 5), jnp.int32)[places // HD] * HD + places % HD
    return ordered(together, source).astype(BF16).reshape(count, PAIRS * 3 * PAIR)


def column_places(pairs):
    start = jnp.arange(pairs, dtype=jnp.int32)[:, None, None] * (3 * PAIR)
    inner = jnp.arange(HD, dtype=jnp.int32)
    for spots in ((1, 0), (3, 4), (2, 5)):
        yield (start + jnp.array(spots, jnp.int32)[:, None] * HD + inner).reshape(-1)


def swapped(value, bit):
    shards = lax.axis_size("ctx")
    return lax.ppermute(value, "ctx", [(i, i ^ bit) for i in range(shards)])


def own_bit(bit):
    return (lax.axis_index("ctx") // bit) % 2


def added(keep, came):
    return (keep.astype(F32) + came.astype(F32)).astype(BF16)


def halved(value, axis, bit):
    mine = own_bit(bit)
    away = lax.dynamic_index_in_dim(value, 1 - mine, axis, keepdims=False)
    keep = lax.dynamic_index_in_dim(value, mine, axis, keepdims=False)
    return added(keep, swapped(away, bit))


def doubled(value, bit):
    other = swapped(value, bit)
    mine = own_bit(bit) == 0
    return jnp.stack([jnp.where(mine, value, other), jnp.where(mine, other, value)])


def plane_gather(value):
    value = value[None]
    for bit in (1, 2, 4):
        value = doubled(value, bit)
        value = value.reshape(-1, *value.shape[2:])
    return value


def line_step(value, bit):
    parts = lax.axis_size("wt")
    other = lax.ppermute(value, "wt", [(i, i ^ bit) for i in range(parts)])
    mine = lax.axis_index("wt") // bit % 2 == 0
    return jnp.concatenate([jnp.where(mine, value, other), jnp.where(mine, other, value)])


def line_gather(value, bit=1):
    while bit < lax.axis_size("wt"):
        value = line_step(value, bit)
        bit *= 2
    return value


def token_gather(own):
    shards, half = lax.axis_size("ctx"), own.shape[0] // 2
    along_x, along_y = swapped(own, 2), swapped(own, 4)
    far = jnp.concatenate([swapped(along_y[:half], 2), swapped(along_x[half:], 4)], axis=0)
    pieces = []
    for piece in (own, along_x, along_y, far):
        pieces += [piece, swapped(piece, 1)]
    bit = PIECES
    while bit < shards:
        pieces += [swapped(piece, bit) for piece in pieces]
        bit *= 2
    return pieces


def far_sum(value, shards):
    if shards == PIECES:
        return value
    return lax.psum(value, "ctx", axis_index_groups=across_groups(shards))


def same_core(shards, block):
    return [list(range(s + k, s + block, 2)) for s in range(0, shards, block) for k in range(2)]


def rows_start(near, came):
    parts, columns = lax.axis_size("wt"), near.shape[1]
    near, came = (a.reshape(parts, PIECES // 2, -1, columns) for a in (near, came))
    return jnp.transpose(added(near, came), (1, 0, 2, 3)).reshape(parts * PIECES // 2, -1, columns)


def rows_sum(sums):
    shards, parts = lax.axis_size("ctx"), lax.axis_size("wt")
    sums = far_sum(sums, shards)
    groups = [[i * parts + w for i in g for w in range(parts)] for g in same_core(shards, PIECES)]
    sums = lax.all_to_all(
        sums, ("ctx", "wt"), split_axis=0, concat_axis=0, axis_index_groups=groups, tiled=True
    )
    return jnp.sum(sums.astype(F32), axis=0).astype(BF16)


def ordered(value, source):
    rows = jnp.arange(value.shape[1], dtype=jnp.int32)
    return dot(value, (rows[:, None] == source[None, :]).astype(BF16))


def vector_kernel(*refs, parts):
    sides = len(BACK)
    joined = lambda some: jnp.concatenate([r[i] for r in some for i in range(r.shape[0])], axis=1)
    grads_ref, expand_ref, _, out_ref = refs[2 * sides :]
    rows = [joined(refs[:sides]), joined(refs[sides : 2 * sides])]
    rows += [grads_ref[i : i + 1, :] for i in (0, 3, 1, 2, 4, 5)]
    width = out_ref.shape[1]
    share, run = width // parts, expand_ref.shape[2] // parts
    out = []
    for part in range(parts):
        cuts = [row[:, part * share : (part + 1) * share] for row in rows]
        out += [jnp.concatenate(cuts[i : i + parts], axis=1) for i in range(0, len(cuts), parts)]
        cuts = [expand_ref[p, :, part * run : (part + 1) * run] for p in range(PIECES)]
        out.append(jnp.concatenate(cuts, axis=1))
        out.append(jnp.zeros((PIECES - len(rows) // parts - 1, width), F32))
    out_ref[...] = jnp.concatenate(out, axis=0).astype(BF16)


def vector_rows(q_sums, v_sums, grads, expand_grads, wait, parts):
    return pl.pallas_call(
        partial(vector_kernel, parts=parts),
        in_specs=[pl.BlockSpec(memory_space=pltpu.VMEM)] * (2 * len(BACK) + 2)
        + [pl.BlockSpec(memory_space=pl.ANY)],
        out_shape=jax.ShapeDtypeStruct((parts * PIECES, grads.shape[1]), BF16),
        cost_estimate=taking(1),
        name="vector_rows",
    )(*q_sums, *v_sums, grads, expand_grads, wait)


def expand_kernel(in_ref, out_ref):
    pieces, half, run = in_ref.shape[0], in_ref.shape[1], in_ref.shape[2] // 2
    parts = out_ref.shape[1] // in_ref.shape[2]
    count = run // parts
    for lower in range(2):
        for part in range(parts):
            at = lower * run + part * count
            runs = [in_ref[p, :, at : at + count].astype(F32) for p in range(pieces)]
            out_ref[
                lower * half : (lower + 1) * half, part * 2 * run : (part + 1) * 2 * run
            ] = jnp.concatenate(runs, axis=1)


def expand_columns(gathered, each_piece, parts):
    width = gathered.shape[2]
    return pl.pallas_call(
        expand_kernel,
        grid=(1,),
        in_specs=[pl.BlockSpec((PIECES, each_piece, width), lambda i: (0, 1, 0))],
        out_specs=pl.BlockSpec((2 * each_piece, parts * width), lambda i: (0, 0)),
        out_shape=jax.ShapeDtypeStruct((2 * each_piece, parts * width), F32),
        compiler_params=pltpu.CompilerParams(vmem_limit_bytes=24 * MIB),
        cost_estimate=taking(2),
        name="expand_columns",
    )(gathered)


def body(
    tokens,
    cotangent,
    lengths,
    rand_blocks,
    query_weight,
    key_weight,
    value_weight,
    output_weight,
    expand_weight,
    contract_weight,
    query_bias,
    value_bias,
    output_bias,
    expand_bias,
    contract_bias,
    attn_gain,
    attn_shift,
    ffn_gain,
    ffn_shift,
):
    shards = lax.axis_size("ctx")
    parts = lax.axis_size("wt")
    c = lax.axis_index("ctx")
    rows, width = tokens.shape[1], tokens.shape[2]
    row_blocks = rows // BLOCK
    seq = shards * rows
    global_count = GLOB * BLOCK
    extra = 16 * (-(-global_count // (16 * shards)))
    hidden_width = expand_weight.shape[1]
    part = expand_weight.shape[0]
    piece = hidden_width // PIECES
    length = lengths[0]
    inputs = tokens[0]

    pieces = token_gather(inputs)
    small = jnp.concatenate(
        [
            query_bias,
            value_bias,
            output_bias,
            contract_bias,
            attn_gain,
            attn_shift,
            ffn_gain,
            ffn_shift,
            expand_bias,
        ]
    )
    half = part // 2
    bundles = [
        lax.dynamic_slice_in_dim(w, own_bit(1) * half, half, 0)
        for w in (query_weight, key_weight, value_weight)
    ]
    bundles = by_pair(*bundles)
    ahead = AHEAD * 3 * PAIR
    small_rows = 8 * (-(-small.shape[0] // (8 * ahead)))
    padded = jnp.pad(small, (0, small_rows * ahead - small.shape[0])).reshape(small_rows, ahead)
    early_lead = line_step(jnp.concatenate([bundles[:, :ahead], padded], axis=0)[None], 1)
    leading = line_gather(early_lead, 2)
    vectors = leading[:, half:].reshape(parts, -1)[:, : small.shape[0]]
    leading = leading[:, :half]

    def joined(bundle):
        return jnp.transpose(doubled(bundle, 1), (1, 0, 2, 3)).reshape(width, -1)

    weights = [joined(leading)]
    behind = bundles[:, ahead:]
    behind = jnp.concatenate([behind[:, :width], behind[:, width:]], axis=0)
    each = width // parts
    b_query, b_value, b_output, b_contract, g_attn, s_attn, g_ffn, s_ffn = (
        vectors[:, i * each : (i + 1) * each].reshape(-1).astype(F32) for i in range(8)
    )
    b_expand = vectors[:, 8 * each :].reshape(parts, PIECES, -1)
    b_expand = jnp.transpose(b_expand, (1, 0, 2)).reshape(PIECES, 1, piece).astype(F32)

    p = c % PIECES
    each_piece = piece // parts
    e_piece = lax.dynamic_index_in_dim(
        expand_weight.reshape(part, parts, PIECES, -1), p, 2, keepdims=False
    ).reshape(part, piece)
    e_piece = jnp.concatenate([e_piece[:each_piece], e_piece[each_piece:]], axis=1)
    c_piece = lax.dynamic_slice_in_dim(contract_weight, p * each_piece, each_piece, 0)
    o_rows = part // PIECES
    o_piece = lax.dynamic_slice_in_dim(output_weight, p * o_rows, o_rows, 0)
    w_hidden = jnp.concatenate([e_piece, c_piece, o_piece, behind], axis=0)
    w_hidden = after(w_hidden, pieces[1])
    w_hidden = lax.all_gather(w_hidden, "wt")
    mixed = 2 * each_piece + o_rows
    following = w_hidden[:, mixed:].reshape(parts, 2, half, width)
    following = jnp.concatenate([following[:, 0], following[:, 1]], axis=2)

    start = jnp.minimum(c * extra, global_count - extra)
    more = lax.dynamic_slice_in_dim(pieces[0], start, extra, 0)
    for i in range(1, shards):
        other = lax.dynamic_slice_in_dim(pieces[i], start, extra, 0)
        more = jnp.where(c == i, other, more)
    x = jnp.concatenate([inputs, more], axis=0)
    index = jnp.arange(rows + extra, dtype=jnp.int32)
    position = jnp.where(index < rows, c * rows + index, c * extra + index - rows)
    is_global = position < global_count
    usable = ((position < length) & (is_global == (index >= rows)))[:, None]
    own = c * row_blocks + jnp.arange(row_blocks, dtype=jnp.int32)
    beside = own[:, None, None] + jnp.arange(-1, 2, dtype=jnp.int32)
    listed = jnp.concatenate(
        [jnp.broadcast_to(beside, (row_blocks, H, 3)), rand_blocks[0]], axis=2
    )
    blocks = seq // BLOCK
    inside = (listed >= 0) & (listed < blocks)
    listed = jnp.clip(listed, 0, blocks - 1)
    limits = jnp.where(inside, length - listed * BLOCK, 0).reshape(-1)
    order = jnp.arange(shards, dtype=jnp.int32) ^ c
    limits = jnp.concatenate([limits, length - order * rows])
    starts = (listed // row_blocks ^ c) * rows + listed % row_blocks * BLOCK
    starts = jnp.concatenate([starts.reshape(-1), jnp.stack([c * rows, c % 2])])

    given = jnp.where(c == 0, cotangent[0, :global_count], jnp.zeros((), BF16))
    given = jnp.pad(given, ((0, shards * extra - global_count), (0, 0)))
    given = given.reshape(shards, extra, width)
    given = lax.all_to_all(given, "ctx", split_axis=0, concat_axis=0, tiled=True)
    cot = jnp.concatenate([cotangent[0], given[0]], axis=0)
    cot = jnp.where(usable, cot, jnp.zeros((), BF16))

    b_qkv = by_pair(*(b.astype(BF16)[None] for b in (b_query, jnp.zeros_like(b_value), b_value)))
    b_qkv = b_qkv.astype(F32).reshape(PAIRS, 1, 3 * PAIR)
    zero = jnp.zeros_like(b_output)
    vectors = jnp.stack([b_output, g_attn, s_attn, b_contract, g_ffn, s_ffn, zero, zero])
    keep = usable.astype(F32)
    w_hidden = after(
        w_hidden[:, :mixed], *pieces, weights[0], cot, starts, limits, b_qkv, vectors, b_expand, keep, x
    )
    w_hidden = lax.all_gather(w_hidden, "ctx", axis_index_groups=groups_of(shards))
    w_output = jnp.transpose(w_hidden[:, :, 2 * each_piece :], (1, 0, 2, 3)).reshape(width, width)
    forward = partial(attention_forward, starts, limits, x, pieces)
    kept = [forward(weights[0], b_qkv, (cot,), *GROUPS[0], extra)]
    weights.append(joined(following))
    kept.append(forward(weights[1], b_qkv, (), *GROUPS[1], extra))

    (
        layer_out,
        grad_one,
        grad_attended,
        o_keep,
        o_away,
        c_keep,
        c_away,
        e_keep,
        e_away,
        expand_bgrad,
        vector_grads,
    ) = layer(
        c,
        x,
        [k[2] for k in kept],
        cot,
        keep,
        w_output,
        w_hidden,
        b_expand,
        vectors,
    )

    def attention_back(side, *waits):
        group, offset, count = BACK[side]
        q, kv, _, probs, global_probs = kept[group]
        first = GROUPS[group][0] + offset
        return attention_backward(
            starts,
            x,
            pieces,
            q,
            grad_attended,
            kv,
            probs,
            global_probs,
            waits,
            first,
            offset,
            count,
            BACK_COST[side],
            extra,
        )

    c_came, e_came = swapped(c_away, 1), swapped(e_away, 1)
    early = [rows_start(o_keep, swapped(o_away, 1))]
    backs = [attention_back(0)]
    steps = PIECES // 2
    c_keep, c_came = (a.reshape(2, 2, piece, width) for a in (c_keep, c_came))
    e_keep, e_came = (a.reshape(2, 2, width, piece) for a in (e_keep, e_came))
    c_away = added(c_keep[:, 1], c_came[:, 1])
    e_away = added(e_keep[1], e_came[1])
    c_came_on, e_came_on = swapped(c_away, 2), swapped(e_away, 4)
    c_keep = added(c_keep[:, 0], c_came[:, 0])
    e_keep = added(e_keep[0], e_came[0])

    early.append(rows_start(backs[0][2], swapped(backs[0][3], 1)))
    early = jnp.concatenate(early, axis=1)
    backs.append(attention_back(1, c_away, e_away, early))
    early = rows_sum(early)
    c_away, e_away = added(c_keep[1], c_came_on[1]), added(e_keep[1], e_came_on[1])
    c_last, e_last = swapped(c_away, 4), swapped(e_away, 2)
    c_keep, e_keep = added(c_keep[0], c_came_on[0]), added(e_keep[0], e_came_on[0])

    middle = rows_start(backs[1][2], swapped(backs[1][3], 1))
    backs.append(attention_back(2, c_away, e_away, early, middle))
    middle = rows_sum(middle)
    c_mine = far_sum(added(c_keep, c_last), shards).reshape(parts, -1, width)
    e_mine = far_sum(added(e_keep, e_last), shards).reshape(parts, 2, -1, piece)
    e_mine = jnp.concatenate([e_mine[:, 0], e_mine[:, 1]], axis=2)
    hidden_sums = jnp.concatenate([c_mine, e_mine], axis=1)
    both = lax.all_to_all(hidden_sums, "wt", split_axis=0, concat_axis=0, tiled=True)
    backs.append(attention_back(3, hidden_sums, middle))

    share = partial(token_share, c, [b[1] for b in backs], weights)
    count = global_count // extra
    above_away, below_away, own = share(
        [b[0] for b in backs] + [grad_one], True, (both,), rows, extra, count
    )
    both = jnp.sum(both.astype(F32), axis=0).astype(BF16)
    both = jnp.concatenate([both, early, middle, layer_out[rows:]], axis=0)
    above, below = share([own[rows:]], False, (above_away, both), rows, extra, count)

    def by_chip(keep, came):
        chips = shards // 2
        if chips > 4:
            keep = added(keep, came)
            while chips > 4:
                keep = added(keep[: chips // 2], swapped(keep[chips // 2 :], chips))
                chips //= 2
            came = jnp.zeros_like(keep)
        return [a.reshape(2, 2, rows // 2, width) for a in (keep, came)]

    above = by_chip(above, swapped(above_away, 1))
    below = by_chip(below, swapped(below_away, 1))
    above_sent = added(above[0][:, 1], above[1][:, 1])
    below_sent = added(below[0][1], below[1][1])
    above_came, below_came = swapped(above_sent, 2), swapped(below_sent, 4)
    above = added(above[0][:, 0], above[1][:, 0])
    below = added(below[0][0], below[1][0])

    hidden_rows = 2 * each_piece
    gathered = lax.all_gather(both, "ctx", axis_index_groups=groups_of(shards))

    contract_wgrad = gathered[:, :each_piece].reshape(-1, width).astype(F32)
    expand_wgrad = expand_columns(gathered, each_piece, parts)
    finished = gathered[:, -extra:].reshape(-1, width)
    on_first = (c == 0) & (index[:rows] < global_count)
    finished = jnp.pad(finished[:global_count], ((0, rows - global_count), (0, 0)))
    layer_out = jnp.where(on_first[:, None], finished, layer_out[:rows])

    above_came = after(above_came, contract_wgrad, expand_wgrad, layer_out)
    below_came = after(below_came, contract_wgrad, expand_wgrad, layer_out)

    small = vector_rows([b[4] for b in backs], [b[5] for b in backs], vector_grads, expand_bgrad, above_sent, parts)
    small = small.reshape(parts, 2, -1, width)
    near = jnp.concatenate([backs[2][2], backs[3][2]], axis=1).reshape(parts, PIECES // 2, -1, width)
    near = jnp.concatenate(
        [near, lax.dynamic_index_in_dim(small, own_bit(1), 1, keepdims=False)[:, :, None]], axis=2
    )
    far = jnp.concatenate([backs[2][3], backs[3][3]], axis=1).reshape(parts, PIECES // 2, -1, width)
    far = jnp.concatenate(
        [far, lax.dynamic_index_in_dim(small, 1 - own_bit(1), 1, keepdims=False)[:, :, None]], axis=2
    )
    late = rows_start(near.reshape(-1, width), swapped(far, 1))
    late = rows_sum(late)

    above_sent = added(above[1], above_came[1])
    below_sent = added(below[1], below_came[1])
    above_last, below_last = swapped(above_sent, 4), swapped(below_sent, 2)
    above = above[0].astype(F32) + above_came[0].astype(F32) + above_last.astype(F32)
    below = below[0].astype(F32) + below_came[0].astype(F32) + below_last.astype(F32)
    input_grad = own[:rows] + jnp.concatenate([above, below], axis=0)

    late = plane_gather(after(late, above_sent, below_sent))
    kinds = [gathered[:, hidden_rows:-extra].reshape(PIECES, 3, -1, width)]
    kinds.append(late[:, None, :-1])
    mine = jnp.concatenate(kinds, axis=1).reshape(PIECES // 2, 2, 4, -1, width)
    mine = jnp.transpose(mine, (2, 1, 0, 3, 4)).reshape(4, part, width)
    small = jnp.transpose(late[:, -1].reshape(PIECES // 2, 2, width), (1, 0, 2)).reshape(-1, width)
    small = small.astype(F32)
    small_grads = [small[i // parts, i % parts * each :][:each] for i in range(8)]
    expand_bias_grad = small[2]
    output_wgrad = mine[0].astype(F32)
    query_wgrad, key_wgrad, value_wgrad = (
        jnp.concatenate([ordered(g, places) for g in (mine[1], mine[2], mine[3])], axis=1)
        for places in column_places(AHEAD)
    )

    return (
        layer_out[None],
        input_grad[None],
        query_wgrad,
        key_wgrad,
        value_wgrad,
        output_wgrad,
        expand_wgrad,
        contract_wgrad,
        small_grads[0],
        small_grads[1],
        small_grads[2],
        expand_bias_grad,
        small_grads[3],
        small_grads[4],
        small_grads[5],
        small_grads[6],
        small_grads[7],
    )


def solution(mesh):
    tokens, weight, vector = P("wt", "ctx", None), P("wt", None), P("wt")
    return jax.shard_map(
        body,
        mesh=mesh,
        in_specs=(tokens, tokens, vector, P("wt", "ctx", None, None)) + (weight,) * 6 + (vector,) * 9,
        out_specs=(tokens, tokens) + (weight,) * 6 + (vector,) * 9,
        check_vma=False,
    )
```

time: 691 us -> 473 us (0.68)
  waiting for transfers between devices: 316 us -> 109 us
  Pallas kernels: 111 us -> 195 us
  matrix products: 87 us -> 3.33 us
  starting transfers between devices: 0.67 us -> 51.1 us
  local copies, waits for them, and re-layouts: 81.7 us -> 35.8 us
  blocking collectives: 33.5 us -> 0 us
  other arithmetic: 36.5 us -> 54.7 us
    all_gather x5 -> x3, waiting for transfers between devices: 152 us -> 0.02 us  [the longest x1 0.01 us: body(): lax.all_gather(w_hidden, 'ctx', axis_index_groups=groups_of(shards))]
    reduce_scatter x4 -> x0, waiting for transfers between devices: 109 us -> none  [the longest x1 50.4 us: reduced(): lax.psum_scatter(pieces, 'ctx', scatter_dimension=0, axis_index_groups=gr...]
    pallas_call x2 -> x16, Pallas kernels: 111 us -> 195 us  [the longest x4 68.9 us: attention_backward(): pl.pallas_call(partial(backward_kernel, first=first, row_blocks=row_block...]
    ppermute x0 -> x31, waiting for transfers between devices: none -> 81.3 us  [the longest x29 48.6 us: swapped(): return lax.ppermute(value, 'ctx', [(i, i ^ bit) for i in range(shards)])]
    dot_general x10 -> x0, matrix products: 61.2 us -> none  [the longest x5 30.8 us: dot_t(): lax.dot_general(a, b, (((1,), (1,)), ((), ())), preferred_element_type=F32)]
    unnamed x12 -> x3, waiting for transfers between devices: 44 us -> 0.05 us
    all_gather x3 -> x0, blocking collectives: 33.5 us -> none  [the longest x1 13.1 us: body(): small = lax.all_gather(small, 'wt', axis=0, tiled=True)]
    all_to_all x0 -> x5, waiting for transfers between devices: none -> 27.9 us  [the longest x3 16.1 us: rows_sum(): lax.all_to_all(sums, ('ctx', 'wt'), split_axis=0, concat_axis=0, axis_ind...]
  transfers between devices with their start and end apart: 11 -> 39, of which waited for: 10 -> 13; matrix products, arithmetic and copies ran while one was open for 17% -> 17% of each run, Pallas kernels for 16% -> 33%
where the time goes in v2:
time: 473 us; the launch traced here: 465 us
  Pallas kernels  195 us (41%)
  waiting for transfers between devices  109 us (23%)
  other arithmetic  54.7 us (12%)
  starting transfers between devices  51.1 us (11%)
  local copies, waits for them, and re-layouts  35.8 us (8%)
  between operations  15.9 us (3%)
    pallas_call x4, Pallas kernels, attention_backward(): pl.pallas_call(partial(backward_kernel, first=first, row_blocks=row_block...  68.9 us
    pallas_call x2, Pallas kernels, attention_forward(): pl.pallas_call(partial(forward_kernel, first=first, row_blocks=row_blocks...  62.6 us
    ppermute x29, waiting for transfers between devices, swapped(): return lax.ppermute(value, 'ctx', [(i, i ^ bit) for i in range(shards)])  48.6 us
    pallas_call x1, Pallas kernels, layer(): pl.pallas_call(layer_kernel, grid_spec=pltpu.PrefetchScalarGridSpec(num_s...  39.6 us
    ppermute x2, waiting for transfers between devices, line_step(): other = lax.ppermute(value, 'wt', [(i, i ^ bit) for i in range(parts)])  32.6 us
    ppermute x29, starting transfers between devices, swapped(): return lax.ppermute(value, 'ctx', [(i, i ^ bit) for i in range(shards)])  23.6 us
    convert_element_type x13, other arithmetic, added(): return (keep.astype(F32) + came.astype(F32)).astype(BF16)  23.5 us
    pallas_call x2, Pallas kernels, token_share(): pl.pallas_call(partial(token_kernel, away=away, extra=extra, count=count)...  20.3 us
  transfers between devices with their start and end apart: 39, of which 13 were waited for; matrix products, arithmetic and copies ran while one was open for 17% of the time, Pallas kernels for 33%

profile of v2, /device:TPU:0, one launch (start us, length us, event | category | flops | bytes accessed | tf_op | source)
XLA Modules:
  0.0 465.1 jit_solution(1043988901970725855)
XLA Ops:
  7.7 2.6 collective-permute-start
  11.8 3.0 reshape.688
  23.3 3.4 all-to-all-start
  31.6 2.7 collective-permute-start.9
  35.3 32.6 %collective-permute-done.9 = bf16[2,104,768]{2,1,0:T(8,128)(2,1)S(1)} collective-permute-done((bf16[2,104,768]{2,1,0:T(8,128)(2,1)S(1)}, bf16[2,104,768]{2,1,0:T(8,128)(2,1)S(1)}, u32[]{:S(2)}, u32[]{:S(2)}) %collective-permute-start.9) | collective-permute-done | bytes 319520 | tf_op jit(solution)/shard_map/ppermute | solution.py:708
  75.4 4.7 %collective-permute-done.1 = bf16[256,768]{1,0:T(8,128)(2,1)S(1)} collective-permute-done((bf16[256,768]{1,0:T(8,128)(2,1)S(1)}, bf16[256,768]{1,0:T(8,128)(2,1)S(1)}, u32[]{:S(2)}, u32[]{:S(2)}) %collective-permute-start.1) | collective-permute-done | bytes 393248 | tf_op jit(solution)/shard_map/ppermute | solution.py:674
  80.2 3.4 collective-permute-done.3
  90.7 2.5 slice.427.refs_0_
  95.3 22.8 %attention_forward.2 = (bf16[528,256]{1,0:T(8,128)(2,1)}, bf16[4096,512]{1,0:T(8,128)(2,1)}, bf16[528,256]{1,0:T(8,128)(2,1)}, bf16[8,2,512,128]{3,2,1,0:T(8,128)(2,1)}, bf16[2,4096,32]{2,1,0:T(8,128)(2,1)}) custom-call(s32[578]{0:T(1024)} %pad_add_fusion.1.starts.refs_11_, s32[584]{0:T(1024)} %pad_add_fusion.2.limits.refs_12_, ...), custom_call_target="tpu_custom_call" | custom-call | flops 20000000000 | bytes 1000000 | tf_op jit(solution)/shard_map/attention_forward/pallas_call | solution.py:289
  120.2 39.8 %attention_forward.3 = (bf16[528,512]{1,0:T(8,128)(2,1)}, bf16[4096,1024]{1,0:T(8,128)(2,1)}, bf16[528,512]{1,0:T(8,128)(2,1)}, bf16[8,4,512,128]{3,2,1,0:T(8,128)(2,1)}, bf16[4,4096,32]{2,1,0:T(8,128)(2,1)}) custom-call(s32[578]{0:T(1024)} %pad_add_fusion.1.starts.refs_11_, s32[584]{0:T(1024)} %pad_add_fusion.2.limits.refs_12_, ...), custom_call_target="tpu_custom_call" | custom-call | flops 40000000000 | bytes 1000000 | tf_op jit(solution)/shard_map/attention_forward/pallas_call | solution.py:289
  162.4 39.6 %layer.1 = (bf16[528,768]{1,0:T(8,128)(2,1)}, f32[528,768]{1,0:T(8,128)}, bf16[528,768]{1,0:T(8,128)(2,1)}, bf16[384,768]{1,0:T(8,128)(2,1)}, bf16[384,768]{1,0:...) custom-call(s32[1]{0:T(128)} %bitcast.me, ...), custom_call_target="tpu_custom_call" | custom-call | flops 35000000512 | bytes 1000000 | tf_op jit(solution)/shard_map/layer/pallas_call | solution.py:517
  202.7 21.0 %attention_backward.4 = (bf16[528,256]{1,0:T(8,128)(2,1)}, bf16[4096,512]{1,0:T(8,128)(2,1)}, bf16[384,768]{1,0:T(8,128)(2,1)}, bf16[384,768]{1,0:T(8,128)(2,1)}...) custom-call(s32[578]{0:T(1024)} %pad_add_fusion.1.starts.refs_11_, bf16[528,768]{1,0:T(8,128)(2,1)} %pad_maximum_fusion.3.x_ref.refs_17_, ...), custom_call_target="tpu_custom_call" | custom-call | flops 8000000000 | bytes 1000000 | tf_op jit(solution)/shard_map/attention_backward/pallas_call | solution.py:337
  227.4 5.2 %all-to-all-start.2 = ((bf16[16,48,768]{2,1,0:T(8,128)(2,1)}), bf16[16,48,768]{2,1,0:T(8,128)(2,1)S(1)}, u32[]{:S(2)}, u32[]{:S(2)}) async-start(bf16[16,48,768]{2,1,0:T(8,128)(2,1)} %pad_maximum_fusion.2.rest_10_), calls=%async_computation.2 | async-start | bytes 2359296 | tf_op jit(solution)/shard_map/all_to_all | solution.py:754
  232.6 4.1 add_convert_fusion.1
  238.6 3.2 add_convert_fusion.3
  243.3 20.8 %attention_backward.5 = (bf16[528,256]{1,0:T(8,128)(2,1)}, bf16[4096,512]{1,0:T(8,128)(2,1)}, bf16[384,768]{1,0:T(8,128)(2,1)}, bf16[384,768]{1,0:T(8,128)(2,1)}...) custom-call(s32[578]{0:T(1024)} %pad_add_fusion.1.starts.refs_11_, bf16[528,768]{1,0:T(8,128)(2,1)} %pad_maximum_fusion.3.x_ref.refs_17_, ...), custom_call_target="tpu_custom_call" | custom-call | flops 8000000000 | bytes 1000000 | tf_op jit(solution)/shard_map/attention_backward/pallas_call | solution.py:337
  264.1 9.2 %collective-permute-done.16 = bf16[2,768,384]{2,1,0:T(8,128)(2,1)} collective-permute-done((bf16[2,768,384]{2,1,0:T(8,128)(2,1)}, bf16[2,768,384]{2,1,0:T(8,128)(2,1)}, u32[]{:S(2)}, u32[]{:S(2)}) %collective-permute-start.16) | collective-permute-done | bytes 1179680 | tf_op jit(solution)/shard_map/ppermute | solution.py:674
  277.8 6.1 %all-to-all-start.3 = ((bf16[16,24,768]{2,1,0:T(8,128)(2,1)}), bf16[16,24,768]{2,1,0:T(8,128)(2,1)}, u32[]{:S(2)}, u32[]{:S(2)}) async-start(bf16[16,24,768]{2,1,0:T(8,128)(2,1)} %bitcast.253), calls=%async_computation.3 | async-start | bytes 1179648 | tf_op jit(solution)/shard_map/all_to_all | solution.py:754
  287.0 7.9 %collective-permute-done.17 = bf16[768,384]{1,0:T(8,128)(2,1)} collective-permute-done((bf16[768,384]{1,0:T(8,128)(2,1)}, bf16[768,384]{1,0:T(8,128)(2,1)}, u32[]{:S(2)}, u32[]{:S(2)}) %collective-permute-start.17) | collective-permute-done | bytes 589856 | tf_op jit(solution)/shard_map/ppermute | solution.py:674
  296.5 8.7 %collective-permute-done.14 = bf16[384,768]{1,0:T(8,128)(2,1)S(1)} collective-permute-done((bf16[384,768]{1,0:T(8,128)(2,1)S(1)}, bf16[384,768]{1,0:T(8,128)(2,1)S(1)}, u32[]{:S(2)}, u32[]{:S(2)}) %collective-permute-start.14) | collective-permute-done | bytes 589856 | tf_op jit(solution)/shard_map/ppermute | solution.py:674
  307.6 4.2 all-to-all-start.1
  313.4 13.6 %attention_backward.6 = (bf16[528,128]{1,0:T(8,128)(2,1)}, bf16[4096,256]{1,0:T(8,128)(2,1)}, bf16[384,384]{1,0:T(8,128)(2,1)}, bf16[384,384]{1,0:T(8,128)(2,1)}...) custom-call(s32[578]{0:T(1024)} %pad_add_fusion.1.starts.refs_11_, bf16[528,768]{1,0:T(8,128)(2,1)} %pad_maximum_fusion.3.x_ref.refs_17_, ...), custom_call_target="tpu_custom_call" | custom-call | flops 8000000000 | bytes 1000000 | tf_op jit(solution)/shard_map/attention_backward/pallas_call | solution.py:337
  328.1 11.8 %all-to-all-done.1.refs_11_ = bf16[4,192,768]{2,1,0:T(8,128)(2,1)S(1)} async-done(((bf16[4,192,768]{2,1,0:T(8,128)(2,1)}), bf16[4,192,768]{2,1,0:T(8,128)(2,1)S(1)}, u32[]{:S(2)}, u32[]{:S(2)}) %all-to-all-start.1) | async-done | bytes 1179680 | tf_op jit(solution)/shard_map/all_to_all | solution.py:1031
  341.1 13.6 %attention_backward.7 = (bf16[528,128]{1,0:T(8,128)(2,1)}, bf16[4096,256]{1,0:T(8,128)(2,1)}, bf16[384,384]{1,0:T(8,128)(2,1)}, bf16[384,384]{1,0:T(8,128)(2,1)}...) custom-call(s32[578]{0:T(1024)} %pad_add_fusion.1.starts.refs_11_, bf16[528,768]{1,0:T(8,128)(2,1)} %pad_maximum_fusion.3.x_ref.refs_17_, ...), custom_call_target="tpu_custom_call" | custom-call | flops 20000000000 | bytes 1000000 | tf_op jit(solution)/shard_map/attention_backward/pallas_call | solution.py:337
  355.6 11.7 %token_share.2 = (bf16[4,256,768]{2,1,0:T(8,128)(2,1)}, bf16[4,256,768]{2,1,0:T(8,128)(2,1)}, f32[528,768]{1,0:T(8,128)}) custom-call(s32[1]{0:T(128)} %bitcast.me, bf16[4096,512]{1,0:T(8,128)(2,1)} %get-tuple-element.89.refs_0_, bf16[4096,512]{1,0:T(8,128)(2,1)} %get-tuple-element.90.refs_1_, bf16[4096,256]{1,0:T(8,128)(2,1)} %get-tuple-element.91.refs_2_, ...), custom_call_target="tpu_custom_call" | custom-call | flops 3000000000 | bytes 1000000 | tf_op jit(solution)/shard_map/token_share/pallas_call | solution.py:636
  369.6 8.6 %token_share.3 = (bf16[4,256,768]{2,1,0:T(8,128)(2,1)S(1)}, bf16[4,256,768]{2,1,0:T(8,128)(2,1)S(1)}) custom-call(s32[1]{0:T(128)} %bitcast.me, bf16[4096,512]{1,0:T(8,128)(2,1)} %get-tuple-element.89.refs_0_, bf16[4096,512]{1,0:T(8,128)(2,1)} %get-tuple-element.90.refs_1_, bf16[4096,256]{1,0:T(8,128)(2,1)} %get-tuple-element.91.refs_2_, ...), custom_call_target="tpu_custom_call" | custom-call | flops 3000000000 | bytes 1000000 | tf_op jit(solution)/shard_map/token_share/pallas_call | solution.py:636
  378.2 2.9 add_convert_fusion.7
  387.9 4.2 all-to-all-start.4
  394.1 3.0 add_convert_fusion.5
  398.6 16.1 %all-to-all-done.4 = bf16[16,25,768]{2,1,0:T(8,128)(2,1)S(1)} async-done(((bf16[16,25,768]{2,1,0:T(8,128)(2,1)}), bf16[16,25,768]{2,1,0:T(8,128)(2,1)S(1)}, u32[]{:S(2)}, u32[]{:S(2)}) %all-to-all-start.4) | async-done | bytes 614432 | tf_op jit(solution)/shard_map/all_to_all | solution.py:754
  430.9 4.9 %collective-permute-done.29 = bf16[2,25,768]{2,1,0:T(8,128)(2,1)} collective-permute-done((bf16[2,25,768]{2,1,0:T(8,128)(2,1)}, bf16[2,25,768]{2,1,0:T(8,128)(2,1)}, u32[]{:S(2)}, u32[]{:S(2)}) %collective-permute-start.29) | collective-permute-done | bytes 76832 | tf_op jit(solution)/shard_map/ppermute | solution.py:674
  440.0 5.6 %collective-permute-done.30 = bf16[4,25,768]{2,1,0:T(8,128)(2,1)} collective-permute-done((bf16[4,25,768]{2,1,0:T(8,128)(2,1)}, bf16[4,25,768]{2,1,0:T(8,128)(2,1)}, u32[]{:S(2)}, u32[]{:S(2)}) %collective-permute-start.30) | collective-permute-done | bytes 153632 | tf_op jit(solution)/shard_map/ppermute | solution.py:674
  (318 shorter events, 105.8 us)
Async XLA Ops:
  7.2 20.1 %collective-permute-start.7 = (bf16[512,768]{1,0:T(8,128)(2,1)}, bf16[512,768]{1,0:T(8,128)(2,1)S(1)}, u32[]{:S(2)}, u32[]{:S(2)}) collective-permute-start(bf16[512,768]{1,0:T(8,128)(2,1)} %bitcast.236), channel_id=1, source_target_pairs={{0,4},{4,0},{8,12},{12,8},{16,20},{20,16},{24,28},{28,24},{1,5},{5... | collective-permute-start | bytes 2359304 | tf_op jit(solution)/shard_map/ppermute | solution.py:674
  7.7 60.3 %collective-permute-start = (bf16[512,768]{1,0:T(8,128)(2,1)}, bf16[512,768]{1,0:T(8,128)(2,1)}, u32[]{:S(2)}, u32[]{:S(2)}) collective-permute-start(bf16[512,768]{1,0:T(8,128)(2,1)} %bitcast.237), channel_id=1, source_target_pairs={{0,16},{4,20},{8,24},{12,28},{16,0},{20,4},{24,8},{28,12},{1,17},{... | collective-permute-start | bytes 2359304 | tf_op jit(solution)/shard_map/ppermute | solution.py:674
  10.3 60.5 %collective-permute-start.2 = (bf16[512,768]{1,0:T(8,128)(2,1)}, bf16[512,768]{1,0:T(8,128)(2,1)}, u32[]{:S(2)}, u32[]{:S(2)}) collective-permute-start(bf16[512,768]{1,0:T(8,128)(2,1)} %bitcast.238), channel_id=1, source_target_pairs={{0,8},{4,12},{8,0},{12,4},{16,24},{20,28},{24,16},{28,20},{1,9},{5... | collective-permute-start | bytes 2359304 | tf_op jit(solution)/shard_map/ppermute | solution.py:674
  21.0 10.5 %collective-permute-start.8 = (bf16[1,104,768]{2,1,0:T(8,128)(2,1)S(1)}, bf16[1,104,768]{2,1,0:T(8,128)(2,1)S(1)}, u32[]{:S(2)}, u32[]{:S(2)}) collective-permute-start(bf16[1,104,768]{2,1,0:T(8,128)(2,1)S(1)} %maximum_bitcast_fusion.2), channel_id=1, source_target_pairs={{0,1},{1,0},{2,3},{3,2},{4,5},{5,4},{6,7},{7,6},{8,9},{9,8},{10,11... | collective-permute-start | bytes 479240 | tf_op jit(solution)/shard_map/ppermute | solution.py:708
  23.3 10.9 %all-to-all-start = ((bf16[8,16,768]{2,1,0:T(8,128)(2,1)}), bf16[8,16,768]{2,1,0:T(8,128)(2,1)S(1)}, u32[]{:S(2)}, u32[]{:S(2)}) async-start(bf16[8,16,768]{2,1,0:T(8,128)(2,1)} %bitcast.14), calls=%async_computation | async-start | bytes 393216 | tf_op jit(solution)/shard_map/all_to_all | solution.py:940
  26.7 64.0 %all-gather.7.cloned.1.call-start = ((), (), s32[]{:S(2)}) async-start(), calls=%async_computation.5 | async-start | bytes 3133440 | tf_op jit(solution)/shard_map/all_gather | solution.py:908
  28.2 131.8 %all-gather.9.cloned.1.call-start = ((), (), s32[]{:S(2)}) async-start(), calls=%async_computation.6 | async-start | bytes 11943936 | tf_op jit(solution)/shard_map/all_gather | solution.py:952
  31.6 36.4 %collective-permute-start.9 = (bf16[2,104,768]{2,1,0:T(8,128)(2,1)S(1)}, bf16[2,104,768]{2,1,0:T(8,128)(2,1)S(1)}, u32[]{:S(2)}, u32[]{:S(2)}) collective-permute-start(bf16[2,104,768]{2,1,0:T(8,128)(2,1)S(1)} %pad_maximum_fusion.12), channel_id=1, source_target_pairs={{0,2},{1,3},{2,0},{3,1},{4,6},{5,7},{6,4},{7,5},{8,10},{9,11},{10,... | collective-permute-start | bytes 958472 | tf_op jit(solution)/shard_map/ppermute | solution.py:708
  69.1 11.1 %collective-permute-start.1 = (bf16[256,768]{1,0:T(8,128)(2,1)S(1)}, bf16[256,768]{1,0:T(8,128)(2,1)S(1)}, u32[]{:S(2)}, u32[]{:S(2)}) collective-permute-start(bf16[256,768]{1,0:T(8,128)(2,1)S(1)} %slice.414), channel_id=1, source_target_pairs={{0,8},{4,12},{8,0},{12,4},{16,24},{20,28},{24,16},{28,20},{1,9},{5... | collective-permute-start | bytes 1179656 | tf_op jit(solution)/shard_map/ppermute | solution.py:674
  72.6 11.0 %collective-permute-start.3 = (bf16[256,768]{1,0:T(8,128)(2,1)}, bf16[256,768]{1,0:T(8,128)(2,1)}, u32[]{:S(2)}, u32[]{:S(2)}) collective-permute-start(bf16[256,768]{1,0:T(8,128)(2,1)} %slice.415), channel_id=1, source_target_pairs={{0,16},{4,20},{8,24},{12,28},{16,0},{20,4},{24,8},{28,12},{1,17},{... | collective-permute-start | bytes 1179656 | tf_op jit(solution)/shard_map/ppermute | solution.py:674
  74.8 12.4 %collective-permute-start.10 = (bf16[4,96,768]{2,1,0:T(8,128)(2,1)S(1)}, bf16[4,96,768]{2,1,0:T(8,128)(2,1)S(1)}, u32[]{:S(2)}, u32[]{:S(2)}) collective-permute-start(bf16[4,96,768]{2,1,0:T(8,128)(2,1)S(1)} %fusion.21), channel_id=1, source_target_pairs={{0,4},{4,0},{8,12},{12,8},{16,20},{20,16},{24,28},{28,24},{1,5},{5... | collective-permute-start | bytes 1769480 | tf_op jit(solution)/shard_map/ppermute | solution.py:674
  74.8 13.6 %collective-permute-start.5 = (bf16[512,768]{1,0:T(8,128)(2,1)}, bf16[512,768]{1,0:T(8,128)(2,1)S(1)}, u32[]{:S(2)}, u32[]{:S(2)}) collective-permute-start(bf16[512,768]{1,0:T(8,128)(2,1)} %collective-permute-done.rest_4_.refs_5_), channel_id=1, source_target_pairs={{0,4},{4,0},{8,12},{12,8},{16,20},{20,16},{24,28},{28,24},{1,5},{5... | collective-permute-start | bytes 2359304 | tf_op jit(solution)/shard_map/ppermute | solution.py:674
  75.3 13.1 %collective-permute-start.6 = (bf16[512,768]{1,0:T(8,128)(2,1)}, bf16[512,768]{1,0:T(8,128)(2,1)}, u32[]{:S(2)}, u32[]{:S(2)}) collective-permute-start(bf16[512,768]{1,0:T(8,128)(2,1)} %collective-permute-done.2.rest_2_.refs_3_), channel_id=1, source_target_pairs={{0,4},{4,0},{8,12},{12,8},{16,20},{20,16},{24,28},{28,24},{1,5},{5... | collective-permute-start | bytes 2359304 | tf_op jit(solution)/shard_map/ppermute | solution.py:674
  94.7 23.4 %collective-permute-start.11 = (bf16[4,96,1536]{2,1,0:T(8,128)(2,1)S(1)}, bf16[4,96,1536]{2,1,0:T(8,128)(2,1)S(1)}, u32[]{:S(2)}, u32[]{:S(2)}) collective-permute-start(bf16[4,96,1536]{2,1,0:T(8,128)(2,1)S(1)} %pad_maximum_fusion.1), channel_id=1, source_target_pairs={{0,4},{4,0},{8,12},{12,8},{16,20},{20,16},{24,28},{28,24},{1,5},{5... | collective-permute-start | bytes 3538952 | tf_op jit(solution)/shard_map/ppermute | solution.py:674
  202.0 30.6 %collective-permute-start.15 = (bf16[4,768,384]{2,1,0:T(8,128)(2,1)}, bf16[4,768,384]{2,1,0:T(8,128)(2,1)}, u32[]{:S(2)}, u32[]{:S(2)}) collective-permute-start(bf16[4,768,384]{2,1,0:T(8,128)(2,1)} %get-tuple-element.72), channel_id=1, source_target_pairs={{0,4},{4,0},{8,12},{12,8},{16,20},{20,16},{24,28},{28,24},{1,5},{5... | collective-permute-start | bytes 7077896 | tf_op jit(solution)/shard_map/ppermute | solution.py:674
  202.1 36.5 %collective-permute-start.12 = (bf16[4,384,768]{2,1,0:T(8,128)(2,1)}, bf16[4,384,768]{2,1,0:T(8,128)(2,1)}, u32[]{:S(2)}, u32[]{:S(2)}) collective-permute-start(bf16[4,384,768]{2,1,0:T(8,128)(2,1)} %get-tuple-element.70), channel_id=1, source_target_pairs={{0,4},{4,0},{8,12},{12,8},{16,20},{20,16},{24,28},{28,24},{1,5},{5... | collective-permute-start | bytes 7077896 | tf_op jit(solution)/shard_map/ppermute | solution.py:674
  202.6 21.6 %collective-permute-start.18 = (bf16[384,768]{1,0:T(8,128)(2,1)}, bf16[384,768]{1,0:T(8,128)(2,1)S(1)}, u32[]{:S(2)}, u32[]{:S(2)}) collective-permute-start(bf16[384,768]{1,0:T(8,128)(2,1)} %get-tuple-element.74), channel_id=1, source_target_pairs={{0,4},{4,0},{8,12},{12,8},{16,20},{20,16},{24,28},{28,24},{1,5},{5... | collective-permute-start | bytes 1769480 | tf_op jit(solution)/shard_map/ppermute | solution.py:674
  227.4 50.4 %all-to-all-start.2 = ((bf16[16,48,768]{2,1,0:T(8,128)(2,1)}), bf16[16,48,768]{2,1,0:T(8,128)(2,1)S(1)}, u32[]{:S(2)}, u32[]{:S(2)}) async-start(bf16[16,48,768]{2,1,0:T(8,128)(2,1)} %pad_maximum_fusion.2.rest_10_), calls=%async_computation.2 | async-start | bytes 2359296 | tf_op jit(solution)/shard_map/all_to_all | solution.py:754
  236.7 36.6 %collective-permute-start.16 = (bf16[2,768,384]{2,1,0:T(8,128)(2,1)}, bf16[2,768,384]{2,1,0:T(8,128)(2,1)}, u32[]{:S(2)}, u32[]{:S(2)}) collective-permute-start(bf16[2,768,384]{2,1,0:T(8,128)(2,1)} %get-tuple-element.122.rest_9_), channel_id=1, source_target_pairs={{0,16},{4,20},{8,24},{12,28},{16,0},{20,4},{24,8},{28,12},{1,17},{... | collective-permute-start | bytes 3538952 | tf_op jit(solution)/shard_map/ppermute | solution.py:674
  241.8 42.1 %collective-permute-start.13 = (bf16[2,384,768]{2,1,0:T(8,128)(2,1)}, bf16[2,384,768]{2,1,0:T(8,128)(2,1)}, u32[]{:S(2)}, u32[]{:S(2)}) collective-permute-start(bf16[2,384,768]{2,1,0:T(8,128)(2,1)} %get-tuple-element.120.rest_8_), channel_id=1, source_target_pairs={{0,8},{4,12},{8,0},{12,4},{16,24},{20,28},{24,16},{28,20},{1,9},{5... | collective-permute-start | bytes 3538952 | tf_op jit(solution)/shard_map/ppermute | solution.py:674
  264.0 12.7 %collective-permute-start.20 = (bf16[384,768]{1,0:T(8,128)(2,1)}, bf16[384,768]{1,0:T(8,128)(2,1)S(1)}, u32[]{:S(2)}, u32[]{:S(2)}) collective-permute-start(bf16[384,768]{1,0:T(8,128)(2,1)} %get-tuple-element.87), channel_id=1, source_target_pairs={{0,4},{4,0},{8,12},{12,8},{16,20},{20,16},{24,28},{28,24},{1,5},{5... | collective-permute-start | bytes 1769480 | tf_op jit(solution)/shard_map/ppermute | solution.py:674
  275.3 19.7 %collective-permute-start.17 = (bf16[768,384]{1,0:T(8,128)(2,1)}, bf16[768,384]{1,0:T(8,128)(2,1)}, u32[]{:S(2)}, u32[]{:S(2)}) collective-permute-start(bf16[768,384]{1,0:T(8,128)(2,1)} %fusion.23.rest_9_), channel_id=1, source_target_pairs={{0,8},{4,12},{8,0},{12,4},{16,24},{20,28},{24,16},{28,20},{1,9},{5... | collective-permute-start | bytes 1769480 | tf_op jit(solution)/shard_map/ppermute | solution.py:674
  277.8 29.8 %all-to-all-start.3 = ((bf16[16,24,768]{2,1,0:T(8,128)(2,1)}), bf16[16,24,768]{2,1,0:T(8,128)(2,1)}, u32[]{:S(2)}, u32[]{:S(2)}) async-start(bf16[16,24,768]{2,1,0:T(8,128)(2,1)} %bitcast.253), calls=%async_computation.3 | async-start | bytes 1179648 | tf_op jit(solution)/shard_map/all_to_all | solution.py:754
  285.1 20.1 %collective-permute-start.14 = (bf16[384,768]{1,0:T(8,128)(2,1)S(1)}, bf16[384,768]{1,0:T(8,128)(2,1)S(1)}, u32[]{:S(2)}, u32[]{:S(2)}) collective-permute-start(bf16[384,768]{1,0:T(8,128)(2,1)S(1)} %fusion.25.rest_8_), channel_id=1, source_target_pairs={{0,16},{4,20},{8,24},{12,28},{16,0},{20,4},{24,8},{28,12},{1,17},{... | collective-permute-start | bytes 1769480 | tf_op jit(solution)/shard_map/ppermute | solution.py:674
  307.6 32.4 %all-to-all-start.1 = ((bf16[4,192,768]{2,1,0:T(8,128)(2,1)}), bf16[4,192,768]{2,1,0:T(8,128)(2,1)S(1)}, u32[]{:S(2)}, u32[]{:S(2)}) async-start(bf16[4,192,768]{2,1,0:T(8,128)(2,1)} %maximum_maximum_fusion.rest_8_), calls=%async_computation.1 | async-start | bytes 2359296 | tf_op jit(solution)/shard_map/all_to_all | solution.py:1031
  311.8 103.6 %all-gather.11.cloned.1.call-start = ((), (), s32[]{:S(2)}) async-start(), calls=%async_computation.7 | async-start | bytes 3870720 | tf_op jit(solution)/shard_map/all_gather | solution.py:1062
  367.4 10.8 %collective-permute-start.21 = (bf16[4,256,768]{2,1,0:T(8,128)(2,1)}, bf16[4,256,768]{2,1,0:T(8,128)(2,1)}, u32[]{:S(2)}, u32[]{:S(2)}) collective-permute-start(bf16[4,256,768]{2,1,0:T(8,128)(2,1)} %get-tuple-element.99.refs_7_), channel_id=1, source_target_pairs={{0,4},{4,0},{8,12},{12,8},{16,20},{20,16},{24,28},{28,24},{1,5},{5... | collective-permute-start | bytes 4718600 | tf_op jit(solution)/shard_map/ppermute | solution.py:674
  387.9 26.7 %all-to-all-start.4 = ((bf16[16,25,768]{2,1,0:T(8,128)(2,1)}), bf16[16,25,768]{2,1,0:T(8,128)(2,1)S(1)}, u32[]{:S(2)}, u32[]{:S(2)}) async-start(bf16[16,25,768]{2,1,0:T(8,128)(2,1)} %bitcast.74), calls=%async_computation.4 | async-start | bytes 1572864 | tf_op jit(solution)/shard_map/all_to_all | solution.py:754
  392.2 31.6 %collective-permute-start.22 = (bf16[2,256,768]{2,1,0:T(8,128)(2,1)}, bf16[2,256,768]{2,1,0:T(8,128)(2,1)}, u32[]{:S(2)}, u32[]{:S(2)}) collective-permute-start(bf16[2,256,768]{2,1,0:T(8,128)(2,1)} %get-tuple-element.124.refs_10_), channel_id=1, source_target_pairs={{0,8},{4,12},{8,0},{12,4},{16,24},{20,28},{24,16},{28,20},{1,9},{5... | collective-permute-start | bytes 2359304 | tf_op jit(solution)/shard_map/ppermute | solution.py:674
  397.1 28.6 %collective-permute-start.25 = (bf16[2,256,768]{2,1,0:T(8,128)(2,1)}, bf16[2,256,768]{2,1,0:T(8,128)(2,1)}, u32[]{:S(2)}, u32[]{:S(2)}) collective-permute-start(bf16[2,256,768]{2,1,0:T(8,128)(2,1)} %get-tuple-element.126), channel_id=1, source_target_pairs={{0,16},{4,20},{8,24},{12,28},{16,0},{20,4},{24,8},{28,12},{1,17},{... | collective-permute-start | bytes 2359304 | tf_op jit(solution)/shard_map/ppermute | solution.py:674
  438.2 16.2 %collective-permute-start.23 = (bf16[256,768]{1,0:T(8,128)(2,1)}, bf16[256,768]{1,0:T(8,128)(2,1)S(1)}, u32[]{:S(2)}, u32[]{:S(2)}) collective-permute-start(bf16[256,768]{1,0:T(8,128)(2,1)} %fusion.32.refs_1_), channel_id=1, source_target_pairs={{0,16},{4,20},{8,24},{12,28},{16,0},{20,4},{24,8},{28,12},{1,17},{... | collective-permute-start | bytes 1179656 | tf_op jit(solution)/shard_map/ppermute | solution.py:674
  439.7 15.9 %collective-permute-start.26 = (bf16[256,768]{1,0:T(8,128)(2,1)}, bf16[256,768]{1,0:T(8,128)(2,1)S(1)}, u32[]{:S(2)}, u32[]{:S(2)}) collective-permute-start(bf16[256,768]{1,0:T(8,128)(2,1)} %fusion.31.refs_2_), channel_id=1, source_target_pairs={{0,8},{4,12},{8,0},{12,4},{16,24},{20,28},{24,16},{28,20},{1,9},{5... | collective-permute-start | bytes 1179656 | tf_op jit(solution)/shard_map/ppermute | solution.py:674
  (51 other events, 282.5 us)
Sparse Core Ops, SparseCore 0:
  29.7 60.2 all-gather.6
  93.3 63.5 all-gather.8
  341.2 32.1 all-gather.10

commit v3 on v2

--- a/solution.py
+++ b/solution.py
@@ -19,7 +19,7 @@
 BACK = ((0, 0, 2), (1, 0, 2), (1, 2, 1), (1, 3, 1))
 BACK_COST = (8, 8, 8, 20)
 MOVING = 3 + RAND
-UNROLL = 2
+TOGETHER = 8
 LISTED = (GLOB + MOVING) * BLOCK
 PIECES = 8
 NEGATIVE = -1e30
@@ -143,23 +143,27 @@
         kv = dot(tokens(i), w_ref[:, PAIR:]) + b_ref[0, :, PAIR:]
         kv_ref[i * rows : (i + 1) * rows, :] = kv.astype(BF16)
 
-    def one_block(block, carry):
-        at = pl.ds(pl.multiple_of(block * BLOCK, BLOCK), BLOCK)
-        spot = (block * H + 2 * pair) * MOVING
-        kv, _ = listed_keys(starts, spot, top, kv_ref)
-        scores = dot_t(kv, by_head(q_ref[at, :], low, True))
-        masked = [scores[: GLOB * BLOCK]]
-        for i in range(MOVING):
-            limit = jnp.where(low, limits[spot + i], limits[spot + MOVING + i])
-            here = scores[(GLOB + i) * BLOCK : (GLOB + i + 1) * BLOCK]
-            masked.append(jnp.where(within < limit, here, NEGATIVE))
-        probs = softmax(jnp.concatenate(masked, axis=0))
-        p_ref[block, 0] = probs
-        out = t_dot(probs, kv)
-        out_ref[at, :] = jnp.where(low, out[:BLOCK, :PAIR], out[BLOCK:, PAIR:]).astype(BF16)
+    def some_blocks(group, carry):
+        blocks = [group * TOGETHER + i for i in range(TOGETHER)]
+        ats = [pl.ds(pl.multiple_of(block * BLOCK, BLOCK), BLOCK) for block in blocks]
+        spots = [(block * H + 2 * pair) * MOVING for block in blocks]
+        kvs = [listed_keys(starts, spot, top, kv_ref)[0] for spot in spots]
+        scores = [dot_t(kv, by_head(q_ref[at, :], low, True)) for kv, at in zip(kvs, ats)]
+        probs = []
+        for some, spot in zip(scores, spots):
+            masked = [some[: GLOB * BLOCK]]
+            for i in range(MOVING):
+                limit = jnp.where(low, limits[spot + i], limits[spot + MOVING + i])
+                here = some[(GLOB + i) * BLOCK : (GLOB + i + 1) * BLOCK]
+                masked.append(jnp.where(within < limit, here, NEGATIVE))
+            probs.append(softmax(jnp.concatenate(masked, axis=0)))
+        outs = [t_dot(some, kv) for some, kv in zip(probs, kvs)]
+        for block, at, some, out in zip(blocks, ats, probs, outs):
+            p_ref[block, 0] = some
+            out_ref[at, :] = jnp.where(low, out[:BLOCK, :PAIR], out[BLOCK:, PAIR:]).astype(BF16)
         return carry
 
-    lax.fori_loop(0, row_blocks, one_block, 0, unroll=UNROLL)
+    lax.fori_loop(0, row_blocks // TOGETHER, some_blocks, 0)
 
     wide = by_head(q_ref[rows : rows + extra, :], low, True)
     within = lax.broadcasted_iota(jnp.int32, (rows, 2 * extra), 0)
@@ -208,17 +212,6 @@
     rows = row_blocks * BLOCK
     low = lax.broadcasted_iota(jnp.int32, (1, PAIR), 1) < HD
 
-    def back(kv, probs, q_both, do_both):
-        count = q_both.shape[0]
-        wide_do = by_head(do_both, low, False)
-        wide = probs.astype(F32)
-        dp = dot_t(kv, wide_do)
-        ds = (wide * (dp - jnp.sum(wide * dp, axis=0, keepdims=True))).astype(BF16)
-        dq = t_dot(ds, kv)
-        dq = (jnp.where(low, dq[count:, PAIR:], dq[:count, :PAIR]) * FACTOR).astype(BF16)
-        rows_in = jnp.concatenate([wide_do, by_head(q_both, low, True)], axis=0)
-        return dq, dot(jnp.concatenate([probs, ds], axis=1), rows_in)
-
     last = slice(rows, rows + extra)
     wide_do = by_head(do_ref[last, :], low, False)
     cuts = [slice(i * rows, (i + 1) * rows) for i in range(shards)]
@@ -236,22 +229,43 @@
     dq = jnp.where(low, dq[extra:, PAIR:], dq[:extra, :PAIR]) * FACTOR
     dq_ref[last, :] = dq.astype(BF16)
 
-    def one_block(block, carry):
-        at = pl.ds(pl.multiple_of(block * BLOCK, BLOCK), BLOCK)
-        spot = (block * H + 2 * pair) * MOVING
-        kv, places = listed_keys(starts, spot, top, kv_ref)
-        dq_ref[at, :], dkv = back(kv, p_ref[block, 0], q_ref[at, :], do_ref[at, :])
-        acc[pl.ds(top, GLOB * BLOCK), :] += dkv[: GLOB * BLOCK]
-        for i in range(MOVING):
-            here = dkv[(GLOB + i) * BLOCK : (GLOB + i + 1) * BLOCK]
-            if i < 3:
-                acc[pl.ds(places[0][i], BLOCK), :] += here
-            else:
-                acc[pl.ds(places[0][i], BLOCK), :PAIR] += here[:, :PAIR]
-                acc[pl.ds(places[1][i], BLOCK), PAIR:] += here[:, PAIR:]
+    def some_blocks(group, carry):
+        blocks = [group * TOGETHER + i for i in range(TOGETHER)]
+        ats = [pl.ds(pl.multiple_of(block * BLOCK, BLOCK), BLOCK) for block in blocks]
+        listed = [
+            listed_keys(starts, (block * H + 2 * pair) * MOVING, top, kv_ref) for block in blocks
+        ]
+        kvs = [kv for kv, _ in listed]
+        dos = [by_head(do_ref[at, :], low, False) for at in ats]
+        dps = [dot_t(kv, do) for kv, do in zip(kvs, dos)]
+        probs = [p_ref[block, 0] for block in blocks]
+        dss = []
+        for some, dp in zip(probs, dps):
+            wide = some.astype(F32)
+            dss.append((wide * (dp - jnp.sum(wide * dp, axis=0, keepdims=True))).astype(BF16))
+        dqs = [t_dot(ds, kv) for ds, kv in zip(dss, kvs)]
+        dkvs = [
+            dot(
+                jnp.concatenate([some, ds], axis=1),
+                jnp.concatenate([do, by_head(q_ref[at, :], low, True)], axis=0),
+            )
+            for some, ds, do, at in zip(probs, dss, dos, ats)
+        ]
+        for at, dq in zip(ats, dqs):
+            dq = jnp.where(low, dq[BLOCK:, PAIR:], dq[:BLOCK, :PAIR]) * FACTOR
+            dq_ref[at, :] = dq.astype(BF16)
+        acc[pl.ds(top, GLOB * BLOCK), :] += reduce(jnp.add, [d[: GLOB * BLOCK] for d in dkvs])
+        for dkv, (_, places) in zip(dkvs, listed):
+            for i in range(MOVING):
+                here = dkv[(GLOB + i) * BLOCK : (GLOB + i + 1) * BLOCK]
+                if i < 3:
+                    acc[pl.ds(places[0][i], BLOCK), :] += here
+                else:
+                    acc[pl.ds(places[0][i], BLOCK), :PAIR] += here[:, :PAIR]
+                    acc[pl.ds(places[1][i], BLOCK), PAIR:] += here[:, PAIR:]
         return carry
 
-    lax.fori_loop(0, row_blocks, one_block, 0, unroll=UNROLL)
+    lax.fori_loop(0, row_blocks // TOGETHER, some_blocks, 0)
     dkv_ref[...] = acc[...].astype(BF16)
     total = jnp.sum(acc[...], axis=0, keepdims=True)
     vsum_ref[0] = jnp.where(low, total[:, :PAIR], total[:, PAIR:])
@@ -392,16 +406,15 @@
     return root * (grad - mean - normed * jnp.mean(grad * normed, axis=1, keepdims=True))
 
 
-def expand_piece(ref, piece):
+def both_pieces(ref, core, columns):
     half = ref.shape[3] // 2
-    blocks = []
-    for part in range(ref.shape[1]):
-        blocks += [ref[piece, part, :, :half], ref[piece, part, :, half:]]
-    return jnp.concatenate(blocks, axis=0)
-
-
-def contract_piece(ref, piece):
-    return jnp.concatenate([ref[piece, part] for part in range(ref.shape[1])], axis=0)
+    pieces = []
+    for piece in (core, 1 - core):
+        blocks = [ref[piece, part] for part in range(ref.shape[1])]
+        if columns:
+            blocks = [b for block in blocks for b in (block[:, :half], block[:, half:])]
+        pieces.append(jnp.concatenate(blocks, axis=0))
+    return jnp.concatenate(pieces, axis=1 if columns else 0)
 
 
 def layer_kernel(
@@ -452,17 +465,17 @@
 
     @pl.when(step < 4)
     def _():
-        for i, piece in enumerate((core, 1 - core)):
-            u = dot(low_ref[...], expand_piece(we_ref, piece)) + be_ref[piece]
-            square = u * u
-            t = jnp.tanh(SLOPE * u * (1.0 + CUBIC * square))
-            half = 0.5 * (1.0 + t)
-            hidden = (u * half).astype(BF16)
-            slope_ref[step, i] = half + (0.5 * SLOPE) * u * (1.0 - t * t) * (
-                1.0 + (3.0 * CUBIC) * square
-            )
-            hid_ref[step, i] = hidden
-            acc_ref[...] += dot(hidden, contract_piece(wc_ref, piece))
+        bias = jnp.concatenate([be_ref[core], be_ref[1 - core]], axis=1)
+        u = dot(low_ref[...], both_pieces(we_ref, core, True)) + bias
+        square = u * u
+        t = jnp.tanh(SLOPE * u * (1.0 + CUBIC * square))
+        half = 0.5 * (1.0 + t)
+        hidden = (u * half).astype(BF16)
+        slope_ref[step] = half + (0.5 * SLOPE) * u * (1.0 - t * t) * (
+            1.0 + (3.0 * CUBIC) * square
+        )
+        hid_ref[step] = hidden
+        acc_ref[...] += dot(hidden, both_pieces(wc_ref, core, False))
 
     @pl.when(step == 4)
     def _():
@@ -480,14 +493,16 @@
     @pl.when(step >= 4)
     def _():
         at = step - 4
-        for i, (piece, c_ref, e_ref) in enumerate(
-            ((core, ck_ref, ek_ref), (1 - core, ca_ref, ea_ref))
-        ):
-            c_ref[0] = t_dot(hid_ref[at, i], two_ref[...]).astype(BF16)
-            grad = (dot_t(two_ref[...], contract_piece(wc_ref, piece)) * slope_ref[at, i]).astype(BF16)
-            e_ref[0] = t_dot(low_ref[...], grad).astype(BF16)
-            beg_ref[piece] = jnp.sum(grad.astype(F32), axis=0, keepdims=True)
-            acc_ref[...] += dot_t(grad, expand_piece(we_ref, piece))
+        piece = ck_ref.shape[1]
+        grad = t_dot(hid_ref[at], two_ref[...]).astype(BF16)
+        ck_ref[0], ca_ref[0] = grad[:piece], grad[piece:]
+        grad = dot_t(two_ref[...], both_pieces(wc_ref, core, False)) * slope_ref[at]
+        grad = grad.astype(BF16)
+        total = jnp.sum(grad.astype(F32), axis=0, keepdims=True)
+        beg_ref[core], beg_ref[1 - core] = total[:, :piece], total[:, piece:]
+        acc_ref[...] += dot_t(grad, both_pieces(we_ref, core, True))
+        grad = t_dot(low_ref[...], grad).astype(BF16)
+        ek_ref[0], ea_ref[0] = grad[:, :piece], grad[:, piece:]
 
     @pl.when(step == 7)
     def _():
@@ -547,8 +562,8 @@
                 pltpu.VMEM((rows, width), F32),
                 pltpu.VMEM((rows, 1), F32),
                 pltpu.VMEM((rows, width), BF16),
-                pltpu.VMEM((steps, 2, rows, piece), F32),
-                pltpu.VMEM((steps, 2, rows, piece), BF16),
+                pltpu.VMEM((steps, rows, 2 * piece), F32),
+                pltpu.VMEM((steps, rows, 2 * piece), BF16),
                 pltpu.VMEM((rows, width), F32),
                 pltpu.VMEM((rows, width), BF16),
             ],
@@ -584,16 +599,13 @@
 
 
 def pair_sum(grad_refs, weight_refs, columns, at):
-    total = None
-    for (group, offset, count), ref in zip(BACK, grad_refs):
-        for pair in range(count):
-            start = 3 * PAIR * (offset + pair) + at
-            term = dot_t(
-                ref[:, pair * columns : (pair + 1) * columns],
-                weight_refs[group][:, start : start + columns],
-            )
-            total = term if total is None else total + term
-    return total
+    grads = jnp.concatenate([ref[...] for ref in grad_refs], axis=1)
+    weights = []
+    for group, offset, count in BACK:
+        for pair in range(offset, offset + count):
+            start = 3 * PAIR * pair + at
+            weights.append(weight_refs[group][:, start : start + columns])
+    return dot_t(grads, jnp.concatenate(weights, axis=1))
 
 
 def token_kernel(me, *refs, away, extra, count):
@@ -604,7 +616,7 @@
     half = dkv_refs[0].shape[0] // 2
     if away:
         dq_refs, one_ref = refs[sides + 2 : 2 * sides + 2], refs[2 * sides + 2]
-        above_ref, below_ref, share_ref = refs[-3:]
+        out_ref, share_ref = refs[-2:]
 
         @pl.when(step == 0)
         def _():
@@ -612,15 +624,15 @@
 
         share = lambda: share_ref[2 * half : 2 * half + extra, :]
     else:
-        share_ref, above_ref, below_ref = refs[sides + 2], *refs[-2:]
+        share_ref, out_ref = refs[sides + 2], refs[-1]
         share = lambda: share_ref[...]
     total = pair_sum(dkv_refs, w_refs, 2 * PAIR, PAIR).astype(BF16)
-    above_ref[0], below_ref[0] = total[:half], total[half:]
+    out_ref[0, 0], out_ref[1, 0] = total[:half], total[half:]
 
     @pl.when((piece == c) & (c < count))
     def _():
         at = pl.ds(pl.multiple_of(c * extra, extra), extra)
-        above_ref[0, at, :] = (above_ref[0, at, :].astype(F32) + share()).astype(BF16)
+        out_ref[0, 0, at, :] = (out_ref[0, 0, at, :].astype(F32) + share()).astype(BF16)
 
 
 def token_share(c, dkvs, weights, more, away, waits, rows, extra, count):
@@ -628,8 +640,8 @@
     chips = seq // rows // 2
     other = 1 if away else 0
     full = lambda a: pl.BlockSpec(a.shape, lambda j, me: (0,) * a.ndim)
-    out_specs = [pl.BlockSpec((1, rows // 2, width), lambda j, me: (j, 0, 0))] * 2
-    out_shape = [jax.ShapeDtypeStruct((chips, rows // 2, width), BF16)] * 2
+    out_specs = [pl.BlockSpec((2, 1, rows // 2, width), lambda j, me: (0, j, 0, 0))]
+    out_shape = [jax.ShapeDtypeStruct((2, chips, rows // 2, width), BF16)]
     if away:
         out_specs.append(pl.BlockSpec((rows + extra, width), lambda j, me: (0, 0)))
         out_shape.append(jax.ShapeDtypeStruct((rows + extra, width), F32))
@@ -747,19 +759,90 @@
     return jnp.transpose(added(near, came), (1, 0, 2, 3)).reshape(parts * PIECES // 2, -1, columns)
 
 
-def rows_sum(sums):
+def rows_send(sums):
     shards, parts = lax.axis_size("ctx"), lax.axis_size("wt")
     sums = far_sum(sums, shards)
     groups = [[i * parts + w for i in g for w in range(parts)] for g in same_core(shards, PIECES)]
-    sums = lax.all_to_all(
+    return lax.all_to_all(
         sums, ("ctx", "wt"), split_axis=0, concat_axis=0, axis_index_groups=groups, tiled=True
     )
+
+
+def rows_add(sums):
     return jnp.sum(sums.astype(F32), axis=0).astype(BF16)
+
+
+def rows_sum(sums):
+    return rows_add(rows_send(sums))
 
 
 def ordered(value, source):
     rows = jnp.arange(value.shape[1], dtype=jnp.int32)
     return dot(value, (rows[:, None] == source[None, :]).astype(BF16))
+
+
+def start_kernel(me, q_ref, k_ref, v_ref, o_ref, e_ref, c_ref, *rest, parts):
+    vectors, (lead_ref, more_ref) = rest[:-2], rest[-2:]
+    c = me[0]
+    half, width = lead_ref.shape[0] - 8, lead_ref.shape[1]
+    piece = c % PIECES
+    own = pl.ds(pl.multiple_of(c % 2 * half, 16), half)
+    low = lax.broadcasted_iota(jnp.int32, (1, PAIR), 1) < HD
+    flip = lambda a: jnp.concatenate([a[:, HD:], a[:, :HD]], axis=1)
+    columns = []
+    for pair in range(PAIRS):
+        at = slice(pair * PAIR, (pair + 1) * PAIR)
+        q, k, v = (ref[own, at].astype(F32) for ref in (q_ref, k_ref, v_ref))
+        k = flip(k)
+        columns += [flip(q), jnp.where(low, v, k), jnp.where(low, k, v)]
+    ahead = 3 * AHEAD
+    small = [r[...].astype(F32).reshape(1, -1) for r in vectors]
+    some = [jnp.concatenate(small[i : i + parts], axis=1) for i in range(0, 2 * parts, parts)]
+    some += small[2 * parts :]
+    small = jnp.concatenate(some + [jnp.zeros((8 - len(some), width), F32)], axis=0)
+    lead = jnp.concatenate([jnp.concatenate(columns[:ahead], axis=1), small], axis=0)
+    lead_ref[...] = lead.astype(BF16)
+
+    run = e_ref.shape[1] // parts // PIECES
+    block = e_ref.shape[1] // parts
+    runs = []
+    for part in range(parts):
+        here = e_ref[:, part * block : (part + 1) * block].astype(F32)
+        runs.append(pltpu.roll(here, block - piece * run, 1)[:, :run])
+    runs = jnp.concatenate(runs, axis=1)
+    count = runs.shape[0] // 2
+    more_ref[:count] = jnp.concatenate([runs[:count], runs[count:]], axis=1).astype(BF16)
+    rows = c_ref.shape[0] // PIECES
+    more_ref[count : count + rows] = c_ref[pl.ds(pl.multiple_of(piece * rows, 16), rows), :]
+    at = count + rows
+    left = (PAIRS - AHEAD) * 3 * PAIR // width
+    for i in range(left):
+        some = columns[ahead + i * width // PAIR : ahead + (i + 1) * width // PAIR]
+        more_ref[at : at + half] = jnp.concatenate(some, axis=1).astype(BF16)
+        at += half
+    rows = o_ref.shape[0] // PIECES
+    whole = o_ref[...].astype(F32)
+    turned = pltpu.roll(whole, whole.shape[0] - piece * rows, 0)
+    more_ref[at:] = turned[: more_ref.shape[0] - at].astype(BF16)
+
+
+def start_arrays(c, weights, vectors, parts):
+    half, width = weights[0].shape[0] // 2, weights[0].shape[1]
+    count = weights[4].shape[0] // 2 + weights[5].shape[0] // PIECES
+    count += (PAIRS - AHEAD) * 3 * PAIR // width * half
+    count += -(-weights[3].shape[0] // PIECES // 16) * 16
+    full = lambda shape: pl.BlockSpec(shape, lambda i: (0,) * len(shape))
+    shapes = [(half + 8, width), (count, width)]
+    return pl.pallas_call(
+        partial(start_kernel, parts=parts),
+        grid=(1,),
+        in_specs=[pl.BlockSpec(memory_space=pltpu.SMEM)] + [full(a.shape) for a in (*weights, *vectors)],
+        out_specs=[full(shape) for shape in shapes],
+        out_shape=[jax.ShapeDtypeStruct(shape, BF16) for shape in shapes],
+        compiler_params=pltpu.CompilerParams(vmem_limit_bytes=60 * MIB),
+        cost_estimate=taking(3),
+        name="start_arrays",
+    )(jnp.reshape(c, (1,)).astype(jnp.int32), *weights, *vectors)
 
 
 def vector_kernel(*refs, parts):
@@ -854,8 +937,11 @@
     inputs = tokens[0]
 
     pieces = token_gather(inputs)
-    small = jnp.concatenate(
-        [
+    half = part // 2
+    leading, behind = start_arrays(
+        c,
+        (query_weight, key_weight, value_weight, output_weight, expand_weight, contract_weight),
+        (
             query_bias,
             value_bias,
             output_bias,
@@ -865,50 +951,34 @@
             ffn_gain,
             ffn_shift,
             expand_bias,
-        ]
-    )
-    half = part // 2
-    bundles = [
-        lax.dynamic_slice_in_dim(w, own_bit(1) * half, half, 0)
-        for w in (query_weight, key_weight, value_weight)
-    ]
-    bundles = by_pair(*bundles)
-    ahead = AHEAD * 3 * PAIR
-    small_rows = 8 * (-(-small.shape[0] // (8 * ahead)))
-    padded = jnp.pad(small, (0, small_rows * ahead - small.shape[0])).reshape(small_rows, ahead)
-    early_lead = line_step(jnp.concatenate([bundles[:, :ahead], padded], axis=0)[None], 1)
-    leading = line_gather(early_lead, 2)
-    vectors = leading[:, half:].reshape(parts, -1)[:, : small.shape[0]]
+        ),
+        parts,
+    )
+    early_lead = line_step(leading[None], 1)
+    leading = line_gather(after(early_lead, pieces[2], pieces[4]), 2)
+    vectors = leading[:, half:].reshape(parts, -1)
     leading = leading[:, :half]
 
     def joined(bundle):
         return jnp.transpose(doubled(bundle, 1), (1, 0, 2, 3)).reshape(width, -1)
 
     weights = [joined(leading)]
-    behind = bundles[:, ahead:]
-    behind = jnp.concatenate([behind[:, :width], behind[:, width:]], axis=0)
     each = width // parts
     b_query, b_value, b_output, b_contract, g_attn, s_attn, g_ffn, s_ffn = (
         vectors[:, i * each : (i + 1) * each].reshape(-1).astype(F32) for i in range(8)
     )
-    b_expand = vectors[:, 8 * each :].reshape(parts, PIECES, -1)
+    b_expand = vectors[:, 8 * each : 8 * each + hidden_width // parts].reshape(parts, PIECES, -1)
     b_expand = jnp.transpose(b_expand, (1, 0, 2)).reshape(PIECES, 1, piece).astype(F32)
 
-    p = c % PIECES
     each_piece = piece // parts
-    e_piece = lax.dynamic_index_in_dim(
-        expand_weight.reshape(part, parts, PIECES, -1), p, 2, keepdims=False
-    ).reshape(part, piece)
-    e_piece = jnp.concatenate([e_piece[:each_piece], e_piece[each_piece:]], axis=1)
-    c_piece = lax.dynamic_slice_in_dim(contract_weight, p * each_piece, each_piece, 0)
     o_rows = part // PIECES
-    o_piece = lax.dynamic_slice_in_dim(output_weight, p * o_rows, o_rows, 0)
-    w_hidden = jnp.concatenate([e_piece, c_piece, o_piece, behind], axis=0)
-    w_hidden = after(w_hidden, pieces[1])
-    w_hidden = lax.all_gather(w_hidden, "wt")
-    mixed = 2 * each_piece + o_rows
-    following = w_hidden[:, mixed:].reshape(parts, 2, half, width)
+    mixed = 2 * each_piece
+    w_hidden = lax.all_gather(behind, "wt")
+    following = w_hidden[:, mixed : mixed + 2 * half].reshape(parts, 2, half, width)
     following = jnp.concatenate([following[:, 0], following[:, 1]], axis=2)
+    w_hidden = jnp.concatenate(
+        [w_hidden[:, :mixed], w_hidden[:, mixed + 2 * half : mixed + 2 * half + o_rows]], axis=1
+    )
 
     start = jnp.minimum(c * extra, global_count - extra)
     more = lax.dynamic_slice_in_dim(pieces[0], start, extra, 0)
@@ -936,7 +1006,7 @@
 
     given = jnp.where(c == 0, cotangent[0, :global_count], jnp.zeros((), BF16))
     given = jnp.pad(given, ((0, shards * extra - global_count), (0, 0)))
-    given = given.reshape(shards, extra, width)
+    given = after(given.reshape(shards, extra, width), pieces[4])
     given = lax.all_to_all(given, "ctx", split_axis=0, concat_axis=0, tiled=True)
     cot = jnp.concatenate([cotangent[0], given[0]], axis=0)
     cot = jnp.where(usable, cot, jnp.zeros((), BF16))
@@ -947,7 +1017,7 @@
     vectors = jnp.stack([b_output, g_attn, s_attn, b_contract, g_ffn, s_ffn, zero, zero])
     keep = usable.astype(F32)
     w_hidden = after(
-        w_hidden[:, :mixed], *pieces, weights[0], cot, starts, limits, b_qkv, vectors, b_expand, keep, x
+        w_hidden, *pieces, weights[0], cot, starts, limits, b_qkv, vectors, b_expand, keep, x
     )
     w_hidden = lax.all_gather(w_hidden, "ctx", axis_index_groups=groups_of(shards))
     w_output = jnp.transpose(w_hidden[:, :, 2 * each_piece :], (1, 0, 2, 3)).reshape(width, width)
@@ -1031,32 +1101,55 @@
     both = lax.all_to_all(hidden_sums, "wt", split_axis=0, concat_axis=0, tiled=True)
     backs.append(attention_back(3, hidden_sums, middle))
 
+    small = vector_rows([b[4] for b in backs], [b[5] for b in backs], vector_grads, expand_bgrad, backs[3][0], parts)
+    small = small.reshape(parts, 2, -1, width)
+    near = jnp.concatenate([backs[2][2], backs[3][2]], axis=1).reshape(parts, PIECES // 2, -1, width)
+    near = jnp.concatenate(
+        [near, lax.dynamic_index_in_dim(small, own_bit(1), 1, keepdims=False)[:, :, None]], axis=2
+    )
+    far = jnp.concatenate([backs[2][3], backs[3][3]], axis=1).reshape(parts, PIECES // 2, -1, width)
+    far = jnp.concatenate(
+        [far, lax.dynamic_index_in_dim(small, 1 - own_bit(1), 1, keepdims=False)[:, :, None]], axis=2
+    )
+    late = rows_start(near.reshape(-1, width), swapped(far, 1))
+
     share = partial(token_share, c, [b[1] for b in backs], weights)
     count = global_count // extra
-    above_away, below_away, own = share(
-        [b[0] for b in backs] + [grad_one], True, (both,), rows, extra, count
-    )
-    both = jnp.sum(both.astype(F32), axis=0).astype(BF16)
+    away, own = share(
+        [b[0] for b in backs] + [grad_one], True, (late,), rows, extra, count
+    )
+    both = jnp.sum(after(both, away).astype(F32), axis=0).astype(BF16)
     both = jnp.concatenate([both, early, middle, layer_out[rows:]], axis=0)
-    above, below = share([own[rows:]], False, (above_away, both), rows, extra, count)
-
-    def by_chip(keep, came):
-        chips = shards // 2
-        if chips > 4:
-            keep = added(keep, came)
-            while chips > 4:
-                keep = added(keep[: chips // 2], swapped(keep[chips // 2 :], chips))
-                chips //= 2
-            came = jnp.zeros_like(keep)
-        return [a.reshape(2, 2, rows // 2, width) for a in (keep, came)]
-
-    above = by_chip(above, swapped(above_away, 1))
-    below = by_chip(below, swapped(below_away, 1))
+    (keep,) = share([own[rows:]], False, (away, both, late), rows, extra, count)
+    late = rows_send(late)
+    came = swapped(away, 1)
+    chips = shards // 2
+    if chips > 4:
+        keep = added(keep, came)
+        while chips > 4:
+            keep = added(keep[:, : chips // 2], swapped(keep[:, chips // 2 :], chips))
+            chips //= 2
+        came = jnp.zeros_like(keep)
+    keep, came = (a.reshape(2, 2, 2, rows // 2, width) for a in (keep, came))
+    above, below = (keep[0], came[0]), (keep[1], came[1])
     above_sent = added(above[0][:, 1], above[1][:, 1])
     below_sent = added(below[0][1], below[1][1])
+    late = rows_add(after(late, above_sent, below_sent))
     above_came, below_came = swapped(above_sent, 2), swapped(below_sent, 4)
     above = added(above[0][:, 0], above[1][:, 0])
     below = added(below[0][0], below[1][0])
+    rows_late = late.shape[0]
+    late = jnp.pad(late, ((0, -rows_late % 8), (0, 0)))
+    late = doubled(late, 1)
+    late = doubled(late, 2).reshape(4, -1, width)
+
+    def carried(sent, more, bit):
+        count = sent.shape[0]
+        flat = swapped(jnp.concatenate([sent, more.reshape(-1, width)], axis=0), bit)
+        other = flat[count:].reshape(more.shape)
+        mine = own_bit(bit) == 0
+        more = jnp.concatenate([jnp.where(mine, more, other), jnp.where(mine, other, more)])
+        return flat[:count], more
 
     hidden_rows = 2 * each_piece
     gathered = lax.all_gather(both, "ctx", axis_index_groups=groups_of(shards))
@@ -1071,27 +1164,15 @@
     above_came = after(above_came, contract_wgrad, expand_wgrad, layer_out)
     below_came = after(below_came, contract_wgrad, expand_wgrad, layer_out)
 
-    small = vector_rows([b[4] for b in backs], [b[5] for b in backs], vector_grads, expand_bgrad, above_sent, parts)
-    small = small.reshape(parts, 2, -1, width)
-    near = jnp.concatenate([backs[2][2], backs[3][2]], axis=1).reshape(parts, PIECES // 2, -1, width)
-    near = jnp.concatenate(
-        [near, lax.dynamic_index_in_dim(small, own_bit(1), 1, keepdims=False)[:, :, None]], axis=2
-    )
-    far = jnp.concatenate([backs[2][3], backs[3][3]], axis=1).reshape(parts, PIECES // 2, -1, width)
-    far = jnp.concatenate(
-        [far, lax.dynamic_index_in_dim(small, 1 - own_bit(1), 1, keepdims=False)[:, :, None]], axis=2
-    )
-    late = rows_start(near.reshape(-1, width), swapped(far, 1))
-    late = rows_sum(late)
-
     above_sent = added(above[1], above_came[1])
     below_sent = added(below[1], below_came[1])
-    above_last, below_last = swapped(above_sent, 4), swapped(below_sent, 2)
+    above_last, late = carried(above_sent, late, 4)
+    below_last = swapped(below_sent, 2)
+    late = late[:, : rows_late]
     above = above[0].astype(F32) + above_came[0].astype(F32) + above_last.astype(F32)
     below = below[0].astype(F32) + below_came[0].astype(F32) + below_last.astype(F32)
     input_grad = own[:rows] + jnp.concatenate([above, below], axis=0)
 
-    late = plane_gather(after(late, above_sent, below_sent))
     kinds = [gathered[:, hidden_rows:-extra].reshape(PIECES, 3, -1, width)]
     kinds.append(late[:, None, :-1])
     mine = jnp.concatenate(kinds, axis=1).reshape(PIECES // 2, 2, 4, -1, width)

time: 473 us -> 431 us (0.911)
  Pallas kernels: 195 us -> 171 us
  waiting for transfers between devices: 109 us -> 87.9 us
    pallas_call x2, Pallas kernels: 62.6 us -> 43.2 us  [attention_forward(): pl.pallas_call(partial(forward_kernel, first=first, row_blocks=row_blocks...]
    all_gather x1, waiting for transfers between devices: 0.01 us -> 18 us  [body(): lax.all_gather(w_hidden, 'ctx', axis_index_groups=groups_of(shards))]
    ppermute x29 -> x27, waiting for transfers between devices: 48.6 us -> 31.5 us  [swapped(): return lax.ppermute(value, 'ctx', [(i, i ^ bit) for i in range(shards)])]
    all_to_all x1, waiting for transfers between devices: 11.8 us -> 0.01 us  [body(): lax.all_to_all(hidden_sums, 'wt', split_axis=0, concat_axis=0, tiled=True)]
    all_to_all x3, waiting for transfers between devices: 16.1 us -> 4.85 us  [rows_send(): lax.all_to_all(sums, ('ctx', 'wt'), split_axis=0, concat_axis=0, axis_ind...]
    unnamed x93 -> x84, local copies, waits for them, and re-layouts: 4.41 us -> 12.6 us
    all_gather x1, waiting for transfers between devices: 0.01 us -> 6.01 us  [body(): gathered = lax.all_gather(both, 'ctx', axis_index_groups=groups_of(shards))]
    ppermute x2, waiting for transfers between devices: 32.6 us -> 27.5 us  [line_step(): other = lax.ppermute(value, 'wt', [(i, i ^ bit) for i in range(parts)])]
  transfers between devices with their start and end apart: 39 -> 37, of which waited for: 13 -> 14; matrix products, arithmetic and copies ran while one was open for 17% -> 15% of each run, Pallas kernels for 33% -> 32%
where the time goes in v3:
time: 431 us; the launch traced here: 424 us
  Pallas kernels  171 us (40%)
  waiting for transfers between devices  87.9 us (20%)
  other arithmetic  55.6 us (13%)
  starting transfers between devices  52.7 us (12%)
  local copies, waits for them, and re-layouts  38.4 us (9%)
  between operations  15.9 us (4%)
    pallas_call x4, Pallas kernels, attention_backward(): pl.pallas_call(partial(backward_kernel, first=first, row_blocks=row_block...  66.9 us
    pallas_call x2, Pallas kernels, attention_forward(): pl.pallas_call(partial(forward_kernel, first=first, row_blocks=row_blocks...  43.2 us
    pallas_call x1, Pallas kernels, layer(): pl.pallas_call(layer_kernel, grid_spec=pltpu.PrefetchScalarGridSpec(num_s...  34.7 us
    ppermute x27, waiting for transfers between devices, swapped(): return lax.ppermute(value, 'ctx', [(i, i ^ bit) for i in range(shards)])  31.5 us
    ppermute x2, waiting for transfers between devices, line_step(): other = lax.ppermute(value, 'wt', [(i, i ^ bit) for i in range(parts)])  27.5 us
    ppermute x27, starting transfers between devices, swapped(): return lax.ppermute(value, 'ctx', [(i, i ^ bit) for i in range(shards)])  22.4 us
    convert_element_type x13, other arithmetic, added(): return (keep.astype(F32) + came.astype(F32)).astype(BF16)  21.2 us
    pallas_call x2, Pallas kernels, token_share(): pl.pallas_call(partial(token_kernel, away=away, extra=extra, count=count)...  19.1 us
  transfers between devices with their start and end apart: 37, of which 14 were waited for; matrix products, arithmetic and copies ran while one was open for 15% of the time, Pallas kernels for 32%

profile of v3, /device:TPU:0, one launch (start us, length us, event | category | flops | bytes accessed | tf_op | source)
XLA Modules:
  0.0 424.5 jit_solution(1153495907261529814)
XLA Ops:
  7.2 3.0 collective-permute-start
  11.8 3.7 start_arrays.1
  22.7 5.3 %collective-permute-done.refs_2_.refs_1_.rest_4_.refs_5_ = bf16[512,768]{1,0:T(8,128)(2,1)S(1)} collective-permute-done((bf16[512,768]{1,0:T(8,128)(2,1)}, bf16[512,768]{1,0:T(8,128)(2,1)S(1)}, u32[]{:S(2)}, u32[]{:S(2)}) %collective-permute-start) | collective-permute-done | bytes 786464 | tf_op jit(solution)/shard_map/ppermute | solution.py:686
  28.9 4.0 all-to-all-start
  34.7 2.8 collective-permute-start.9
  45.3 27.5 %collective-permute-done.9 = bf16[2,104,768]{2,1,0:T(8,128)(2,1)S(1)} collective-permute-done((bf16[2,104,768]{2,1,0:T(8,128)(2,1)}, bf16[2,104,768]{2,1,0:T(8,128)(2,1)S(1)}, u32[]{:S(2)}, u32[]{:S(2)}) %collective-permute-start.9) | collective-permute-done | bytes 319520 | tf_op jit(solution)/shard_map/ppermute | solution.py:720
  88.6 16.3 %attention_forward.2 = (bf16[528,256]{1,0:T(8,128)(2,1)}, bf16[4096,512]{1,0:T(8,128)(2,1)}, bf16[528,256]{1,0:T(8,128)(2,1)}, bf16[8,2,512,128]{3,2,1,0:T(8,128)(2,1)}, bf16[2,4096,32]{2,1,0:T(8,128)(2,1)}) custom-call(s32[578]{0:T(1024)} %pad_add_fusion.1.starts.refs_11_, s32[584]{0:T(1024)} %pad_add_fusion.2.limits.refs_12_, ...), custom_call_target="tpu_custom_call" | custom-call | flops 20000000000 | bytes 1000000 | tf_op jit(solution)/shard_map/attention_forward/pallas_call | solution.py:303
  107.0 26.9 %attention_forward.3 = (bf16[528,512]{1,0:T(8,128)(2,1)}, bf16[4096,1024]{1,0:T(8,128)(2,1)}, bf16[528,512]{1,0:T(8,128)(2,1)}, bf16[8,4,512,128]{3,2,1,0:T(8,128)(2,1)}, bf16[4,4096,32]{2,1,0:T(8,128)(2,1)}) custom-call(s32[578]{0:T(1024)} %pad_add_fusion.1.starts.refs_11_, s32[584]{0:T(1024)} %pad_add_fusion.2.limits.refs_12_, ...), custom_call_target="tpu_custom_call" | custom-call | flops 40000000000 | bytes 1000000 | tf_op jit(solution)/shard_map/attention_forward/pallas_call | solution.py:303
  133.9 18.0 %all-gather.9.cloned.1.call-done = bf16[32,216,768]{2,1,0:T(8,128)(2,1)} async-done(((bf16[4,216,768]{2,1,0:T(8,128)(2,1)}), bf16[32,216,768]{2,1,0:T(8,128)(2,1)}) %all-gather.9.cloned.1.call-update) | async-done | bytes 10616848 | tf_op jit(solution)/shard_map/all_gather | solution.py:1022
  154.3 34.7 %layer.1 = (bf16[528,768]{1,0:T(8,128)(2,1)}, f32[528,768]{1,0:T(8,128)}, bf16[528,768]{1,0:T(8,128)(2,1)}, bf16[384,768]{1,0:T(8,128)(2,1)}, bf16[384,768]{1,0:...) custom-call(s32[1]{0:T(128)} %bitcast.me, ...), custom_call_target="tpu_custom_call" | custom-call | flops 35000000512 | bytes 1000000 | tf_op jit(solution)/shard_map/layer/pallas_call | solution.py:532
  189.8 20.8 %attention_backward.4 = (bf16[528,256]{1,0:T(8,128)(2,1)}, bf16[4096,512]{1,0:T(8,128)(2,1)}, bf16[384,768]{1,0:T(8,128)(2,1)}, bf16[384,768]{1,0:T(8,128)(2,1)}...) custom-call(s32[578]{0:T(1024)} %pad_add_fusion.1.starts.refs_11_, bf16[528,768]{1,0:T(8,128)(2,1)} %pad_maximum_fusion.4.x_ref.refs_17_, ...), custom_call_target="tpu_custom_call" | custom-call | flops 8000000000 | bytes 1000000 | tf_op jit(solution)/shard_map/attention_backward/pallas_call | solution.py:351
  214.3 5.8 %all-to-all-start.2 = ((bf16[16,48,768]{2,1,0:T(8,128)(2,1)}), bf16[16,48,768]{2,1,0:T(8,128)(2,1)S(1)}, u32[]{:S(2)}, u32[]{:S(2)}) async-start(bf16[16,48,768]{2,1,0:T(8,128)(2,1)} %pad_maximum_fusion.3.rest_10_), calls=%async_computation.2 | async-start | bytes 2359296 | tf_op jit(solution)/shard_map/all_to_all | solution.py:766
  221.6 4.0 add_convert_fusion.3
  227.7 3.2 add_convert_fusion.1
  232.4 20.3 %attention_backward.5 = (bf16[528,256]{1,0:T(8,128)(2,1)}, bf16[4096,512]{1,0:T(8,128)(2,1)}, bf16[384,768]{1,0:T(8,128)(2,1)}, bf16[384,768]{1,0:T(8,128)(2,1)}...) custom-call(s32[578]{0:T(1024)} %pad_add_fusion.1.starts.refs_11_, bf16[528,768]{1,0:T(8,128)(2,1)} %pad_maximum_fusion.4.x_ref.refs_17_, ...), custom_call_target="tpu_custom_call" | custom-call | flops 8000000000 | bytes 1000000 | tf_op jit(solution)/shard_map/attention_backward/pallas_call | solution.py:351
  257.3 4.9 %all-to-all-start.3 = ((bf16[16,24,768]{2,1,0:T(8,128)(2,1)}), bf16[16,24,768]{2,1,0:T(8,128)(2,1)S(1)}, u32[]{:S(2)}, u32[]{:S(2)}) async-start(bf16[16,24,768]{2,1,0:T(8,128)(2,1)} %bitcast.50.rest_11_), calls=%async_computation.3 | async-start | bytes 1179648 | tf_op jit(solution)/shard_map/all_to_all | solution.py:766
  263.4 2.1 collective-permute-start.14
  265.5 2.0 fusion.27.rest_9_
  268.9 12.9 %attention_backward.6 = (bf16[528,128]{1,0:T(8,128)(2,1)}, bf16[4096,256]{1,0:T(8,128)(2,1)}, bf16[384,384]{1,0:T(8,128)(2,1)}, bf16[384,384]{1,0:T(8,128)(2,1)}...) custom-call(s32[578]{0:T(1024)} %pad_add_fusion.1.starts.refs_11_, bf16[528,768]{1,0:T(8,128)(2,1)} %pad_maximum_fusion.4.x_ref.refs_17_, ...), custom_call_target="tpu_custom_call" | custom-call | flops 8000000000 | bytes 1000000 | tf_op jit(solution)/shard_map/attention_backward/pallas_call | solution.py:351
  282.5 2.4 collective-permute-done.17
  289.0 4.3 %all-to-all-start.1 = ((bf16[4,192,768]{2,1,0:T(8,128)(2,1)}), bf16[4,192,768]{2,1,0:T(8,128)(2,1)S(1)}, u32[]{:S(2)}, u32[]{:S(2)}) async-start(bf16[4,192,768]{2,1,0:T(8,128)(2,1)} %maximum_maximum_fusion.rest_8_), calls=%async_computation.1 | async-start | bytes 2359296 | tf_op jit(solution)/shard_map/all_to_all | solution.py:1101
  293.6 12.9 %attention_backward.7 = (bf16[528,128]{1,0:T(8,128)(2,1)}, bf16[4096,256]{1,0:T(8,128)(2,1)}, bf16[384,384]{1,0:T(8,128)(2,1)}, bf16[384,384]{1,0:T(8,128)(2,1)}...) custom-call(s32[578]{0:T(1024)} %pad_add_fusion.1.starts.refs_11_, bf16[528,768]{1,0:T(8,128)(2,1)} %pad_maximum_fusion.4.x_ref.refs_17_, ...), custom_call_target="tpu_custom_call" | custom-call | flops 20000000000 | bytes 1000000 | tf_op jit(solution)/shard_map/attention_backward/pallas_call | solution.py:351
  315.0 10.1 %token_share.2 = (bf16[2,4,256,768]{3,2,1,0:T(8,128)(2,1)}, f32[528,768]{1,0:T(8,128)S(1)}) custom-call(s32[1]{0:T(128)} %bitcast.me, bf16[4096,512]{1,0:T(8,128)(2,1)} %get-tuple-element.79.refs_0_, bf16[4096,512]{1,0:T(8,128)(2,1)} %get-tuple-element.88.refs_1_, bf16[4096,256]{1,0:T(8,128)(2,1)} %get-tuple-element.91.refs_2_, ...), custom_call_target="tpu_custom_call" | custom-call | flops 3000000000 | bytes 1000000 | tf_op jit(solution)/shard_map/token_share/pallas_call | solution.py:648
  329.9 6.6 %all-to-all-start.4 = ((bf16[16,25,768]{2,1,0:T(8,128)(2,1)}), bf16[16,25,768]{2,1,0:T(8,128)(2,1)}, u32[]{:S(2)}, u32[]{:S(2)}) async-start(bf16[16,25,768]{2,1,0:T(8,128)(2,1)} %bitcast.60.refs_11_.refs_9_), calls=%async_computation.4 | async-start | bytes 1572864 | tf_op jit(solution)/shard_map/all_to_all | solution.py:766
  338.3 9.0 %token_share.3 = bf16[2,4,256,768]{3,2,1,0:T(8,128)(2,1)} custom-call(s32[1]{0:T(128)} %bitcast.me, bf16[4096,512]{1,0:T(8,128)(2,1)} %get-tuple-element.79.refs_0_, bf16[4096,512]{1,0:T(8,128)(2,1)} %get-tuple-element.88.refs_1_, bf16[4096,256]{1,0:T(8,128)(2,1)S(1)} %copy-done.1, bf16[4096,256]{1,0:T(8,128)(2,1)} %get-tuple-element.92.refs_3_, ...), custom_call_target="tpu_custom_call" | custom-call | flops 3000000000 | bytes 1000000 | tf_op jit(solution)/shard_map/token_share/pallas_call | solution.py:648
  351.3 2.7 add_convert_fusion.4
  354.0 4.8 %all-to-all-done.4.refs_0_ = bf16[16,25,768]{2,1,0:T(8,128)(2,1)} async-done(((bf16[16,25,768]{2,1,0:T(8,128)(2,1)}), bf16[16,25,768]{2,1,0:T(8,128)(2,1)}, u32[]{:S(2)}, u32[]{:S(2)}) %all-to-all-start.4) | async-done | bytes 614432 | tf_op jit(solution)/shard_map/all_to_all | solution.py:766
  364.4 5.0 %collective-permute-done.25 = bf16[2,32,768]{2,1,0:T(8,128)(2,1)S(1)} collective-permute-done((bf16[2,32,768]{2,1,0:T(8,128)(2,1)S(1)}, bf16[2,32,768]{2,1,0:T(8,128)(2,1)S(1)}, u32[]{:S(2)}, u32[]{:S(2)}) %collective-permute-start.25) | collective-permute-done | bytes 98336 | tf_op jit(solution)/shard_map/ppermute | solution.py:686
  369.5 6.0 %all-gather.11.cloned.1.call-done = bf16[2240,768]{1,0:T(8,128)(2,1)} async-done(((bf16[280,768]{1,0:T(8,128)(2,1)}), bf16[2240,768]{1,0:T(8,128)(2,1)}) %all-gather.11.cloned.1.call-update) | async-done | bytes 3440656 | tf_op jit(solution)/shard_map/all_gather | solution.py:1155
  376.4 2.2 slice_select_fusion.refs_3_
  384.3 3.9 collective-permute-done.23.refs_0_
  395.0 8.5 %collective-permute-done.28 = bf16[256,768]{1,0:T(8,128)(2,1)} collective-permute-done((bf16[256,768]{1,0:T(8,128)(2,1)S(1)}, bf16[256,768]{1,0:T(8,128)(2,1)}, u32[]{:S(2)}, u32[]{:S(2)}) %collective-permute-start.28) | collective-permute-done | bytes 393248 | tf_op jit(solution)/shard_map/ppermute | solution.py:686
  (294 shorter events, 111.8 us)
Async XLA Ops:
  7.2 77.0 %all-gather.7.cloned.1.call-start = ((), (), s32[]{:S(2)}) async-start(), calls=%async_computation.5 | async-start | bytes 3194880 | tf_op jit(solution)/shard_map/all_gather | solution.py:976
  7.2 20.8 %collective-permute-start = (bf16[512,768]{1,0:T(8,128)(2,1)}, bf16[512,768]{1,0:T(8,128)(2,1)S(1)}, u32[]{:S(2)}, u32[]{:S(2)}) collective-permute-start(bf16[512,768]{1,0:T(8,128)(2,1)} %bitcast.240), channel_id=1, source_target_pairs={{0,16},{4,20},{8,24},{12,28},{16,0},{20,4},{24,8},{28,12},{1,17},{... | collective-permute-start | bytes 2359304 | tf_op jit(solution)/shard_map/ppermute | solution.py:686
  10.3 23.5 %collective-permute-start.2 = (bf16[512,768]{1,0:T(8,128)(2,1)}, bf16[512,768]{1,0:T(8,128)(2,1)S(1)}, u32[]{:S(2)}, u32[]{:S(2)}) collective-permute-start(bf16[512,768]{1,0:T(8,128)(2,1)} %bitcast.241), channel_id=1, source_target_pairs={{0,8},{4,12},{8,0},{12,4},{16,24},{20,28},{24,16},{28,20},{1,9},{5... | collective-permute-start | bytes 2359304 | tf_op jit(solution)/shard_map/ppermute | solution.py:686
  11.8 70.2 %collective-permute-start.7 = (bf16[512,768]{1,0:T(8,128)(2,1)}, bf16[512,768]{1,0:T(8,128)(2,1)}, u32[]{:S(2)}, u32[]{:S(2)}) collective-permute-start(bf16[512,768]{1,0:T(8,128)(2,1)} %bitcast.242), channel_id=1, source_target_pairs={{0,4},{4,0},{8,12},{12,8},{16,20},{20,16},{24,28},{28,24},{1,5},{5... | collective-permute-start | bytes 2359304 | tf_op jit(solution)/shard_map/ppermute | solution.py:686
  15.5 17.5 %collective-permute-start.8 = (bf16[1,104,768]{2,1,0:T(8,128)(2,1)}, bf16[1,104,768]{2,1,0:T(8,128)(2,1)S(1)}, u32[]{:S(2)}, u32[]{:S(2)}) collective-permute-start(bf16[1,104,768]{2,1,0:T(8,128)(2,1)} %bitcast.280), channel_id=1, source_target_pairs={{0,1},{1,0},{2,3},{3,2},{4,5},{5,4},{6,7},{7,6},{8,9},{9,8},{10,11... | collective-permute-start | bytes 479240 | tf_op jit(solution)/shard_map/ppermute | solution.py:720
  28.9 14.5 %all-to-all-start = ((bf16[8,16,768]{2,1,0:T(8,128)(2,1)}), bf16[8,16,768]{2,1,0:T(8,128)(2,1)}, u32[]{:S(2)}, u32[]{:S(2)}) async-start(bf16[8,16,768]{2,1,0:T(8,128)(2,1)} %after.8), calls=%async_computation | async-start | bytes 393216 | tf_op jit(solution)/shard_map/all_to_all | solution.py:1010
  33.0 118.9 %all-gather.9.cloned.1.call-start = ((), (), s32[]{:S(2)}) async-start(), calls=%async_computation.6 | async-start | bytes 11943936 | tf_op jit(solution)/shard_map/all_gather | solution.py:1022
  34.7 38.1 %collective-permute-start.9 = (bf16[2,104,768]{2,1,0:T(8,128)(2,1)}, bf16[2,104,768]{2,1,0:T(8,128)(2,1)S(1)}, u32[]{:S(2)}, u32[]{:S(2)}) collective-permute-start(bf16[2,104,768]{2,1,0:T(8,128)(2,1)} %after.7), channel_id=1, source_target_pairs={{0,2},{1,3},{2,0},{3,1},{4,6},{5,7},{6,4},{7,5},{8,10},{9,11},{10,... | collective-permute-start | bytes 958472 | tf_op jit(solution)/shard_map/ppermute | solution.py:720
  38.3 36.1 %collective-permute-start.1 = (bf16[256,768]{1,0:T(8,128)(2,1)}, bf16[256,768]{1,0:T(8,128)(2,1)}, u32[]{:S(2)}, u32[]{:S(2)}) collective-permute-start(bf16[256,768]{1,0:T(8,128)(2,1)} %slice.408), channel_id=1, source_target_pairs={{0,8},{4,12},{8,0},{12,4},{16,24},{20,28},{24,16},{28,20},{1,9},{5... | collective-permute-start | bytes 1179656 | tf_op jit(solution)/shard_map/ppermute | solution.py:686
  41.9 34.6 %collective-permute-start.3 = (bf16[256,768]{1,0:T(8,128)(2,1)}, bf16[256,768]{1,0:T(8,128)(2,1)S(1)}, u32[]{:S(2)}, u32[]{:S(2)}) collective-permute-start(bf16[256,768]{1,0:T(8,128)(2,1)} %slice.409), channel_id=1, source_target_pairs={{0,16},{4,20},{8,24},{12,28},{16,0},{20,4},{24,8},{28,12},{1,17},{... | collective-permute-start | bytes 1179656 | tf_op jit(solution)/shard_map/ppermute | solution.py:686
  43.4 38.6 %collective-permute-start.5 = (bf16[512,768]{1,0:T(8,128)(2,1)S(1)}, bf16[512,768]{1,0:T(8,128)(2,1)}, u32[]{:S(2)}, u32[]{:S(2)}) collective-permute-start(bf16[512,768]{1,0:T(8,128)(2,1)S(1)} %copy-done.14), channel_id=1, source_target_pairs={{0,4},{4,0},{8,12},{12,8},{16,20},{20,16},{24,28},{28,24},{1,5},{5... | collective-permute-start | bytes 2359304 | tf_op jit(solution)/shard_map/ppermute | solution.py:686
  72.8 9.2 %collective-permute-start.6 = (bf16[512,768]{1,0:T(8,128)(2,1)S(1)}, bf16[512,768]{1,0:T(8,128)(2,1)}, u32[]{:S(2)}, u32[]{:S(2)}) collective-permute-start(bf16[512,768]{1,0:T(8,128)(2,1)S(1)} %copy-done.16), channel_id=1, source_target_pairs={{0,4},{4,0},{8,12},{12,8},{16,20},{20,16},{24,28},{28,24},{1,5},{5... | collective-permute-start | bytes 2359304 | tf_op jit(solution)/shard_map/ppermute | solution.py:686
  74.4 6.3 %collective-permute-start.10 = (bf16[4,96,768]{2,1,0:T(8,128)(2,1)S(1)}, bf16[4,96,768]{2,1,0:T(8,128)(2,1)S(1)}, u32[]{:S(2)}, u32[]{:S(2)}) collective-permute-start(bf16[4,96,768]{2,1,0:T(8,128)(2,1)S(1)} %fusion.25), channel_id=1, source_target_pairs={{0,4},{4,0},{8,12},{12,8},{16,20},{20,16},{24,28},{28,24},{1,5},{5... | collective-permute-start | bytes 1769480 | tf_op jit(solution)/shard_map/ppermute | solution.py:686
  88.3 16.7 %collective-permute-start.11 = (bf16[4,96,1536]{2,1,0:T(8,128)(2,1)S(1)}, bf16[4,96,1536]{2,1,0:T(8,128)(2,1)S(1)}, u32[]{:S(2)}, u32[]{:S(2)}) collective-permute-start(bf16[4,96,1536]{2,1,0:T(8,128)(2,1)S(1)} %pad_maximum_fusion.2), channel_id=1, source_target_pairs={{0,4},{4,0},{8,12},{12,8},{16,20},{20,16},{24,28},{28,24},{1,5},{5... | collective-permute-start | bytes 3538952 | tf_op jit(solution)/shard_map/ppermute | solution.py:686
  189.0 31.1 %collective-permute-start.12 = (bf16[4,384,768]{2,1,0:T(8,128)(2,1)}, bf16[4,384,768]{2,1,0:T(8,128)(2,1)S(1)}, u32[]{:S(2)}, u32[]{:S(2)}) collective-permute-start(bf16[4,384,768]{2,1,0:T(8,128)(2,1)} %get-tuple-element.71), channel_id=1, source_target_pairs={{0,4},{4,0},{8,12},{12,8},{16,20},{20,16},{24,28},{28,24},{1,5},{5... | collective-permute-start | bytes 7077896 | tf_op jit(solution)/shard_map/ppermute | solution.py:686
  189.3 38.3 %collective-permute-start.15 = (bf16[4,768,384]{2,1,0:T(8,128)(2,1)}, bf16[4,768,384]{2,1,0:T(8,128)(2,1)}, u32[]{:S(2)}, u32[]{:S(2)}) collective-permute-start(bf16[4,768,384]{2,1,0:T(8,128)(2,1)} %get-tuple-element.73), channel_id=1, source_target_pairs={{0,4},{4,0},{8,12},{12,8},{16,20},{20,16},{24,28},{28,24},{1,5},{5... | collective-permute-start | bytes 7077896 | tf_op jit(solution)/shard_map/ppermute | solution.py:686
  189.6 21.4 %collective-permute-start.18 = (bf16[384,768]{1,0:T(8,128)(2,1)}, bf16[384,768]{1,0:T(8,128)(2,1)S(1)}, u32[]{:S(2)}, u32[]{:S(2)}) collective-permute-start(bf16[384,768]{1,0:T(8,128)(2,1)} %get-tuple-element.85), channel_id=1, source_target_pairs={{0,4},{4,0},{8,12},{12,8},{16,20},{20,16},{24,28},{28,24},{1,5},{5... | collective-permute-start | bytes 1769480 | tf_op jit(solution)/shard_map/ppermute | solution.py:686
  214.3 38.4 %all-to-all-start.2 = ((bf16[16,48,768]{2,1,0:T(8,128)(2,1)}), bf16[16,48,768]{2,1,0:T(8,128)(2,1)S(1)}, u32[]{:S(2)}, u32[]{:S(2)}) async-start(bf16[16,48,768]{2,1,0:T(8,128)(2,1)} %pad_maximum_fusion.3.rest_10_), calls=%async_computation.2 | async-start | bytes 2359296 | tf_op jit(solution)/shard_map/all_to_all | solution.py:766
  225.6 36.5 %collective-permute-start.13 = (bf16[2,384,768]{2,1,0:T(8,128)(2,1)}, bf16[2,384,768]{2,1,0:T(8,128)(2,1)}, u32[]{:S(2)}, u32[]{:S(2)}) collective-permute-start(bf16[2,384,768]{2,1,0:T(8,128)(2,1)} %get-tuple-element.118.rest_8_), channel_id=1, source_target_pairs={{0,8},{4,12},{8,0},{12,4},{16,24},{20,28},{24,16},{28,20},{1,9},{5... | collective-permute-start | bytes 3538952 | tf_op jit(solution)/shard_map/ppermute | solution.py:686
  230.9 34.6 %collective-permute-start.16 = (bf16[2,768,384]{2,1,0:T(8,128)(2,1)}, bf16[2,768,384]{2,1,0:T(8,128)(2,1)}, u32[]{:S(2)}, u32[]{:S(2)}) collective-permute-start(bf16[2,768,384]{2,1,0:T(8,128)(2,1)} %get-tuple-element.120.rest_9_), channel_id=1, source_target_pairs={{0,16},{4,20},{8,24},{12,28},{16,0},{20,4},{24,8},{28,12},{1,17},{... | collective-permute-start | bytes 3538952 | tf_op jit(solution)/shard_map/ppermute | solution.py:686
  257.3 24.6 %all-to-all-start.3 = ((bf16[16,24,768]{2,1,0:T(8,128)(2,1)}), bf16[16,24,768]{2,1,0:T(8,128)(2,1)S(1)}, u32[]{:S(2)}, u32[]{:S(2)}) async-start(bf16[16,24,768]{2,1,0:T(8,128)(2,1)} %bitcast.50.rest_11_), calls=%async_computation.3 | async-start | bytes 1179648 | tf_op jit(solution)/shard_map/all_to_all | solution.py:766
  263.4 23.1 %collective-permute-start.14 = (bf16[384,768]{1,0:T(8,128)(2,1)S(1)}, bf16[384,768]{1,0:T(8,128)(2,1)}, u32[]{:S(2)}, u32[]{:S(2)}) collective-permute-start(bf16[384,768]{1,0:T(8,128)(2,1)S(1)} %fusion.29.rest_8_), channel_id=1, source_target_pairs={{0,16},{4,20},{8,24},{12,28},{16,0},{20,4},{24,8},{28,12},{1,17},{... | collective-permute-start | bytes 1769480 | tf_op jit(solution)/shard_map/ppermute | solution.py:686
  267.5 17.4 %collective-permute-start.17 = (bf16[768,384]{1,0:T(8,128)(2,1)}, bf16[768,384]{1,0:T(8,128)(2,1)}, u32[]{:S(2)}, u32[]{:S(2)}) collective-permute-start(bf16[768,384]{1,0:T(8,128)(2,1)} %fusion.27.rest_9_), channel_id=1, source_target_pairs={{0,8},{4,12},{8,0},{12,4},{16,24},{20,28},{24,16},{28,20},{1,9},{5... | collective-permute-start | bytes 1769480 | tf_op jit(solution)/shard_map/ppermute | solution.py:686
  289.0 37.2 %all-to-all-start.1 = ((bf16[4,192,768]{2,1,0:T(8,128)(2,1)}), bf16[4,192,768]{2,1,0:T(8,128)(2,1)S(1)}, u32[]{:S(2)}, u32[]{:S(2)}) async-start(bf16[4,192,768]{2,1,0:T(8,128)(2,1)} %maximum_maximum_fusion.rest_8_), calls=%async_computation.1 | async-start | bytes 2359296 | tf_op jit(solution)/shard_map/all_to_all | solution.py:1101
  293.3 82.2 %all-gather.11.cloned.1.call-start = ((), (), s32[]{:S(2)}) async-start(), calls=%async_computation.7 | async-start | bytes 3870720 | tf_op jit(solution)/shard_map/all_gather | solution.py:1155
  329.7 17.6 %collective-permute-start.22 = (bf16[2,4,256,768]{3,2,1,0:T(8,128)(2,1)}, bf16[2,4,256,768]{3,2,1,0:T(8,128)(2,1)}, u32[]{:S(2)}, u32[]{:S(2)}) collective-permute-start(bf16[2,4,256,768]{3,2,1,0:T(8,128)(2,1)} %get-tuple-element.112.refs_1_.refs_7_), channel_id=1, source_target_pairs={{0,4},{4,0},{8,12},{12,8},{16,20},{20,16},{24,28},{28,24},{1,5},{5... | collective-permute-start | bytes 9437192 | tf_op jit(solution)/shard_map/ppermute | solution.py:686
  329.9 29.0 %all-to-all-start.4 = ((bf16[16,25,768]{2,1,0:T(8,128)(2,1)}), bf16[16,25,768]{2,1,0:T(8,128)(2,1)}, u32[]{:S(2)}, u32[]{:S(2)}) async-start(bf16[16,25,768]{2,1,0:T(8,128)(2,1)} %bitcast.60.refs_11_.refs_9_), calls=%async_computation.4 | async-start | bytes 1572864 | tf_op jit(solution)/shard_map/all_to_all | solution.py:766
  361.6 7.8 %collective-permute-start.25 = (bf16[2,32,768]{2,1,0:T(8,128)(2,1)S(1)}, bf16[2,32,768]{2,1,0:T(8,128)(2,1)S(1)}, u32[]{:S(2)}, u32[]{:S(2)}) collective-permute-start(bf16[2,32,768]{2,1,0:T(8,128)(2,1)S(1)} %pad_maximum_fusion.15), channel_id=1, source_target_pairs={{0,8},{4,12},{8,0},{12,4},{16,24},{20,28},{24,16},{28,20},{1,9},{5... | collective-permute-start | bytes 294920 | tf_op jit(solution)/shard_map/ppermute | solution.py:686
  361.8 26.5 %collective-permute-start.23 = (bf16[2,256,768]{2,1,0:T(8,128)(2,1)S(1)}, bf16[2,256,768]{2,1,0:T(8,128)(2,1)}, u32[]{:S(2)}, u32[]{:S(2)}) collective-permute-start(bf16[2,256,768]{2,1,0:T(8,128)(2,1)S(1)} %copy-done.19), channel_id=1, source_target_pairs={{0,8},{4,12},{8,0},{12,4},{16,24},{20,28},{24,16},{28,20},{1,9},{5... | collective-permute-start | bytes 2359304 | tf_op jit(solution)/shard_map/ppermute | solution.py:686
  363.8 27.9 %collective-permute-start.27 = (bf16[2,256,768]{2,1,0:T(8,128)(2,1)S(1)}, bf16[2,256,768]{2,1,0:T(8,128)(2,1)}, u32[]{:S(2)}, u32[]{:S(2)}) collective-permute-start(bf16[2,256,768]{2,1,0:T(8,128)(2,1)S(1)} %copy-done.18), channel_id=1, source_target_pairs={{0,16},{4,20},{8,24},{12,28},{16,0},{20,4},{24,8},{28,12},{1,17},{... | collective-permute-start | bytes 2359304 | tf_op jit(solution)/shard_map/ppermute | solution.py:686
  390.2 15.4 %collective-permute-start.26 = (bf16[384,768]{1,0:T(8,128)(2,1)}, bf16[384,768]{1,0:T(8,128)(2,1)}, u32[]{:S(2)}, u32[]{:S(2)}) collective-permute-start(bf16[384,768]{1,0:T(8,128)(2,1)} %pad_maximum_fusion.8), channel_id=1, source_target_pairs={{0,16},{4,20},{8,24},{12,28},{16,0},{20,4},{24,8},{28,12},{1,17},{... | collective-permute-start | bytes 1769480 | tf_op jit(solution)/shard_map/ppermute | solution.py:686
  392.8 10.8 %collective-permute-start.28 = (bf16[256,768]{1,0:T(8,128)(2,1)S(1)}, bf16[256,768]{1,0:T(8,128)(2,1)}, u32[]{:S(2)}, u32[]{:S(2)}) collective-permute-start(bf16[256,768]{1,0:T(8,128)(2,1)S(1)} %fusion.31), channel_id=1, source_target_pairs={{0,8},{4,12},{8,0},{12,4},{16,24},{20,28},{24,16},{28,20},{1,9},{5... | collective-permute-start | bytes 1179656 | tf_op jit(solution)/shard_map/ppermute | solution.py:686
  (47 other events, 247.8 us)
Sparse Core Ops, SparseCore 0:
  17.2 65.5 all-gather.6
  88.2 63.5 all-gather.8
  329.8 45.6 all-gather.10

commit v4 on v3

--- a/solution.py
+++ b/solution.py
@@ -660,7 +660,7 @@
         ),
         out_shape=out_shape,
         compiler_params=pltpu.CompilerParams(vmem_limit_bytes=48 * MIB),
-        cost_estimate=taking(3),
+        cost_estimate=taking(0.5),
         name="token_share",
     )(jnp.reshape(c, (1,)).astype(jnp.int32), *dkvs, *weights, *more, *waits)
 
@@ -815,21 +815,25 @@
     rows = c_ref.shape[0] // PIECES
     more_ref[count : count + rows] = c_ref[pl.ds(pl.multiple_of(piece * rows, 16), rows), :]
     at = count + rows
+    rows = o_ref.shape[0] // PIECES
+    whole = o_ref[...].astype(F32)
+    turned = pltpu.roll(whole, whole.shape[0] - piece * rows, 0)
+    rows = -(-rows // 16) * 16
+    more_ref[at : at + rows] = turned[:rows].astype(BF16)
+    at += rows
     left = (PAIRS - AHEAD) * 3 * PAIR // width
     for i in range(left):
         some = columns[ahead + i * width // PAIR : ahead + (i + 1) * width // PAIR]
-        more_ref[at : at + half] = jnp.concatenate(some, axis=1).astype(BF16)
-        at += half
-    rows = o_ref.shape[0] // PIECES
-    whole = o_ref[...].astype(F32)
-    turned = pltpu.roll(whole, whole.shape[0] - piece * rows, 0)
-    more_ref[at:] = turned[: more_ref.shape[0] - at].astype(BF16)
+        some = jnp.concatenate(some, axis=1)
+        some = jnp.where(c // (2 << i) % 2 == 0, some[: half // 2], some[half // 2 :])
+        more_ref[at : at + half // 2] = some.astype(BF16)
+        at += half // 2
 
 
 def start_arrays(c, weights, vectors, parts):
     half, width = weights[0].shape[0] // 2, weights[0].shape[1]
     count = weights[4].shape[0] // 2 + weights[5].shape[0] // PIECES
-    count += (PAIRS - AHEAD) * 3 * PAIR // width * half
+    count += (PAIRS - AHEAD) * 3 * PAIR // width * half // 2
     count += -(-weights[3].shape[0] // PIECES // 16) * 16
     full = lambda shape: pl.BlockSpec(shape, lambda i: (0,) * len(shape))
     shapes = [(half + 8, width), (count, width)]
@@ -974,11 +978,14 @@
     o_rows = part // PIECES
     mixed = 2 * each_piece
     w_hidden = lax.all_gather(behind, "wt")
-    following = w_hidden[:, mixed : mixed + 2 * half].reshape(parts, 2, half, width)
-    following = jnp.concatenate([following[:, 0], following[:, 1]], axis=2)
-    w_hidden = jnp.concatenate(
-        [w_hidden[:, :mixed], w_hidden[:, mixed + 2 * half : mixed + 2 * half + o_rows]], axis=1
-    )
+    mixed += -(-o_rows // 16) * 16
+    following = w_hidden[:, mixed:].reshape(parts, 2, half // 2, width)
+    following = [
+        jnp.transpose(doubled(following[:, i], 2 << i), (1, 0, 2, 3)).reshape(parts, half, width)
+        for i in range(2)
+    ]
+    following = jnp.concatenate(following, axis=2)
+    w_hidden = w_hidden[:, :mixed]
 
     start = jnp.minimum(c * extra, global_count - extra)
     more = lax.dynamic_slice_in_dim(pieces[0], start, extra, 0)
@@ -1017,10 +1024,11 @@
     vectors = jnp.stack([b_output, g_attn, s_attn, b_contract, g_ffn, s_ffn, zero, zero])
     keep = usable.astype(F32)
     w_hidden = after(
-        w_hidden, *pieces, weights[0], cot, starts, limits, b_qkv, vectors, b_expand, keep, x
+        w_hidden, *pieces[:PIECES:2], leading, cot, starts, limits, b_qkv, vectors, b_expand, keep
     )
     w_hidden = lax.all_gather(w_hidden, "ctx", axis_index_groups=groups_of(shards))
-    w_output = jnp.transpose(w_hidden[:, :, 2 * each_piece :], (1, 0, 2, 3)).reshape(width, width)
+    w_output = w_hidden[:, :, 2 * each_piece : 2 * each_piece + o_rows]
+    w_output = jnp.transpose(w_output, (1, 0, 2, 3)).reshape(width, width)
     forward = partial(attention_forward, starts, limits, x, pieces)
     kept = [forward(weights[0], b_qkv, (cot,), *GROUPS[0], extra)]
     weights.append(joined(following))

time: 431 us -> 424 us (0.984)
  waiting for transfers between devices: 87.9 us -> 80.5 us
    all_gather x1, waiting for transfers between devices: 18 us -> 1.07 us  [body(): lax.all_gather(w_hidden, 'ctx', axis_index_groups=groups_of(shards))]
    ppermute x27 -> x29, waiting for transfers between devices: 31.5 us -> 42.9 us  [swapped(): return lax.ppermute(value, 'ctx', [(i, i ^ bit) for i in range(shards)])]
    ppermute x27 -> x29, starting transfers between devices: 22.4 us -> 25.8 us  [swapped(): return lax.ppermute(value, 'ctx', [(i, i ^ bit) for i in range(shards)])]
  transfers between devices with their start and end apart: 37 -> 39, of which waited for: 14 -> 17; matrix products, arithmetic and copies ran while one was open for 15% -> 14% of each run, Pallas kernels for 32% -> 33%
where the time goes in v4:
time: 424 us; the launch traced here: 417 us
  Pallas kernels  171 us (40%)
  waiting for transfers between devices  80.5 us (19%)
  starting transfers between devices  56.1 us (13%)
  other arithmetic  54.5 us (13%)
  local copies, waits for them, and re-layouts  36.5 us (9%)
  between operations  15.9 us (4%)
    pallas_call x4, Pallas kernels, attention_backward(): pl.pallas_call(partial(backward_kernel, first=first, row_blocks=row_block...  66.9 us
    pallas_call x2, Pallas kernels, attention_forward(): pl.pallas_call(partial(forward_kernel, first=first, row_blocks=row_blocks...  43.2 us
    ppermute x29, waiting for transfers between devices, swapped(): return lax.ppermute(value, 'ctx', [(i, i ^ bit) for i in range(shards)])  42.9 us
    pallas_call x1, Pallas kernels, layer(): pl.pallas_call(layer_kernel, grid_spec=pltpu.PrefetchScalarGridSpec(num_s...  34.7 us
    ppermute x29, starting transfers between devices, swapped(): return lax.ppermute(value, 'ctx', [(i, i ^ bit) for i in range(shards)])  25.8 us
    ppermute x2, waiting for transfers between devices, line_step(): other = lax.ppermute(value, 'wt', [(i, i ^ bit) for i in range(parts)])  25.6 us
    convert_element_type x13, other arithmetic, added(): return (keep.astype(F32) + came.astype(F32)).astype(BF16)  21.2 us
    pallas_call x2, Pallas kernels, token_share(): pl.pallas_call(partial(token_kernel, away=away, extra=extra, count=count)...  19.1 us
  transfers between devices with their start and end apart: 39, of which 17 were waited for; matrix products, arithmetic and copies ran while one was open for 14% of the time, Pallas kernels for 33%

profile of v4, /device:TPU:0, one launch (start us, length us, event | category | flops | bytes accessed | tf_op | source)
XLA Modules:
  0.0 417.5 jit_solution(9421568298809422894)
XLA Ops:
  7.2 3.0 collective-permute-start
  11.8 3.7 start_arrays.1
  21.5 6.5 %collective-permute-done.refs_2_.refs_1_.rest_4_.refs_3_ = bf16[512,768]{1,0:T(8,128)(2,1)S(1)} collective-permute-done((bf16[512,768]{1,0:T(8,128)(2,1)}, bf16[512,768]{1,0:T(8,128)(2,1)S(1)}, u32[]{:S(2)}, u32[]{:S(2)}) %collective-permute-start) | collective-permute-done | bytes 786464 | tf_op jit(solution)/shard_map/ppermute | solution.py:686
  28.9 4.0 all-to-all-start
  34.7 2.8 collective-permute-start.9
  44.0 25.6 %collective-permute-done.9 = bf16[2,104,768]{2,1,0:T(8,128)(2,1)S(1)} collective-permute-done((bf16[2,104,768]{2,1,0:T(8,128)(2,1)}, bf16[2,104,768]{2,1,0:T(8,128)(2,1)S(1)}, u32[]{:S(2)}, u32[]{:S(2)}) %collective-permute-start.9) | collective-permute-done | bytes 319520 | tf_op jit(solution)/shard_map/ppermute | solution.py:720
  73.6 2.8 slice.414.refs_0_
  88.7 7.6 %collective-permute-done.11 = bf16[4,48,768]{2,1,0:T(8,128)(2,1)S(1)} collective-permute-done((bf16[4,48,768]{2,1,0:T(8,128)(2,1)S(1)}, bf16[4,48,768]{2,1,0:T(8,128)(2,1)S(1)}, u32[]{:S(2)}, u32[]{:S(2)}) %collective-permute-start.11) | collective-permute-done | bytes 294944 | tf_op jit(solution)/shard_map/ppermute | solution.py:686
  98.7 16.3 %attention_forward.2 = (bf16[528,256]{1,0:T(8,128)(2,1)}, bf16[4096,512]{1,0:T(8,128)(2,1)}, bf16[528,256]{1,0:T(8,128)(2,1)}, bf16[8,2,512,128]{3,2,1,0:T(8,128)(2,1)}, bf16[2,4096,32]{2,1,0:T(8,128)(2,1)}) custom-call(s32[578]{0:T(1024)} %pad_add_fusion.1.starts.refs_7_, s32[584]{0:T(1024)} %pad_add_fusion.2.limits.refs_8_, ...), custom_call_target="tpu_custom_call" | custom-call | flops 20000000000 | bytes 1000000 | tf_op jit(solution)/shard_map/attention_forward/pallas_call | solution.py:303
  117.1 26.9 %attention_forward.3 = (bf16[528,512]{1,0:T(8,128)(2,1)}, bf16[4096,1024]{1,0:T(8,128)(2,1)}, bf16[528,512]{1,0:T(8,128)(2,1)}, bf16[8,4,512,128]{3,2,1,0:T(8,128)(2,1)}, bf16[4,4096,32]{2,1,0:T(8,128)(2,1)}) custom-call(s32[578]{0:T(1024)} %pad_add_fusion.1.starts.refs_7_, s32[584]{0:T(1024)} %pad_add_fusion.2.limits.refs_8_, ...), custom_call_target="tpu_custom_call" | custom-call | flops 40000000000 | bytes 1000000 | tf_op jit(solution)/shard_map/attention_forward/pallas_call | solution.py:303
  147.5 34.7 %layer.1 = (bf16[528,768]{1,0:T(8,128)(2,1)}, f32[528,768]{1,0:T(8,128)}, bf16[528,768]{1,0:T(8,128)(2,1)}, bf16[384,768]{1,0:T(8,128)(2,1)}, bf16[384,768]{1,0:...) custom-call(s32[1]{0:T(128)} %bitcast.me, ...), custom_call_target="tpu_custom_call" | custom-call | flops 35000000512 | bytes 1000000 | tf_op jit(solution)/shard_map/layer/pallas_call | solution.py:532
  183.1 20.8 %attention_backward.4 = (bf16[528,256]{1,0:T(8,128)(2,1)}, bf16[4096,512]{1,0:T(8,128)(2,1)}, bf16[384,768]{1,0:T(8,128)(2,1)}, bf16[384,768]{1,0:T(8,128)(2,1)}...) custom-call(s32[578]{0:T(1024)} %pad_add_fusion.1.starts.refs_7_, bf16[528,768]{1,0:T(8,128)(2,1)} %pad_maximum_fusion.3.x_ref, ...), custom_call_target="tpu_custom_call" | custom-call | flops 8000000000 | bytes 1000000 | tf_op jit(solution)/shard_map/attention_backward/pallas_call | solution.py:351
  207.5 5.8 %all-to-all-start.2 = ((bf16[16,48,768]{2,1,0:T(8,128)(2,1)}), bf16[16,48,768]{2,1,0:T(8,128)(2,1)S(1)}, u32[]{:S(2)}, u32[]{:S(2)}) async-start(bf16[16,48,768]{2,1,0:T(8,128)(2,1)} %pad_maximum_fusion.2.rest_10_), calls=%async_computation.2 | async-start | bytes 2359296 | tf_op jit(solution)/shard_map/all_to_all | solution.py:766
  214.7 4.0 add_convert_fusion.3
  220.8 3.2 add_convert_fusion.1
  225.4 20.3 %attention_backward.5 = (bf16[528,256]{1,0:T(8,128)(2,1)}, bf16[4096,512]{1,0:T(8,128)(2,1)}, bf16[384,768]{1,0:T(8,128)(2,1)}, bf16[384,768]{1,0:T(8,128)(2,1)}...) custom-call(s32[578]{0:T(1024)} %pad_add_fusion.1.starts.refs_7_, bf16[528,768]{1,0:T(8,128)(2,1)} %pad_maximum_fusion.3.x_ref, ...), custom_call_target="tpu_custom_call" | custom-call | flops 8000000000 | bytes 1000000 | tf_op jit(solution)/shard_map/attention_backward/pallas_call | solution.py:351
  250.4 4.9 %all-to-all-start.3 = ((bf16[16,24,768]{2,1,0:T(8,128)(2,1)}), bf16[16,24,768]{2,1,0:T(8,128)(2,1)S(1)}, u32[]{:S(2)}, u32[]{:S(2)}) async-start(bf16[16,24,768]{2,1,0:T(8,128)(2,1)} %bitcast.58.rest_11_), calls=%async_computation.3 | async-start | bytes 1179648 | tf_op jit(solution)/shard_map/all_to_all | solution.py:766
  256.5 2.1 collective-permute-start.16
  262.0 12.9 %attention_backward.6 = (bf16[528,128]{1,0:T(8,128)(2,1)}, bf16[4096,256]{1,0:T(8,128)(2,1)}, bf16[384,384]{1,0:T(8,128)(2,1)}, bf16[384,384]{1,0:T(8,128)(2,1)}...) custom-call(s32[578]{0:T(1024)} %pad_add_fusion.1.starts.refs_7_, bf16[528,768]{1,0:T(8,128)(2,1)} %pad_maximum_fusion.3.x_ref, ...), custom_call_target="tpu_custom_call" | custom-call | flops 8000000000 | bytes 1000000 | tf_op jit(solution)/shard_map/attention_backward/pallas_call | solution.py:351
  275.6 2.4 collective-permute-done.19
  282.1 4.3 %all-to-all-start.1 = ((bf16[4,192,768]{2,1,0:T(8,128)(2,1)}), bf16[4,192,768]{2,1,0:T(8,128)(2,1)S(1)}, u32[]{:S(2)}, u32[]{:S(2)}) async-start(bf16[4,192,768]{2,1,0:T(8,128)(2,1)} %maximum_maximum_fusion.rest_8_), calls=%async_computation.1 | async-start | bytes 2359296 | tf_op jit(solution)/shard_map/all_to_all | solution.py:1109
  286.7 12.9 %attention_backward.7 = (bf16[528,128]{1,0:T(8,128)(2,1)}, bf16[4096,256]{1,0:T(8,128)(2,1)}, bf16[384,384]{1,0:T(8,128)(2,1)}, bf16[384,384]{1,0:T(8,128)(2,1)}...) custom-call(s32[578]{0:T(1024)} %pad_add_fusion.1.starts.refs_7_, bf16[528,768]{1,0:T(8,128)(2,1)} %pad_maximum_fusion.3.x_ref, ...), custom_call_target="tpu_custom_call" | custom-call | flops 20000000000 | bytes 1000000 | tf_op jit(solution)/shard_map/attention_backward/pallas_call | solution.py:351
  308.0 10.1 %token_share.2 = (bf16[2,4,256,768]{3,2,1,0:T(8,128)(2,1)}, f32[528,768]{1,0:T(8,128)S(1)}) custom-call(s32[1]{0:T(128)} %bitcast.me, bf16[4096,512]{1,0:T(8,128)(2,1)} %get-tuple-element.79.refs_0_, bf16[4096,512]{1,0:T(8,128)(2,1)} %get-tuple-element.88.refs_1_, bf16[4096,256]{1,0:T(8,128)(2,1)} %get-tuple-element.91.refs_2_, ...), custom_call_target="tpu_custom_call" | custom-call | flops 500000000 | bytes 1000000 | tf_op jit(solution)/shard_map/token_share/pallas_call | solution.py:648
  322.9 6.6 %all-to-all-start.4 = ((bf16[16,25,768]{2,1,0:T(8,128)(2,1)}), bf16[16,25,768]{2,1,0:T(8,128)(2,1)}, u32[]{:S(2)}, u32[]{:S(2)}) async-start(bf16[16,25,768]{2,1,0:T(8,128)(2,1)} %bitcast.68.refs_11_.refs_9_), calls=%async_computation.4 | async-start | bytes 1572864 | tf_op jit(solution)/shard_map/all_to_all | solution.py:766
  331.3 9.0 %token_share.3 = bf16[2,4,256,768]{3,2,1,0:T(8,128)(2,1)} custom-call(s32[1]{0:T(128)} %bitcast.me, bf16[4096,512]{1,0:T(8,128)(2,1)} %get-tuple-element.79.refs_0_, bf16[4096,512]{1,0:T(8,128)(2,1)} %get-tuple-element.88.refs_1_, bf16[4096,256]{1,0:T(8,128)(2,1)S(1)} %copy-done.1, bf16[4096,256]{1,0:T(8,128)(2,1)} %get-tuple-element.92.refs_3_, ...), custom_call_target="tpu_custom_call" | custom-call | flops 500000000 | bytes 1000000 | tf_op jit(solution)/shard_map/token_share/pallas_call | solution.py:648
  344.4 2.7 add_convert_fusion.4
  347.0 4.8 %all-to-all-done.4.refs_0_ = bf16[16,25,768]{2,1,0:T(8,128)(2,1)} async-done(((bf16[16,25,768]{2,1,0:T(8,128)(2,1)}), bf16[16,25,768]{2,1,0:T(8,128)(2,1)}, u32[]{:S(2)}, u32[]{:S(2)}) %all-to-all-start.4) | async-done | bytes 614432 | tf_op jit(solution)/shard_map/all_to_all | solution.py:766
  357.4 5.0 %collective-permute-done.27 = bf16[2,32,768]{2,1,0:T(8,128)(2,1)S(1)} collective-permute-done((bf16[2,32,768]{2,1,0:T(8,128)(2,1)S(1)}, bf16[2,32,768]{2,1,0:T(8,128)(2,1)S(1)}, u32[]{:S(2)}, u32[]{:S(2)}) %collective-permute-start.27) | collective-permute-done | bytes 98336 | tf_op jit(solution)/shard_map/ppermute | solution.py:686
  362.5 6.0 %all-gather.11.cloned.1.call-done = bf16[2240,768]{1,0:T(8,128)(2,1)} async-done(((bf16[280,768]{1,0:T(8,128)(2,1)}), bf16[2240,768]{1,0:T(8,128)(2,1)}) %all-gather.11.cloned.1.call-update) | async-done | bytes 3440656 | tf_op jit(solution)/shard_map/all_gather | solution.py:1163
  369.5 2.2 slice_select_fusion.refs_3_
  377.4 3.9 collective-permute-done.25.refs_0_
  388.0 8.5 %collective-permute-done.30 = bf16[256,768]{1,0:T(8,128)(2,1)} collective-permute-done((bf16[256,768]{1,0:T(8,128)(2,1)S(1)}, bf16[256,768]{1,0:T(8,128)(2,1)}, u32[]{:S(2)}, u32[]{:S(2)}) %collective-permute-start.30) | collective-permute-done | bytes 393248 | tf_op jit(solution)/shard_map/ppermute | solution.py:686
  (302 shorter events, 115.3 us)
Async XLA Ops:
  7.2 66.4 %all-gather.7.cloned.1.call-start = ((), (), s32[]{:S(2)}) async-start(), calls=%async_computation.5 | async-start | bytes 2457600 | tf_op jit(solution)/shard_map/all_gather | solution.py:980
  7.2 20.8 %collective-permute-start = (bf16[512,768]{1,0:T(8,128)(2,1)}, bf16[512,768]{1,0:T(8,128)(2,1)S(1)}, u32[]{:S(2)}, u32[]{:S(2)}) collective-permute-start(bf16[512,768]{1,0:T(8,128)(2,1)} %bitcast.262), channel_id=1, source_target_pairs={{0,16},{4,20},{8,24},{12,28},{16,0},{20,4},{24,8},{28,12},{1,17},{... | collective-permute-start | bytes 2359304 | tf_op jit(solution)/shard_map/ppermute | solution.py:686
  10.3 23.6 %collective-permute-start.2 = (bf16[512,768]{1,0:T(8,128)(2,1)}, bf16[512,768]{1,0:T(8,128)(2,1)S(1)}, u32[]{:S(2)}, u32[]{:S(2)}) collective-permute-start(bf16[512,768]{1,0:T(8,128)(2,1)} %bitcast.263), channel_id=1, source_target_pairs={{0,8},{4,12},{8,0},{12,4},{16,24},{20,28},{24,16},{28,20},{1,9},{5... | collective-permute-start | bytes 2359304 | tf_op jit(solution)/shard_map/ppermute | solution.py:686
  15.4 17.6 %collective-permute-start.8 = (bf16[1,104,768]{2,1,0:T(8,128)(2,1)}, bf16[1,104,768]{2,1,0:T(8,128)(2,1)S(1)}, u32[]{:S(2)}, u32[]{:S(2)}) collective-permute-start(bf16[1,104,768]{2,1,0:T(8,128)(2,1)} %bitcast.302), channel_id=1, source_target_pairs={{0,1},{1,0},{2,3},{3,2},{4,5},{5,4},{6,7},{7,6},{8,9},{9,8},{10,11... | collective-permute-start | bytes 479240 | tf_op jit(solution)/shard_map/ppermute | solution.py:720
  28.9 13.1 %all-to-all-start = ((bf16[8,16,768]{2,1,0:T(8,128)(2,1)}), bf16[8,16,768]{2,1,0:T(8,128)(2,1)}, u32[]{:S(2)}, u32[]{:S(2)}) async-start(bf16[8,16,768]{2,1,0:T(8,128)(2,1)} %after.8), calls=%async_computation | async-start | bytes 393216 | tf_op jit(solution)/shard_map/all_to_all | solution.py:1017
  33.0 112.1 %all-gather.9.cloned.1.call-start = ((), (), s32[]{:S(2)}) async-start(), calls=%async_computation.6 | async-start | bytes 12386304 | tf_op jit(solution)/shard_map/all_gather | solution.py:1029
  34.7 34.8 %collective-permute-start.9 = (bf16[2,104,768]{2,1,0:T(8,128)(2,1)}, bf16[2,104,768]{2,1,0:T(8,128)(2,1)S(1)}, u32[]{:S(2)}, u32[]{:S(2)}) collective-permute-start(bf16[2,104,768]{2,1,0:T(8,128)(2,1)} %after.7), channel_id=1, source_target_pairs={{0,2},{1,3},{2,0},{3,1},{4,6},{5,7},{6,4},{7,5},{8,10},{9,11},{10,... | collective-permute-start | bytes 958472 | tf_op jit(solution)/shard_map/ppermute | solution.py:720
  37.6 35.9 %collective-permute-start.1 = (bf16[256,768]{1,0:T(8,128)(2,1)S(1)}, bf16[256,768]{1,0:T(8,128)(2,1)S(1)}, u32[]{:S(2)}, u32[]{:S(2)}) collective-permute-start(bf16[256,768]{1,0:T(8,128)(2,1)S(1)} %slice.404), channel_id=1, source_target_pairs={{0,8},{4,12},{8,0},{12,4},{16,24},{20,28},{24,16},{28,20},{1,9},{5... | collective-permute-start | bytes 1179656 | tf_op jit(solution)/shard_map/ppermute | solution.py:686
  40.5 33.0 %collective-permute-start.3 = (bf16[256,768]{1,0:T(8,128)(2,1)S(1)}, bf16[256,768]{1,0:T(8,128)(2,1)S(1)}, u32[]{:S(2)}, u32[]{:S(2)}) collective-permute-start(bf16[256,768]{1,0:T(8,128)(2,1)S(1)} %slice.405), channel_id=1, source_target_pairs={{0,16},{4,20},{8,24},{12,28},{16,0},{20,4},{24,8},{28,12},{1,17},{... | collective-permute-start | bytes 1179656 | tf_op jit(solution)/shard_map/ppermute | solution.py:686
  78.1 8.1 %collective-permute-start.5 = (bf16[512,768]{1,0:T(8,128)(2,1)S(1)}, bf16[512,768]{1,0:T(8,128)(2,1)}, u32[]{:S(2)}, u32[]{:S(2)}) collective-permute-start(bf16[512,768]{1,0:T(8,128)(2,1)S(1)} %copy-done.15), channel_id=1, source_target_pairs={{0,4},{4,0},{8,12},{12,8},{16,20},{20,16},{24,28},{28,24},{1,5},{5... | collective-permute-start | bytes 2359304 | tf_op jit(solution)/shard_map/ppermute | solution.py:686
  78.4 7.9 %collective-permute-start.6 = (bf16[512,768]{1,0:T(8,128)(2,1)S(1)}, bf16[512,768]{1,0:T(8,128)(2,1)}, u32[]{:S(2)}, u32[]{:S(2)}) collective-permute-start(bf16[512,768]{1,0:T(8,128)(2,1)S(1)} %copy-done.18), channel_id=1, source_target_pairs={{0,4},{4,0},{8,12},{12,8},{16,20},{20,16},{24,28},{28,24},{1,5},{5... | collective-permute-start | bytes 2359304 | tf_op jit(solution)/shard_map/ppermute | solution.py:686
  82.0 14.2 %collective-permute-start.11 = (bf16[4,48,768]{2,1,0:T(8,128)(2,1)S(1)}, bf16[4,48,768]{2,1,0:T(8,128)(2,1)S(1)}, u32[]{:S(2)}, u32[]{:S(2)}) collective-permute-start(bf16[4,48,768]{2,1,0:T(8,128)(2,1)S(1)} %get-tuple-element.141), channel_id=1, source_target_pairs={{0,8},{4,12},{8,0},{12,4},{16,24},{20,28},{24,16},{28,20},{1,9},{5... | collective-permute-start | bytes 884744 | tf_op jit(solution)/shard_map/ppermute | solution.py:686
  83.6 14.7 %collective-permute-start.12 = (bf16[4,48,768]{2,1,0:T(8,128)(2,1)S(1)}, bf16[4,48,768]{2,1,0:T(8,128)(2,1)S(1)}, u32[]{:S(2)}, u32[]{:S(2)}) collective-permute-start(bf16[4,48,768]{2,1,0:T(8,128)(2,1)S(1)} %get-tuple-element.142), channel_id=1, source_target_pairs={{0,16},{4,20},{8,24},{12,28},{16,0},{20,4},{24,8},{28,12},{1,17},{... | collective-permute-start | bytes 884744 | tf_op jit(solution)/shard_map/ppermute | solution.py:686
  98.7 16.4 %collective-permute-start.13 = (bf16[4,96,1536]{2,1,0:T(8,128)(2,1)S(1)}, bf16[4,96,1536]{2,1,0:T(8,128)(2,1)S(1)}, u32[]{:S(2)}, u32[]{:S(2)}) collective-permute-start(bf16[4,96,1536]{2,1,0:T(8,128)(2,1)S(1)} %pad_maximum_fusion.1), channel_id=1, source_target_pairs={{0,4},{4,0},{8,12},{12,8},{16,20},{20,16},{24,28},{28,24},{1,5},{5... | collective-permute-start | bytes 3538952 | tf_op jit(solution)/shard_map/ppermute | solution.py:686
  182.2 31.0 %collective-permute-start.14 = (bf16[4,384,768]{2,1,0:T(8,128)(2,1)}, bf16[4,384,768]{2,1,0:T(8,128)(2,1)S(1)}, u32[]{:S(2)}, u32[]{:S(2)}) collective-permute-start(bf16[4,384,768]{2,1,0:T(8,128)(2,1)} %get-tuple-element.71), channel_id=1, source_target_pairs={{0,4},{4,0},{8,12},{12,8},{16,20},{20,16},{24,28},{28,24},{1,5},{5... | collective-permute-start | bytes 7077896 | tf_op jit(solution)/shard_map/ppermute | solution.py:686
  182.6 38.2 %collective-permute-start.17 = (bf16[4,768,384]{2,1,0:T(8,128)(2,1)}, bf16[4,768,384]{2,1,0:T(8,128)(2,1)}, u32[]{:S(2)}, u32[]{:S(2)}) collective-permute-start(bf16[4,768,384]{2,1,0:T(8,128)(2,1)} %get-tuple-element.73), channel_id=1, source_target_pairs={{0,4},{4,0},{8,12},{12,8},{16,20},{20,16},{24,28},{28,24},{1,5},{5... | collective-permute-start | bytes 7077896 | tf_op jit(solution)/shard_map/ppermute | solution.py:686
  182.8 21.4 %collective-permute-start.20 = (bf16[384,768]{1,0:T(8,128)(2,1)}, bf16[384,768]{1,0:T(8,128)(2,1)S(1)}, u32[]{:S(2)}, u32[]{:S(2)}) collective-permute-start(bf16[384,768]{1,0:T(8,128)(2,1)} %get-tuple-element.85), channel_id=1, source_target_pairs={{0,4},{4,0},{8,12},{12,8},{16,20},{20,16},{24,28},{28,24},{1,5},{5... | collective-permute-start | bytes 1769480 | tf_op jit(solution)/shard_map/ppermute | solution.py:686
  207.5 38.4 %all-to-all-start.2 = ((bf16[16,48,768]{2,1,0:T(8,128)(2,1)}), bf16[16,48,768]{2,1,0:T(8,128)(2,1)S(1)}, u32[]{:S(2)}, u32[]{:S(2)}) async-start(bf16[16,48,768]{2,1,0:T(8,128)(2,1)} %pad_maximum_fusion.2.rest_10_), calls=%async_computation.2 | async-start | bytes 2359296 | tf_op jit(solution)/shard_map/all_to_all | solution.py:766
  218.7 36.5 %collective-permute-start.15 = (bf16[2,384,768]{2,1,0:T(8,128)(2,1)}, bf16[2,384,768]{2,1,0:T(8,128)(2,1)}, u32[]{:S(2)}, u32[]{:S(2)}) collective-permute-start(bf16[2,384,768]{2,1,0:T(8,128)(2,1)} %get-tuple-element.118.rest_8_), channel_id=1, source_target_pairs={{0,8},{4,12},{8,0},{12,4},{16,24},{20,28},{24,16},{28,20},{1,9},{5... | collective-permute-start | bytes 3538952 | tf_op jit(solution)/shard_map/ppermute | solution.py:686
  224.0 34.6 %collective-permute-start.18 = (bf16[2,768,384]{2,1,0:T(8,128)(2,1)}, bf16[2,768,384]{2,1,0:T(8,128)(2,1)}, u32[]{:S(2)}, u32[]{:S(2)}) collective-permute-start(bf16[2,768,384]{2,1,0:T(8,128)(2,1)} %get-tuple-element.120.rest_9_), channel_id=1, source_target_pairs={{0,16},{4,20},{8,24},{12,28},{16,0},{20,4},{24,8},{28,12},{1,17},{... | collective-permute-start | bytes 3538952 | tf_op jit(solution)/shard_map/ppermute | solution.py:686
  250.4 24.6 %all-to-all-start.3 = ((bf16[16,24,768]{2,1,0:T(8,128)(2,1)}), bf16[16,24,768]{2,1,0:T(8,128)(2,1)S(1)}, u32[]{:S(2)}, u32[]{:S(2)}) async-start(bf16[16,24,768]{2,1,0:T(8,128)(2,1)} %bitcast.58.rest_11_), calls=%async_computation.3 | async-start | bytes 1179648 | tf_op jit(solution)/shard_map/all_to_all | solution.py:766
  256.5 23.1 %collective-permute-start.16 = (bf16[384,768]{1,0:T(8,128)(2,1)S(1)}, bf16[384,768]{1,0:T(8,128)(2,1)}, u32[]{:S(2)}, u32[]{:S(2)}) collective-permute-start(bf16[384,768]{1,0:T(8,128)(2,1)S(1)} %fusion.29.rest_8_), channel_id=1, source_target_pairs={{0,16},{4,20},{8,24},{12,28},{16,0},{20,4},{24,8},{28,12},{1,17},{... | collective-permute-start | bytes 1769480 | tf_op jit(solution)/shard_map/ppermute | solution.py:686
  260.6 17.4 %collective-permute-start.19 = (bf16[768,384]{1,0:T(8,128)(2,1)}, bf16[768,384]{1,0:T(8,128)(2,1)}, u32[]{:S(2)}, u32[]{:S(2)}) collective-permute-start(bf16[768,384]{1,0:T(8,128)(2,1)} %fusion.27.rest_9_), channel_id=1, source_target_pairs={{0,8},{4,12},{8,0},{12,4},{16,24},{20,28},{24,16},{28,20},{1,9},{5... | collective-permute-start | bytes 1769480 | tf_op jit(solution)/shard_map/ppermute | solution.py:686
  282.1 37.1 %all-to-all-start.1 = ((bf16[4,192,768]{2,1,0:T(8,128)(2,1)}), bf16[4,192,768]{2,1,0:T(8,128)(2,1)S(1)}, u32[]{:S(2)}, u32[]{:S(2)}) async-start(bf16[4,192,768]{2,1,0:T(8,128)(2,1)} %maximum_maximum_fusion.rest_8_), calls=%async_computation.1 | async-start | bytes 2359296 | tf_op jit(solution)/shard_map/all_to_all | solution.py:1109
  286.4 82.1 %all-gather.11.cloned.1.call-start = ((), (), s32[]{:S(2)}) async-start(), calls=%async_computation.7 | async-start | bytes 3870720 | tf_op jit(solution)/shard_map/all_gather | solution.py:1163
  322.6 17.7 %collective-permute-start.24 = (bf16[2,4,256,768]{3,2,1,0:T(8,128)(2,1)}, bf16[2,4,256,768]{3,2,1,0:T(8,128)(2,1)}, u32[]{:S(2)}, u32[]{:S(2)}) collective-permute-start(bf16[2,4,256,768]{3,2,1,0:T(8,128)(2,1)} %get-tuple-element.112.refs_1_.refs_7_), channel_id=1, source_target_pairs={{0,4},{4,0},{8,12},{12,8},{16,20},{20,16},{24,28},{28,24},{1,5},{5... | collective-permute-start | bytes 9437192 | tf_op jit(solution)/shard_map/ppermute | solution.py:686
  322.9 29.0 %all-to-all-start.4 = ((bf16[16,25,768]{2,1,0:T(8,128)(2,1)}), bf16[16,25,768]{2,1,0:T(8,128)(2,1)}, u32[]{:S(2)}, u32[]{:S(2)}) async-start(bf16[16,25,768]{2,1,0:T(8,128)(2,1)} %bitcast.68.refs_11_.refs_9_), calls=%async_computation.4 | async-start | bytes 1572864 | tf_op jit(solution)/shard_map/all_to_all | solution.py:766
  354.6 7.8 %collective-permute-start.27 = (bf16[2,32,768]{2,1,0:T(8,128)(2,1)S(1)}, bf16[2,32,768]{2,1,0:T(8,128)(2,1)S(1)}, u32[]{:S(2)}, u32[]{:S(2)}) collective-permute-start(bf16[2,32,768]{2,1,0:T(8,128)(2,1)S(1)} %pad_maximum_fusion.14), channel_id=1, source_target_pairs={{0,8},{4,12},{8,0},{12,4},{16,24},{20,28},{24,16},{28,20},{1,9},{5... | collective-permute-start | bytes 294920 | tf_op jit(solution)/shard_map/ppermute | solution.py:686
  354.7 26.5 %collective-permute-start.25 = (bf16[2,256,768]{2,1,0:T(8,128)(2,1)S(1)}, bf16[2,256,768]{2,1,0:T(8,128)(2,1)}, u32[]{:S(2)}, u32[]{:S(2)}) collective-permute-start(bf16[2,256,768]{2,1,0:T(8,128)(2,1)S(1)} %copy-done.22), channel_id=1, source_target_pairs={{0,8},{4,12},{8,0},{12,4},{16,24},{20,28},{24,16},{28,20},{1,9},{5... | collective-permute-start | bytes 2359304 | tf_op jit(solution)/shard_map/ppermute | solution.py:686
  356.8 27.9 %collective-permute-start.29 = (bf16[2,256,768]{2,1,0:T(8,128)(2,1)S(1)}, bf16[2,256,768]{2,1,0:T(8,128)(2,1)}, u32[]{:S(2)}, u32[]{:S(2)}) collective-permute-start(bf16[2,256,768]{2,1,0:T(8,128)(2,1)S(1)} %copy-done.21), channel_id=1, source_target_pairs={{0,16},{4,20},{8,24},{12,28},{16,0},{20,4},{24,8},{28,12},{1,17},{... | collective-permute-start | bytes 2359304 | tf_op jit(solution)/shard_map/ppermute | solution.py:686
  383.2 15.4 %collective-permute-start.28 = (bf16[384,768]{1,0:T(8,128)(2,1)}, bf16[384,768]{1,0:T(8,128)(2,1)}, u32[]{:S(2)}, u32[]{:S(2)}) collective-permute-start(bf16[384,768]{1,0:T(8,128)(2,1)} %pad_maximum_fusion.7), channel_id=1, source_target_pairs={{0,16},{4,20},{8,24},{12,28},{16,0},{20,4},{24,8},{28,12},{1,17},{... | collective-permute-start | bytes 1769480 | tf_op jit(solution)/shard_map/ppermute | solution.py:686
  385.8 10.8 %collective-permute-start.30 = (bf16[256,768]{1,0:T(8,128)(2,1)S(1)}, bf16[256,768]{1,0:T(8,128)(2,1)}, u32[]{:S(2)}, u32[]{:S(2)}) collective-permute-start(bf16[256,768]{1,0:T(8,128)(2,1)S(1)} %fusion.31), channel_id=1, source_target_pairs={{0,8},{4,12},{8,0},{12,4},{16,24},{20,28},{24,16},{28,20},{1,9},{5... | collective-permute-start | bytes 1179656 | tf_op jit(solution)/shard_map/ppermute | solution.py:686
  (49 other events, 200.8 us)
Sparse Core Ops, SparseCore 0:
  17.2 55.5 all-gather.6
  76.5 68.5 all-gather.8
  322.8 45.7 all-gather.10

commit v5 on v4

--- a/solution.py
+++ b/solution.py
@@ -1181,18 +1181,20 @@
     below = below[0].astype(F32) + below_came[0].astype(F32) + below_last.astype(F32)
     input_grad = own[:rows] + jnp.concatenate([above, below], axis=0)
 
-    kinds = [gathered[:, hidden_rows:-extra].reshape(PIECES, 3, -1, width)]
-    kinds.append(late[:, None, :-1])
-    mine = jnp.concatenate(kinds, axis=1).reshape(PIECES // 2, 2, 4, -1, width)
-    mine = jnp.transpose(mine, (2, 1, 0, 3, 4)).reshape(4, part, width)
+    mine = gathered[:, hidden_rows:-extra].reshape(PIECES // 2, 2, 3, -1, width)
+    mine = jnp.transpose(mine, (2, 1, 0, 3, 4)).reshape(3, part, width)
+    last = late[:, :-1].reshape(PIECES // 2, 2, -1, width)
+    last = jnp.transpose(last, (1, 0, 2, 3)).reshape(part, width)
     small = jnp.transpose(late[:, -1].reshape(PIECES // 2, 2, width), (1, 0, 2)).reshape(-1, width)
     small = small.astype(F32)
     small_grads = [small[i // parts, i % parts * each :][:each] for i in range(8)]
     expand_bias_grad = small[2]
     output_wgrad = mine[0].astype(F32)
+    places = jnp.concatenate(list(column_places(AHEAD)))
+    sides = [ordered(g, places) for g in (mine[1], mine[2], last)]
     query_wgrad, key_wgrad, value_wgrad = (
-        jnp.concatenate([ordered(g, places) for g in (mine[1], mine[2], mine[3])], axis=1)
-        for places in column_places(AHEAD)
+        jnp.concatenate([g[:, at : at + width // 3] for g in sides], axis=1)
+        for at in range(0, width, width // 3)
     )
 
     return (

time: 424 us -> 424 us (level)
    unnamed x84 -> x98, local copies, waits for them, and re-layouts: 12.2 us -> 11.6 us
  transfers between devices with their start and end apart: 39 -> 39, of which waited for: 17 -> 16; matrix products, arithmetic and copies ran while one was open for 14% -> 15% of each run, Pallas kernels for 33% -> 33%
where the time goes in v5:
time: 424 us; the launch traced here: 417 us
  Pallas kernels  171 us (40%)
  waiting for transfers between devices  79.4 us (19%)
  starting transfers between devices  56.1 us (13%)
  other arithmetic  53.4 us (13%)
  local copies, waits for them, and re-layouts  39.1 us (9%)
  between operations  15.9 us (4%)
    pallas_call x4, Pallas kernels, attention_backward(): pl.pallas_call(partial(backward_kernel, first=first, row_blocks=row_block...  66.9 us
    pallas_call x2, Pallas kernels, attention_forward(): pl.pallas_call(partial(forward_kernel, first=first, row_blocks=row_blocks...  43.3 us
    ppermute x29, waiting for transfers between devices, swapped(): return lax.ppermute(value, 'ctx', [(i, i ^ bit) for i in range(shards)])  42.2 us
    pallas_call x1, Pallas kernels, layer(): pl.pallas_call(layer_kernel, grid_spec=pltpu.PrefetchScalarGridSpec(num_s...  34.7 us
    ppermute x29, starting transfers between devices, swapped(): return lax.ppermute(value, 'ctx', [(i, i ^ bit) for i in range(shards)])  25.8 us
    ppermute x2, waiting for transfers between devices, line_step(): other = lax.ppermute(value, 'wt', [(i, i ^ bit) for i in range(parts)])  25.6 us
    convert_element_type x13, other arithmetic, added(): return (keep.astype(F32) + came.astype(F32)).astype(BF16)  21.5 us
    pallas_call x2, Pallas kernels, token_share(): pl.pallas_call(partial(token_kernel, away=away, extra=extra, count=count)...  19.1 us
  transfers between devices with their start and end apart: 39, of which 16 were waited for; matrix products, arithmetic and copies ran while one was open for 15% of the time, Pallas kernels for 33%

profile of v5, /device:TPU:0, one launch (start us, length us, event | category | flops | bytes accessed | tf_op | source)
XLA Modules:
  0.0 417.1 jit_solution(5526181347072324781)
XLA Ops:
  7.2 3.0 collective-permute-start
  11.8 3.7 start_arrays.1
  21.5 6.6 %collective-permute-done.refs_2_.refs_1_.rest_4_.refs_3_ = bf16[512,768]{1,0:T(8,128)(2,1)S(1)} collective-permute-done((bf16[512,768]{1,0:T(8,128)(2,1)}, bf16[512,768]{1,0:T(8,128)(2,1)S(1)}, u32[]{:S(2)}, u32[]{:S(2)}) %collective-permute-start) | collective-permute-done | bytes 786464 | tf_op jit(solution)/shard_map/ppermute | solution.py:686
  28.9 4.0 all-to-all-start
  34.7 2.8 collective-permute-start.9
  43.9 25.6 %collective-permute-done.9 = bf16[2,104,768]{2,1,0:T(8,128)(2,1)S(1)} collective-permute-done((bf16[2,104,768]{2,1,0:T(8,128)(2,1)}, bf16[2,104,768]{2,1,0:T(8,128)(2,1)S(1)}, u32[]{:S(2)}, u32[]{:S(2)}) %collective-permute-start.9) | collective-permute-done | bytes 319520 | tf_op jit(solution)/shard_map/ppermute | solution.py:720
  73.6 2.8 slice.439.refs_0_
  88.6 7.6 %collective-permute-done.11 = bf16[4,48,768]{2,1,0:T(8,128)(2,1)S(1)} collective-permute-done((bf16[4,48,768]{2,1,0:T(8,128)(2,1)S(1)}, bf16[4,48,768]{2,1,0:T(8,128)(2,1)S(1)}, u32[]{:S(2)}, u32[]{:S(2)}) %collective-permute-start.11) | collective-permute-done | bytes 294944 | tf_op jit(solution)/shard_map/ppermute | solution.py:686
  98.7 16.3 %attention_forward.2 = (bf16[528,256]{1,0:T(8,128)(2,1)}, bf16[4096,512]{1,0:T(8,128)(2,1)}, bf16[528,256]{1,0:T(8,128)(2,1)}, bf16[8,2,512,128]{3,2,1,0:T(8,128)(2,1)}, bf16[2,4096,32]{2,1,0:T(8,128)(2,1)}) custom-call(s32[578]{0:T(1024)} %pad_add_fusion.1.starts.refs_7_, s32[584]{0:T(1024)} %pad_add_fusion.2.limits.refs_8_, ...), custom_call_target="tpu_custom_call" | custom-call | flops 20000000000 | bytes 1000000 | tf_op jit(solution)/shard_map/attention_forward/pallas_call | solution.py:303
  117.1 26.9 %attention_forward.3 = (bf16[528,512]{1,0:T(8,128)(2,1)}, bf16[4096,1024]{1,0:T(8,128)(2,1)}, bf16[528,512]{1,0:T(8,128)(2,1)}, bf16[8,4,512,128]{3,2,1,0:T(8,128)(2,1)}, bf16[4,4096,32]{2,1,0:T(8,128)(2,1)}) custom-call(s32[578]{0:T(1024)} %pad_add_fusion.1.starts.refs_7_, s32[584]{0:T(1024)} %pad_add_fusion.2.limits.refs_8_, ...), custom_call_target="tpu_custom_call" | custom-call | flops 40000000000 | bytes 1000000 | tf_op jit(solution)/shard_map/attention_forward/pallas_call | solution.py:303
  147.5 34.7 %layer.1 = (bf16[528,768]{1,0:T(8,128)(2,1)}, f32[528,768]{1,0:T(8,128)}, bf16[528,768]{1,0:T(8,128)(2,1)}, bf16[384,768]{1,0:T(8,128)(2,1)}, bf16[384,768]{1,0:...) custom-call(s32[1]{0:T(128)} %bitcast.me, ...), custom_call_target="tpu_custom_call" | custom-call | flops 35000000512 | bytes 1000000 | tf_op jit(solution)/shard_map/layer/pallas_call | solution.py:532
  183.1 20.8 %attention_backward.4 = (bf16[528,256]{1,0:T(8,128)(2,1)}, bf16[4096,512]{1,0:T(8,128)(2,1)}, bf16[384,768]{1,0:T(8,128)(2,1)}, bf16[384,768]{1,0:T(8,128)(2,1)}...) custom-call(s32[578]{0:T(1024)} %pad_add_fusion.1.starts.refs_7_, bf16[528,768]{1,0:T(8,128)(2,1)} %pad_maximum_fusion.3.x_ref, ...), custom_call_target="tpu_custom_call" | custom-call | flops 8000000000 | bytes 1000000 | tf_op jit(solution)/shard_map/attention_backward/pallas_call | solution.py:351
  207.5 5.8 %all-to-all-start.2 = ((bf16[16,48,768]{2,1,0:T(8,128)(2,1)}), bf16[16,48,768]{2,1,0:T(8,128)(2,1)S(1)}, u32[]{:S(2)}, u32[]{:S(2)}) async-start(bf16[16,48,768]{2,1,0:T(8,128)(2,1)} %pad_maximum_fusion.2.rest_10_), calls=%async_computation.2 | async-start | bytes 2359296 | tf_op jit(solution)/shard_map/all_to_all | solution.py:766
  214.7 4.0 add_convert_fusion.3
  220.8 3.2 add_convert_fusion.1
  225.4 20.3 %attention_backward.5 = (bf16[528,256]{1,0:T(8,128)(2,1)}, bf16[4096,512]{1,0:T(8,128)(2,1)}, bf16[384,768]{1,0:T(8,128)(2,1)}, bf16[384,768]{1,0:T(8,128)(2,1)}...) custom-call(s32[578]{0:T(1024)} %pad_add_fusion.1.starts.refs_7_, bf16[528,768]{1,0:T(8,128)(2,1)} %pad_maximum_fusion.3.x_ref, ...), custom_call_target="tpu_custom_call" | custom-call | flops 8000000000 | bytes 1000000 | tf_op jit(solution)/shard_map/attention_backward/pallas_call | solution.py:351
  250.4 4.9 %all-to-all-start.3 = ((bf16[16,24,768]{2,1,0:T(8,128)(2,1)}), bf16[16,24,768]{2,1,0:T(8,128)(2,1)S(1)}, u32[]{:S(2)}, u32[]{:S(2)}) async-start(bf16[16,24,768]{2,1,0:T(8,128)(2,1)} %bitcast.58.rest_11_), calls=%async_computation.3 | async-start | bytes 1179648 | tf_op jit(solution)/shard_map/all_to_all | solution.py:766
  256.5 2.1 collective-permute-start.16
  262.0 12.9 %attention_backward.6 = (bf16[528,128]{1,0:T(8,128)(2,1)}, bf16[4096,256]{1,0:T(8,128)(2,1)}, bf16[384,384]{1,0:T(8,128)(2,1)}, bf16[384,384]{1,0:T(8,128)(2,1)}...) custom-call(s32[578]{0:T(1024)} %pad_add_fusion.1.starts.refs_7_, bf16[528,768]{1,0:T(8,128)(2,1)} %pad_maximum_fusion.3.x_ref, ...), custom_call_target="tpu_custom_call" | custom-call | flops 8000000000 | bytes 1000000 | tf_op jit(solution)/shard_map/attention_backward/pallas_call | solution.py:351
  275.6 2.4 collective-permute-done.19
  282.1 4.3 %all-to-all-start.1 = ((bf16[4,192,768]{2,1,0:T(8,128)(2,1)}), bf16[4,192,768]{2,1,0:T(8,128)(2,1)S(1)}, u32[]{:S(2)}, u32[]{:S(2)}) async-start(bf16[4,192,768]{2,1,0:T(8,128)(2,1)} %maximum_maximum_fusion.rest_8_), calls=%async_computation.1 | async-start | bytes 2359296 | tf_op jit(solution)/shard_map/all_to_all | solution.py:1109
  286.7 12.9 %attention_backward.7 = (bf16[528,128]{1,0:T(8,128)(2,1)}, bf16[4096,256]{1,0:T(8,128)(2,1)}, bf16[384,384]{1,0:T(8,128)(2,1)}, bf16[384,384]{1,0:T(8,128)(2,1)}...) custom-call(s32[578]{0:T(1024)} %pad_add_fusion.1.starts.refs_7_, bf16[528,768]{1,0:T(8,128)(2,1)} %pad_maximum_fusion.3.x_ref, ...), custom_call_target="tpu_custom_call" | custom-call | flops 20000000000 | bytes 1000000 | tf_op jit(solution)/shard_map/attention_backward/pallas_call | solution.py:351
  308.0 10.1 %token_share.2 = (bf16[2,4,256,768]{3,2,1,0:T(8,128)(2,1)}, f32[528,768]{1,0:T(8,128)S(1)}) custom-call(s32[1]{0:T(128)} %bitcast.me, bf16[4096,512]{1,0:T(8,128)(2,1)} %get-tuple-element.79.refs_0_, bf16[4096,512]{1,0:T(8,128)(2,1)} %get-tuple-element.88.refs_1_, bf16[4096,256]{1,0:T(8,128)(2,1)} %get-tuple-element.91.refs_2_, ...), custom_call_target="tpu_custom_call" | custom-call | flops 500000000 | bytes 1000000 | tf_op jit(solution)/shard_map/token_share/pallas_call | solution.py:648
  322.9 6.6 %all-to-all-start.4 = ((bf16[16,25,768]{2,1,0:T(8,128)(2,1)}), bf16[16,25,768]{2,1,0:T(8,128)(2,1)}, u32[]{:S(2)}, u32[]{:S(2)}) async-start(bf16[16,25,768]{2,1,0:T(8,128)(2,1)} %bitcast.68.refs_11_.refs_9_), calls=%async_computation.4 | async-start | bytes 1572864 | tf_op jit(solution)/shard_map/all_to_all | solution.py:766
  331.5 9.0 %token_share.3 = bf16[2,4,256,768]{3,2,1,0:T(8,128)(2,1)} custom-call(s32[1]{0:T(128)} %bitcast.me, bf16[4096,512]{1,0:T(8,128)(2,1)} %get-tuple-element.79.refs_0_, bf16[4096,512]{1,0:T(8,128)(2,1)} %get-tuple-element.88.refs_1_, bf16[4096,256]{1,0:T(8,128)(2,1)S(1)} %copy-done.1, bf16[4096,256]{1,0:T(8,128)(2,1)} %get-tuple-element.92.refs_3_, ...), custom_call_target="tpu_custom_call" | custom-call | flops 500000000 | bytes 1000000 | tf_op jit(solution)/shard_map/token_share/pallas_call | solution.py:648
  344.6 2.9 add_convert_fusion.4
  347.5 4.4 %all-to-all-done.4.refs_0_ = bf16[16,25,768]{2,1,0:T(8,128)(2,1)} async-done(((bf16[16,25,768]{2,1,0:T(8,128)(2,1)}), bf16[16,25,768]{2,1,0:T(8,128)(2,1)}, u32[]{:S(2)}, u32[]{:S(2)}) %all-to-all-start.4) | async-done | bytes 614432 | tf_op jit(solution)/shard_map/all_to_all | solution.py:766
  354.8 2.1 collective-permute-start.25
  357.4 5.0 %collective-permute-done.27 = bf16[2,32,768]{2,1,0:T(8,128)(2,1)S(1)} collective-permute-done((bf16[2,32,768]{2,1,0:T(8,128)(2,1)S(1)}, bf16[2,32,768]{2,1,0:T(8,128)(2,1)S(1)}, u32[]{:S(2)}, u32[]{:S(2)}) %collective-permute-start.27) | collective-permute-done | bytes 98336 | tf_op jit(solution)/shard_map/ppermute | solution.py:686
  362.5 6.1 %all-gather.11.cloned.1.call-done = bf16[2240,768]{1,0:T(8,128)(2,1)} async-done(((bf16[280,768]{1,0:T(8,128)(2,1)}), bf16[2240,768]{1,0:T(8,128)(2,1)}) %all-gather.11.cloned.1.call-update) | async-done | bytes 3440656 | tf_op jit(solution)/shard_map/all_gather | solution.py:1163
  377.0 4.3 %collective-permute-done.25.refs_0_ = bf16[2,256,768]{2,1,0:T(8,128)(2,1)} collective-permute-done((bf16[2,256,768]{2,1,0:T(8,128)(2,1)S(1)}, bf16[2,256,768]{2,1,0:T(8,128)(2,1)}, u32[]{:S(2)}, u32[]{:S(2)}) %collective-permute-start.25) | collective-permute-done | bytes 786464 | tf_op jit(solution)/shard_map/ppermute | solution.py:686
  391.5 8.4 %collective-permute-done.30 = bf16[256,768]{1,0:T(8,128)(2,1)S(1)} collective-permute-done((bf16[256,768]{1,0:T(8,128)(2,1)S(1)}, bf16[256,768]{1,0:T(8,128)(2,1)S(1)}, u32[]{:S(2)}, u32[]{:S(2)}) %collective-permute-start.30) | collective-permute-done | bytes 393248 | tf_op jit(solution)/shard_map/ppermute | solution.py:686
  (315 shorter events, 114.7 us)
Async XLA Ops:
  7.2 66.4 %all-gather.7.cloned.1.call-start = ((), (), s32[]{:S(2)}) async-start(), calls=%async_computation.5 | async-start | bytes 2457600 | tf_op jit(solution)/shard_map/all_gather | solution.py:980
  7.2 20.8 %collective-permute-start = (bf16[512,768]{1,0:T(8,128)(2,1)}, bf16[512,768]{1,0:T(8,128)(2,1)S(1)}, u32[]{:S(2)}, u32[]{:S(2)}) collective-permute-start(bf16[512,768]{1,0:T(8,128)(2,1)} %bitcast.260), channel_id=1, source_target_pairs={{0,16},{4,20},{8,24},{12,28},{16,0},{20,4},{24,8},{28,12},{1,17},{... | collective-permute-start | bytes 2359304 | tf_op jit(solution)/shard_map/ppermute | solution.py:686
  10.3 23.5 %collective-permute-start.2 = (bf16[512,768]{1,0:T(8,128)(2,1)}, bf16[512,768]{1,0:T(8,128)(2,1)S(1)}, u32[]{:S(2)}, u32[]{:S(2)}) collective-permute-start(bf16[512,768]{1,0:T(8,128)(2,1)} %bitcast.261), channel_id=1, source_target_pairs={{0,8},{4,12},{8,0},{12,4},{16,24},{20,28},{24,16},{28,20},{1,9},{5... | collective-permute-start | bytes 2359304 | tf_op jit(solution)/shard_map/ppermute | solution.py:686
  15.4 17.6 %collective-permute-start.8 = (bf16[1,104,768]{2,1,0:T(8,128)(2,1)}, bf16[1,104,768]{2,1,0:T(8,128)(2,1)S(1)}, u32[]{:S(2)}, u32[]{:S(2)}) collective-permute-start(bf16[1,104,768]{2,1,0:T(8,128)(2,1)} %bitcast.294), channel_id=1, source_target_pairs={{0,1},{1,0},{2,3},{3,2},{4,5},{5,4},{6,7},{7,6},{8,9},{9,8},{10,11... | collective-permute-start | bytes 479240 | tf_op jit(solution)/shard_map/ppermute | solution.py:720
  28.9 13.1 %all-to-all-start = ((bf16[8,16,768]{2,1,0:T(8,128)(2,1)}), bf16[8,16,768]{2,1,0:T(8,128)(2,1)}, u32[]{:S(2)}, u32[]{:S(2)}) async-start(bf16[8,16,768]{2,1,0:T(8,128)(2,1)} %after.8), calls=%async_computation | async-start | bytes 393216 | tf_op jit(solution)/shard_map/all_to_all | solution.py:1017
  33.0 112.1 %all-gather.9.cloned.1.call-start = ((), (), s32[]{:S(2)}) async-start(), calls=%async_computation.6 | async-start | bytes 12386304 | tf_op jit(solution)/shard_map/all_gather | solution.py:1029
  34.7 34.8 %collective-permute-start.9 = (bf16[2,104,768]{2,1,0:T(8,128)(2,1)}, bf16[2,104,768]{2,1,0:T(8,128)(2,1)S(1)}, u32[]{:S(2)}, u32[]{:S(2)}) collective-permute-start(bf16[2,104,768]{2,1,0:T(8,128)(2,1)} %after.7), channel_id=1, source_target_pairs={{0,2},{1,3},{2,0},{3,1},{4,6},{5,7},{6,4},{7,5},{8,10},{9,11},{10,... | collective-permute-start | bytes 958472 | tf_op jit(solution)/shard_map/ppermute | solution.py:720
  37.6 35.9 %collective-permute-start.1 = (bf16[256,768]{1,0:T(8,128)(2,1)S(1)}, bf16[256,768]{1,0:T(8,128)(2,1)S(1)}, u32[]{:S(2)}, u32[]{:S(2)}) collective-permute-start(bf16[256,768]{1,0:T(8,128)(2,1)S(1)} %slice.429), channel_id=1, source_target_pairs={{0,8},{4,12},{8,0},{12,4},{16,24},{20,28},{24,16},{28,20},{1,9},{5... | collective-permute-start | bytes 1179656 | tf_op jit(solution)/shard_map/ppermute | solution.py:686
  40.5 33.0 %collective-permute-start.3 = (bf16[256,768]{1,0:T(8,128)(2,1)S(1)}, bf16[256,768]{1,0:T(8,128)(2,1)S(1)}, u32[]{:S(2)}, u32[]{:S(2)}) collective-permute-start(bf16[256,768]{1,0:T(8,128)(2,1)S(1)} %slice.430), channel_id=1, source_target_pairs={{0,16},{4,20},{8,24},{12,28},{16,0},{20,4},{24,8},{28,12},{1,17},{... | collective-permute-start | bytes 1179656 | tf_op jit(solution)/shard_map/ppermute | solution.py:686
  78.1 8.2 %collective-permute-start.5 = (bf16[512,768]{1,0:T(8,128)(2,1)S(1)}, bf16[512,768]{1,0:T(8,128)(2,1)}, u32[]{:S(2)}, u32[]{:S(2)}) collective-permute-start(bf16[512,768]{1,0:T(8,128)(2,1)S(1)} %copy-done.15), channel_id=1, source_target_pairs={{0,4},{4,0},{8,12},{12,8},{16,20},{20,16},{24,28},{28,24},{1,5},{5... | collective-permute-start | bytes 2359304 | tf_op jit(solution)/shard_map/ppermute | solution.py:686
  78.4 7.9 %collective-permute-start.6 = (bf16[512,768]{1,0:T(8,128)(2,1)S(1)}, bf16[512,768]{1,0:T(8,128)(2,1)}, u32[]{:S(2)}, u32[]{:S(2)}) collective-permute-start(bf16[512,768]{1,0:T(8,128)(2,1)S(1)} %copy-done.18), channel_id=1, source_target_pairs={{0,4},{4,0},{8,12},{12,8},{16,20},{20,16},{24,28},{28,24},{1,5},{5... | collective-permute-start | bytes 2359304 | tf_op jit(solution)/shard_map/ppermute | solution.py:686
  82.0 14.2 %collective-permute-start.11 = (bf16[4,48,768]{2,1,0:T(8,128)(2,1)S(1)}, bf16[4,48,768]{2,1,0:T(8,128)(2,1)S(1)}, u32[]{:S(2)}, u32[]{:S(2)}) collective-permute-start(bf16[4,48,768]{2,1,0:T(8,128)(2,1)S(1)} %get-tuple-element.149), channel_id=1, source_target_pairs={{0,8},{4,12},{8,0},{12,4},{16,24},{20,28},{24,16},{28,20},{1,9},{5... | collective-permute-start | bytes 884744 | tf_op jit(solution)/shard_map/ppermute | solution.py:686
  83.6 14.7 %collective-permute-start.12 = (bf16[4,48,768]{2,1,0:T(8,128)(2,1)S(1)}, bf16[4,48,768]{2,1,0:T(8,128)(2,1)S(1)}, u32[]{:S(2)}, u32[]{:S(2)}) collective-permute-start(bf16[4,48,768]{2,1,0:T(8,128)(2,1)S(1)} %get-tuple-element.150), channel_id=1, source_target_pairs={{0,16},{4,20},{8,24},{12,28},{16,0},{20,4},{24,8},{28,12},{1,17},{... | collective-permute-start | bytes 884744 | tf_op jit(solution)/shard_map/ppermute | solution.py:686
  98.7 16.4 %collective-permute-start.13 = (bf16[4,96,1536]{2,1,0:T(8,128)(2,1)S(1)}, bf16[4,96,1536]{2,1,0:T(8,128)(2,1)S(1)}, u32[]{:S(2)}, u32[]{:S(2)}) collective-permute-start(bf16[4,96,1536]{2,1,0:T(8,128)(2,1)S(1)} %pad_maximum_fusion.1), channel_id=1, source_target_pairs={{0,4},{4,0},{8,12},{12,8},{16,20},{20,16},{24,28},{28,24},{1,5},{5... | collective-permute-start | bytes 3538952 | tf_op jit(solution)/shard_map/ppermute | solution.py:686
  182.2 31.1 %collective-permute-start.14 = (bf16[4,384,768]{2,1,0:T(8,128)(2,1)}, bf16[4,384,768]{2,1,0:T(8,128)(2,1)S(1)}, u32[]{:S(2)}, u32[]{:S(2)}) collective-permute-start(bf16[4,384,768]{2,1,0:T(8,128)(2,1)} %get-tuple-element.71), channel_id=1, source_target_pairs={{0,4},{4,0},{8,12},{12,8},{16,20},{20,16},{24,28},{28,24},{1,5},{5... | collective-permute-start | bytes 7077896 | tf_op jit(solution)/shard_map/ppermute | solution.py:686
  182.6 38.2 %collective-permute-start.17 = (bf16[4,768,384]{2,1,0:T(8,128)(2,1)}, bf16[4,768,384]{2,1,0:T(8,128)(2,1)}, u32[]{:S(2)}, u32[]{:S(2)}) collective-permute-start(bf16[4,768,384]{2,1,0:T(8,128)(2,1)} %get-tuple-element.73), channel_id=1, source_target_pairs={{0,4},{4,0},{8,12},{12,8},{16,20},{20,16},{24,28},{28,24},{1,5},{5... | collective-permute-start | bytes 7077896 | tf_op jit(solution)/shard_map/ppermute | solution.py:686
  182.8 21.4 %collective-permute-start.20 = (bf16[384,768]{1,0:T(8,128)(2,1)}, bf16[384,768]{1,0:T(8,128)(2,1)S(1)}, u32[]{:S(2)}, u32[]{:S(2)}) collective-permute-start(bf16[384,768]{1,0:T(8,128)(2,1)} %get-tuple-element.85), channel_id=1, source_target_pairs={{0,4},{4,0},{8,12},{12,8},{16,20},{20,16},{24,28},{28,24},{1,5},{5... | collective-permute-start | bytes 1769480 | tf_op jit(solution)/shard_map/ppermute | solution.py:686
  207.5 38.3 %all-to-all-start.2 = ((bf16[16,48,768]{2,1,0:T(8,128)(2,1)}), bf16[16,48,768]{2,1,0:T(8,128)(2,1)S(1)}, u32[]{:S(2)}, u32[]{:S(2)}) async-start(bf16[16,48,768]{2,1,0:T(8,128)(2,1)} %pad_maximum_fusion.2.rest_10_), calls=%async_computation.2 | async-start | bytes 2359296 | tf_op jit(solution)/shard_map/all_to_all | solution.py:766
  218.7 36.5 %collective-permute-start.15 = (bf16[2,384,768]{2,1,0:T(8,128)(2,1)}, bf16[2,384,768]{2,1,0:T(8,128)(2,1)}, u32[]{:S(2)}, u32[]{:S(2)}) collective-permute-start(bf16[2,384,768]{2,1,0:T(8,128)(2,1)} %get-tuple-element.118.rest_8_), channel_id=1, source_target_pairs={{0,8},{4,12},{8,0},{12,4},{16,24},{20,28},{24,16},{28,20},{1,9},{5... | collective-permute-start | bytes 3538952 | tf_op jit(solution)/shard_map/ppermute | solution.py:686
  224.0 34.6 %collective-permute-start.18 = (bf16[2,768,384]{2,1,0:T(8,128)(2,1)}, bf16[2,768,384]{2,1,0:T(8,128)(2,1)}, u32[]{:S(2)}, u32[]{:S(2)}) collective-permute-start(bf16[2,768,384]{2,1,0:T(8,128)(2,1)} %get-tuple-element.120.rest_9_), channel_id=1, source_target_pairs={{0,16},{4,20},{8,24},{12,28},{16,0},{20,4},{24,8},{28,12},{1,17},{... | collective-permute-start | bytes 3538952 | tf_op jit(solution)/shard_map/ppermute | solution.py:686
  250.4 24.6 %all-to-all-start.3 = ((bf16[16,24,768]{2,1,0:T(8,128)(2,1)}), bf16[16,24,768]{2,1,0:T(8,128)(2,1)S(1)}, u32[]{:S(2)}, u32[]{:S(2)}) async-start(bf16[16,24,768]{2,1,0:T(8,128)(2,1)} %bitcast.58.rest_11_), calls=%async_computation.3 | async-start | bytes 1179648 | tf_op jit(solution)/shard_map/all_to_all | solution.py:766
  256.5 23.1 %collective-permute-start.16 = (bf16[384,768]{1,0:T(8,128)(2,1)S(1)}, bf16[384,768]{1,0:T(8,128)(2,1)}, u32[]{:S(2)}, u32[]{:S(2)}) collective-permute-start(bf16[384,768]{1,0:T(8,128)(2,1)S(1)} %fusion.26.rest_8_), channel_id=1, source_target_pairs={{0,16},{4,20},{8,24},{12,28},{16,0},{20,4},{24,8},{28,12},{1,17},{... | collective-permute-start | bytes 1769480 | tf_op jit(solution)/shard_map/ppermute | solution.py:686
  260.6 17.4 %collective-permute-start.19 = (bf16[768,384]{1,0:T(8,128)(2,1)}, bf16[768,384]{1,0:T(8,128)(2,1)}, u32[]{:S(2)}, u32[]{:S(2)}) collective-permute-start(bf16[768,384]{1,0:T(8,128)(2,1)} %fusion.24.rest_9_), channel_id=1, source_target_pairs={{0,8},{4,12},{8,0},{12,4},{16,24},{20,28},{24,16},{28,20},{1,9},{5... | collective-permute-start | bytes 1769480 | tf_op jit(solution)/shard_map/ppermute | solution.py:686
  282.1 37.1 %all-to-all-start.1 = ((bf16[4,192,768]{2,1,0:T(8,128)(2,1)}), bf16[4,192,768]{2,1,0:T(8,128)(2,1)S(1)}, u32[]{:S(2)}, u32[]{:S(2)}) async-start(bf16[4,192,768]{2,1,0:T(8,128)(2,1)} %maximum_maximum_fusion.rest_8_), calls=%async_computation.1 | async-start | bytes 2359296 | tf_op jit(solution)/shard_map/all_to_all | solution.py:1109
  286.4 82.2 %all-gather.11.cloned.1.call-start = ((), (), s32[]{:S(2)}) async-start(), calls=%async_computation.7 | async-start | bytes 3870720 | tf_op jit(solution)/shard_map/all_gather | solution.py:1163
  322.7 17.9 %collective-permute-start.24 = (bf16[2,4,256,768]{3,2,1,0:T(8,128)(2,1)}, bf16[2,4,256,768]{3,2,1,0:T(8,128)(2,1)}, u32[]{:S(2)}, u32[]{:S(2)}) collective-permute-start(bf16[2,4,256,768]{3,2,1,0:T(8,128)(2,1)} %get-tuple-element.112.refs_1_.refs_7_), channel_id=1, source_target_pairs={{0,4},{4,0},{8,12},{12,8},{16,20},{20,16},{24,28},{28,24},{1,5},{5... | collective-permute-start | bytes 9437192 | tf_op jit(solution)/shard_map/ppermute | solution.py:686
  322.9 29.0 %all-to-all-start.4 = ((bf16[16,25,768]{2,1,0:T(8,128)(2,1)}), bf16[16,25,768]{2,1,0:T(8,128)(2,1)}, u32[]{:S(2)}, u32[]{:S(2)}) async-start(bf16[16,25,768]{2,1,0:T(8,128)(2,1)} %bitcast.68.refs_11_.refs_9_), calls=%async_computation.4 | async-start | bytes 1572864 | tf_op jit(solution)/shard_map/all_to_all | solution.py:766
  354.7 7.8 %collective-permute-start.27 = (bf16[2,32,768]{2,1,0:T(8,128)(2,1)S(1)}, bf16[2,32,768]{2,1,0:T(8,128)(2,1)S(1)}, u32[]{:S(2)}, u32[]{:S(2)}) collective-permute-start(bf16[2,32,768]{2,1,0:T(8,128)(2,1)S(1)} %pad_maximum_fusion.14), channel_id=1, source_target_pairs={{0,8},{4,12},{8,0},{12,4},{16,24},{20,28},{24,16},{28,20},{1,9},{5... | collective-permute-start | bytes 294920 | tf_op jit(solution)/shard_map/ppermute | solution.py:686
  354.8 26.6 %collective-permute-start.25 = (bf16[2,256,768]{2,1,0:T(8,128)(2,1)S(1)}, bf16[2,256,768]{2,1,0:T(8,128)(2,1)}, u32[]{:S(2)}, u32[]{:S(2)}) collective-permute-start(bf16[2,256,768]{2,1,0:T(8,128)(2,1)S(1)} %copy-done.22), channel_id=1, source_target_pairs={{0,8},{4,12},{8,0},{12,4},{16,24},{20,28},{24,16},{28,20},{1,9},{5... | collective-permute-start | bytes 2359304 | tf_op jit(solution)/shard_map/ppermute | solution.py:686
  356.8 30.2 %collective-permute-start.29 = (bf16[2,256,768]{2,1,0:T(8,128)(2,1)S(1)}, bf16[2,256,768]{2,1,0:T(8,128)(2,1)}, u32[]{:S(2)}, u32[]{:S(2)}) collective-permute-start(bf16[2,256,768]{2,1,0:T(8,128)(2,1)S(1)} %copy-done.21), channel_id=1, source_target_pairs={{0,16},{4,20},{8,24},{12,28},{16,0},{20,4},{24,8},{28,12},{1,17},{... | collective-permute-start | bytes 2359304 | tf_op jit(solution)/shard_map/ppermute | solution.py:686
  383.3 17.7 %collective-permute-start.28 = (bf16[384,768]{1,0:T(8,128)(2,1)}, bf16[384,768]{1,0:T(8,128)(2,1)}, u32[]{:S(2)}, u32[]{:S(2)}) collective-permute-start(bf16[384,768]{1,0:T(8,128)(2,1)} %pad_maximum_fusion.7), channel_id=1, source_target_pairs={{0,16},{4,20},{8,24},{12,28},{16,0},{20,4},{24,8},{28,12},{1,17},{... | collective-permute-start | bytes 1769480 | tf_op jit(solution)/shard_map/ppermute | solution.py:686
  389.2 10.7 %collective-permute-start.30 = (bf16[256,768]{1,0:T(8,128)(2,1)S(1)}, bf16[256,768]{1,0:T(8,128)(2,1)S(1)}, u32[]{:S(2)}, u32[]{:S(2)}) collective-permute-start(bf16[256,768]{1,0:T(8,128)(2,1)S(1)} %fusion.28), channel_id=1, source_target_pairs={{0,8},{4,12},{8,0},{12,4},{16,24},{20,28},{24,16},{28,20},{1,9},{5... | collective-permute-start | bytes 1179656 | tf_op jit(solution)/shard_map/ppermute | solution.py:686
  (56 other events, 232.4 us)
Sparse Core Ops, SparseCore 0:
  17.2 55.5 all-gather.6
  76.5 68.4 all-gather.8
  322.8 45.7 all-gather.10
